TPU v7x, 32 devices: a whole 2x2x4 slice. The times are simulated.
32 devices in a mesh: clips: 2 (over y), tok: 4 (over z), head: 4 (over x, core).
Axes of the slice: x: 2, y: 2, z: 4, core: 2. Of those that a mesh axis runs over, the one named last changes fastest.
Arguments:
- query: bfloat16 [24, 256, 1536], P(('clips', 'tok'), 'head'), parts along dimension 0, may hold values from -16 to 16, as said below
- key: bfloat16 [24, 256, 1536], P(('clips', 'tok'), 'head'), parts along dimension 0, may hold values from -16 to 16
- value: bfloat16 [24, 256, 1536], P(('clips', 'tok'), 'head'), parts along dimension 0, may hold values from -6 to 6
- valid_rows: int32 [24], P(('clips', 'tok')), parts along dimension 0, may hold values from 1 to 8, as said below
Outputs:
- attended: bfloat16 [24, 256, 1536], P(('clips', 'tok'), 'head'), parts along dimension 0
There are 2 independent parts, one for each index of `clips`. A program takes and returns all parts, laid end to end along the dimension named above; each array names one. Nothing has to cross between parts.
Inputs may be any that keep to these rules, and one draw needn't show every extreme that they name: Entries of query and key lie within -16 and 16. `valid_rows`: tiles outside the last height-tile row have all 8 rows real; tiles of the last height-tile row each have their own count.
All inputs are finite; a program needn't handle non-finite values.
Results may differ from a plain program's by a relative error of at most 0.0031.
Values may be sent and summed in bfloat16 or wider, within the bound.
No kernel may reach another device: no remote copies, remote signals or barrier semaphores. Data moves between devices by JAX's collectives and lax.ppermute only.
A program may use at most 64 MiB of HBM per device.

v0:
```python
import math

import jax
import jax.numpy as jnp
from jax import lax
from jax.sharding import PartitionSpec as P

HEAD_DIM = 128
TILE_H = 8
TILE_W = 8
TIME_TILES = 4


def shifted(block, axis, distance):
    devices = range(lax.axis_size(axis))
    route = [(i - distance, i) for i in devices if i - distance in devices]
    return lax.ppermute(block, axis, route)


def blank_piece(piece):
    return tuple((jnp.zeros_like(member) for member in piece))


def clear_counts(piece, keep):
    return (piece[0], piece[1], jnp.where(keep, piece[2], 0))


def body(query, key, value, valid_rows):
    q_heads, k_heads, v_heads = (
        lax.all_to_all(query, "head", split_axis=2, concat_axis=1, tiled=True),
        lax.all_to_all(key, "head", split_axis=2, concat_axis=1, tiled=True),
        lax.all_to_all(value, "head", split_axis=2, concat_axis=1, tiled=True),
    )
    width = q_heads.shape[0]
    tile_len = q_heads.shape[1]
    local = q_heads.shape[2] // HEAD_DIM
    scale = 1.0 / math.sqrt(HEAD_DIM)
    rows_grid = lax.axis_size("tok") // TIME_TILES
    height = lax.axis_index("tok") % rows_grid
    own = (k_heads, v_heads, valid_rows)
    pieces = []
    for down in (-1, 0, 1):
        for side in (-1, 0, 1):
            if down == 0 and side == 0:
                pieces.append(own)
            elif side != 0 and rows_grid == 1:
                pieces.append(blank_piece(own))
            else:
                moved = shifted((own[0], own[1], own[2]), "tok", -(down * rows_grid + side))
                if side != 0:
                    moved = clear_counts(moved, (height + side >= 0) & (height + side < rows_grid))
                pieces.append(moved)
    padded = [
        (
            jnp.pad(piece[0], ((1, 1), (0, 0), (0, 0))),
            jnp.pad(piece[1], ((1, 1), (0, 0), (0, 0))),
            jnp.pad(piece[2], (1, 1)),
        )
        for piece in pieces
    ]
    counts_all = jnp.stack([piece[2] for piece in padded])
    row_index = jnp.arange(tile_len) // TILE_W % TILE_H

    def attend(number):
        tile = number // local
        start = number % local * HEAD_DIM
        block_keys = jnp.concatenate(
            [
                lax.dynamic_slice(piece[0], (tile, 0, start), (3, tile_len, HEAD_DIM))
                for piece in padded
            ],
            0,
        ).reshape(-1, HEAD_DIM)
        block_values = jnp.concatenate(
            [
                lax.dynamic_slice(piece[1], (tile, 0, start), (3, tile_len, HEAD_DIM))
                for piece in padded
            ],
            0,
        ).reshape(-1, HEAD_DIM)
        counts = lax.dynamic_slice_in_dim(counts_all, tile, 3, 1)
        mask = (row_index[None, None, :] < counts[:, :, None]).reshape(-1)
        queries = lax.dynamic_slice(q_heads, (tile, 0, start), (1, tile_len, HEAD_DIM))[0]
        scores = (
            jnp.einsum("qd,kd->qk", queries, block_keys, preferred_element_type=jnp.float32) * scale
        )
        scores = jnp.where(mask[None, :], scores, -jnp.inf)
        largest = jnp.max(scores, axis=-1, keepdims=True)
        weight = jnp.exp(scores - largest)
        total = jnp.sum(weight, axis=-1, keepdims=True)
        rounded = weight.astype(jnp.bfloat16)
        summed = jnp.dot(rounded, block_values, preferred_element_type=jnp.float32)
        return (summed / total).astype(jnp.bfloat16)

    results = lax.map(attend, jnp.arange(width * local, dtype=jnp.int32))
    attended = results.reshape(width, local, tile_len, HEAD_DIM).transpose(0, 2, 1, 3)
    attended = attended.reshape(width, tile_len, local * HEAD_DIM)
    return lax.all_to_all(attended, "head", split_axis=1, concat_axis=2, tiled=True)


def solution(mesh):
    placed = (
        P(("clips", "tok"), "head", None),
        P(("clips", "tok"), "head", None),
        P(("clips", "tok"), "head", None),
        P(("clips", "tok")),
    )
    return jax.shard_map(
        body,
        mesh=mesh,
        in_specs=placed,
        out_specs=P(("clips", "tok"), "head", None),
        check_vma=False,
    )
```

profile of v0, /device:TPU:9, one launch (start us, length us, event | category | flops | bytes accessed | tf_op | source)
XLA Modules:
  0.0 202.6 jit_solution(15187029604609117367)
XLA Ops:
  0.0 2.5 %copy.28 = bf16[3,64,1536]{1,0,2:T(4,128)(2,1)S(1)} copy(bf16[3,64,1536]{2,1,0:T(8,128)(2,1)} %param.7) | data formatting | bytes 1179648 | tf_op args[1]
  2.5 2.2 %reshape.59 = bf16[4,2,36864]{2,1,0:T(2,128)(2,1)} reshape(bf16[1536,3,64]{2,1,0:T(4,128)(2,1)S(1)} %bitcast.73) | data formatting | bytes 1179648
  4.7 4.1 %all-to-all-start.1 = ((bf16[4,2,36864]{2,1,0:T(2,128)(2,1)}), bf16[4,2,36864]{2,1,0:T(2,128)(2,1)S(1)}, u32[]{:S(2)}, u32[]{:S(2)}) async-start(bf16[4,2,36864]{2,1,0:T(2,128)(2,1)} %reshape.59), calls=%async_computation.1 | async-start | bytes 1179648 | tf_op jit(solution)/shard_map/all_to_all | solution.py:31
  9.9 2.2 %reshape.61 = bf16[4,2,36864]{2,1,0:T(2,128)(2,1)} reshape(bf16[1536,3,64]{2,1,0:T(4,128)(2,1)S(1)} %bitcast.74) | data formatting | bytes 1179648
  12.0 5.5 %all-to-all-done.1 = bf16[4,2,36864]{2,1,0:T(2,128)(2,1)S(1)} async-done(((bf16[4,2,36864]{2,1,0:T(2,128)(2,1)}), bf16[4,2,36864]{2,1,0:T(2,128)(2,1)S(1)}, u32[]{:S(2)}, u32[]{:S(2)}) %all-to-all-start.1) | async-done | bytes 589856 | tf_op jit(solution)/shard_map/all_to_all | solution.py:31
  17.5 4.3 %all-to-all-start.2 = ((bf16[4,2,36864]{2,1,0:T(2,128)(2,1)}), bf16[4,2,36864]{2,1,0:T(2,128)(2,1)S(1)}, u32[]{:S(2)}, u32[]{:S(2)}) async-start(bf16[4,2,36864]{2,1,0:T(2,128)(2,1)} %reshape.61), calls=%async_computation.2 | async-start | bytes 1179648 | tf_op jit(solution)/shard_map/all_to_all | solution.py:32
  24.8 2.0 %collective-permute-start.3 = (bf16[3,256,384]{2,1,0:T(8,128)(2,1)}, bf16[3,256,384]{2,1,0:T(8,128)(2,1)}, u32[]{:S(2)}, u32[]{:S(2)}) collective-permute-start(bf16[3,256,384]{2,1,0:T(8,128)(2,1)} %bitcast.9), channel_id=1, source_target_pairs={{4,0},{8,4},{12,8},{5,1},{9,5},{13,9},{6,2},{10,6},{14,10},{7,3},{... | collective-permute-start | bytes 1769480 | tf_op jit(solution)/shard_map/ppermute | solution.py:17
  26.9 3.4 %collective-permute-start.2 = (bf16[3,256,384]{2,1,0:T(8,128)(2,1)}, bf16[3,256,384]{2,1,0:T(8,128)(2,1)}, u32[]{:S(2)}, u32[]{:S(2)}) collective-permute-start(bf16[3,256,384]{2,1,0:T(8,128)(2,1)} %bitcast.9), channel_id=1, source_target_pairs={{0,4},{4,8},{8,12},{1,5},{5,9},{9,13},{2,6},{6,10},{10,14},{3,7},{... | collective-permute-start | bytes 1769480 | tf_op jit(solution)/shard_map/ppermute | solution.py:17
  33.6 2.4 %collective-permute-start.5 = (bf16[3,256,384]{2,1,0:T(8,128)(2,1)}, bf16[3,256,384]{2,1,0:T(8,128)(2,1)}, u32[]{:S(2)}, u32[]{:S(2)}) collective-permute-start(bf16[3,256,384]{2,1,0:T(8,128)(2,1)} %bitcast.12), channel_id=1, source_target_pairs={{4,0},{8,4},{12,8},{5,1},{9,5},{13,9},{6,2},{10,6},{14,10},{7,3},{... | collective-permute-start | bytes 1769480 | tf_op jit(solution)/shard_map/ppermute | solution.py:17
  36.0 3.2 %collective-permute-start.4 = (bf16[3,256,384]{2,1,0:T(8,128)(2,1)}, bf16[3,256,384]{2,1,0:T(8,128)(2,1)}, u32[]{:S(2)}, u32[]{:S(2)}) collective-permute-start(bf16[3,256,384]{2,1,0:T(8,128)(2,1)} %bitcast.12), channel_id=1, source_target_pairs={{0,4},{4,8},{8,12},{1,5},{5,9},{9,13},{2,6},{6,10},{10,14},{3,7},{... | collective-permute-start | bytes 1769480 | tf_op jit(solution)/shard_map/ppermute | solution.py:17
  40.3 2.2 %reshape.57 = bf16[4,2,36864]{2,1,0:T(2,128)(2,1)} reshape(bf16[1536,3,64]{2,1,0:T(4,128)(2,1)S(1)} %bitcast.75) | data formatting | bytes 1179648
  42.5 5.1 %all-to-all-start = ((bf16[4,2,36864]{2,1,0:T(2,128)(2,1)}), bf16[4,2,36864]{2,1,0:T(2,128)(2,1)}, u32[]{:S(2)}, u32[]{:S(2)}) async-start(bf16[4,2,36864]{2,1,0:T(2,128)(2,1)} %reshape.57), calls=%async_computation | async-start | bytes 1179648 | tf_op jit(solution)/shard_map/all_to_all | solution.py:30
  47.6 4.4 %collective-permute-start = (s32[3]{0:T(128)S(1)}, s32[3]{0:T(128)S(1)}, u32[]{:S(2)}, u32[]{:S(2)}) collective-permute-start(s32[3]{0:T(128)S(1)} %copy-done.2), channel_id=1, source_target_pairs={{0,4},{4,8},{8,12},{1,5},{5,9},{9,13},{2,6},{6,10},{10,14},{3,7},{... | collective-permute-start | bytes 44 | tf_op jit(solution)/shard_map/ppermute | solution.py:17
  52.1 4.5 %collective-permute-done = s32[3]{0:T(128)S(1)} collective-permute-done((s32[3]{0:T(128)S(1)}, s32[3]{0:T(128)S(1)}, u32[]{:S(2)}, u32[]{:S(2)}) %collective-permute-start) | collective-permute-done | bytes 44 | tf_op jit(solution)/shard_map/ppermute | solution.py:17
  58.6 2.3 %collective-permute-done.1 = s32[3]{0:T(128)S(1)} collective-permute-done((s32[3]{0:T(128)S(1)}, s32[3]{0:T(128)S(1)}, u32[]{:S(2)}, u32[]{:S(2)}) %collective-permute-start.1) | collective-permute-done | bytes 44 | tf_op jit(solution)/shard_map/ppermute | solution.py:17
  63.4 2.7 %reshape.58 = bf16[1536,3,64]{2,1,0:T(4,128)(2,1)S(1)} reshape(bf16[4,2,36864]{2,1,0:T(2,128)(2,1)} %all-to-all-done) | data formatting | bytes 1179648
  68.0 2.1 %pad.61 = bf16[5,256,384]{2,1,0:T(8,128)(2,1)} pad(bf16[3,256,384]{2,1,0:T(8,128)(2,1)} %collective-permute-done.3, bf16[]{:T(256)} %constant.114.clone.1), padding=1_1x0_0x0_0 | pad | bytes 1572866 | tf_op jit(solution)/shard_map/jit(_pad)/pad | solution.py:55
  70.1 2.2 %pad.59 = bf16[5,256,384]{2,1,0:T(8,128)(2,1)} pad(bf16[3,256,384]{2,1,0:T(8,128)(2,1)} %collective-permute-done.2, bf16[]{:T(256)} %constant.114.clone.1), padding=1_1x0_0x0_0 | pad | bytes 1572866 | tf_op jit(solution)/shard_map/jit(_pad)/pad | solution.py:55
  72.3 2.1 %pad.64 = bf16[5,256,384]{2,1,0:T(8,128)(2,1)} pad(bf16[3,256,384]{2,1,0:T(8,128)(2,1)} %collective-permute-done.5, bf16[]{:T(256)} %constant.114.clone.1), padding=1_1x0_0x0_0 | pad | bytes 1572866 | tf_op jit(solution)/shard_map/jit(_pad)/pad | solution.py:56
  74.5 2.1 %pad.62 = bf16[5,256,384]{2,1,0:T(8,128)(2,1)} pad(bf16[3,256,384]{2,1,0:T(8,128)(2,1)} %collective-permute-done.4, bf16[]{:T(256)} %constant.114.clone.1), padding=1_1x0_0x0_0 | pad | bytes 1572866 | tf_op jit(solution)/shard_map/jit(_pad)/pad | solution.py:56
  76.7 108.1 %while.14 = (s32[]{:T(128)}, bf16[9,256,128]{1,2,0:T(8,128)(2,1)}, s32[9]{0:T(128)S(1)}, s32[9,5]{0,1:T(8,128)S(1)}, bf16[3,256,384]{2,1,0:T(8,128)(2,1)}, /*ind...) while((s32[]{:T(128)}, bf16[9,256,128]{1,2,0:T(8,128)(2,1)}, ...), condition=%wide.region_3.4_spmd.clone, body=%wide.region_0.3_spmd.clone.sunk | while | flops 918432768 | bytes 35228752 | solution.py:95
  83.5 2.0 %fusion.33 = (f32[256]{0:T(256)S(1)}, f32[256,6912]{1,0:T(8,128)S(1)}) fusion(bf16[6912,128]{1,0:T(8,128)(2,1)S(1)} %bitcast.68, bf16[3,256,384]{2,1,0:T(8,128)(2,1)} %get-tuple-element.469, s32[]{:T(128)S(6)} %select_n.210, s32[]{:T(128)S(6)} %select_n.209, pred[6912]{0:T(1024)(128)(4,1)S(1)} %lt.134), kind=kOutput, calls=%fused_computation.48.clone.1 | convolution fusion | flops 458292992 | bytes 8920840 | tf_op jit(solution)/shard_map/while/body/eval_jaxpr/qd,kd->qk/dot_general | solution.py:85
  95.5 2.0 %fusion.33 = (f32[256]{0:T(256)S(1)}, f32[256,6912]{1,0:T(8,128)S(1)}) fusion(bf16[6912,128]{1,0:T(8,128)(2,1)S(1)} %bitcast.68, bf16[3,256,384]{2,1,0:T(8,128)(2,1)} %get-tuple-element.469, s32[]{:T(128)S(6)} %select_n.210, s32[]{:T(128)S(6)} %select_n.209, pred[6912]{0:T(1024)(128)(4,1)S(1)} %lt.134), kind=kOutput, calls=%fused_computation.48.clone.1 | convolution fusion | flops 458292992 | bytes 8920840 | tf_op jit(solution)/shard_map/while/body/eval_jaxpr/qd,kd->qk/dot_general | solution.py:85
  186.3 15.3 %all_to_all.72 = bf16[3,256,384]{2,0,1:T(4,128)(2,1)S(1)} all-to-all(bf16[3,256,384]{2,0,1:T(4,128)(2,1)S(1)} %copy.34), channel_id=1, replica_groups=mesh['clips'=2,'tok'=4,'head'=4] {'head'}, dimensions={1} | all-to-all | bytes 1179648 | tf_op jit(solution)/shard_map/all_to_all | solution.py:98
  (277 shorter events, 102.9 us)
Async XLA Ops:
  2.5 6.3 %copy-start = (bf16[3,64,1536]{2,1,0:T(8,128)(2,1)S(1)}, bf16[3,64,1536]{2,1,0:T(8,128)(2,1)}, u32[]{:S(2)}) copy-start(bf16[3,64,1536]{2,1,0:T(8,128)(2,1)} %param.8) | copy-start | bytes 1769476
  4.7 12.8 %all-to-all-start.1 = ((bf16[4,2,36864]{2,1,0:T(2,128)(2,1)}), bf16[4,2,36864]{2,1,0:T(2,128)(2,1)S(1)}, u32[]{:S(2)}, u32[]{:S(2)}) async-start(bf16[4,2,36864]{2,1,0:T(2,128)(2,1)} %reshape.59), calls=%async_computation.1 | async-start | bytes 1179648 | tf_op jit(solution)/shard_map/all_to_all | solution.py:31
  17.5 13.1 %all-to-all-start.2 = ((bf16[4,2,36864]{2,1,0:T(2,128)(2,1)}), bf16[4,2,36864]{2,1,0:T(2,128)(2,1)S(1)}, u32[]{:S(2)}, u32[]{:S(2)}) async-start(bf16[4,2,36864]{2,1,0:T(2,128)(2,1)} %reshape.61), calls=%async_computation.2 | async-start | bytes 1179648 | tf_op jit(solution)/shard_map/all_to_all | solution.py:32
  24.8 14.4 %copy-start.1 = (bf16[3,64,1536]{2,1,0:T(8,128)(2,1)S(1)}, bf16[3,64,1536]{2,1,0:T(8,128)(2,1)}, u32[]{:S(2)}) copy-start(bf16[3,64,1536]{2,1,0:T(8,128)(2,1)} %param.6) | copy-start | bytes 1769476
  24.8 43.2 %collective-permute-start.3 = (bf16[3,256,384]{2,1,0:T(8,128)(2,1)}, bf16[3,256,384]{2,1,0:T(8,128)(2,1)}, u32[]{:S(2)}, u32[]{:S(2)}) collective-permute-start(bf16[3,256,384]{2,1,0:T(8,128)(2,1)} %bitcast.9), channel_id=1, source_target_pairs={{4,0},{8,4},{12,8},{5,1},{9,5},{13,9},{6,2},{10,6},{14,10},{7,3},{... | collective-permute-start | bytes 1769480 | tf_op jit(solution)/shard_map/ppermute | solution.py:17
  26.9 43.3 %collective-permute-start.2 = (bf16[3,256,384]{2,1,0:T(8,128)(2,1)}, bf16[3,256,384]{2,1,0:T(8,128)(2,1)}, u32[]{:S(2)}, u32[]{:S(2)}) collective-permute-start(bf16[3,256,384]{2,1,0:T(8,128)(2,1)} %bitcast.9), channel_id=1, source_target_pairs={{0,4},{4,8},{8,12},{1,5},{5,9},{9,13},{2,6},{6,10},{10,14},{3,7},{... | collective-permute-start | bytes 1769480 | tf_op jit(solution)/shard_map/ppermute | solution.py:17
  33.6 38.7 %collective-permute-start.5 = (bf16[3,256,384]{2,1,0:T(8,128)(2,1)}, bf16[3,256,384]{2,1,0:T(8,128)(2,1)}, u32[]{:S(2)}, u32[]{:S(2)}) collective-permute-start(bf16[3,256,384]{2,1,0:T(8,128)(2,1)} %bitcast.12), channel_id=1, source_target_pairs={{4,0},{8,4},{12,8},{5,1},{9,5},{13,9},{6,2},{10,6},{14,10},{7,3},{... | collective-permute-start | bytes 1769480 | tf_op jit(solution)/shard_map/ppermute | solution.py:17
  36.0 38.5 %collective-permute-start.4 = (bf16[3,256,384]{2,1,0:T(8,128)(2,1)}, bf16[3,256,384]{2,1,0:T(8,128)(2,1)}, u32[]{:S(2)}, u32[]{:S(2)}) collective-permute-start(bf16[3,256,384]{2,1,0:T(8,128)(2,1)} %bitcast.12), channel_id=1, source_target_pairs={{0,4},{4,8},{8,12},{1,5},{5,9},{9,13},{2,6},{6,10},{10,14},{3,7},{... | collective-permute-start | bytes 1769480 | tf_op jit(solution)/shard_map/ppermute | solution.py:17
  40.3 7.3 %copy-start.2 = (s32[3]{0:T(128)S(1)}, s32[3]{0:T(128)}, u32[]{:S(2)}) copy-start(s32[3]{0:T(128)} %param.9) | copy-start | bytes 40
  42.5 20.9 %all-to-all-start = ((bf16[4,2,36864]{2,1,0:T(2,128)(2,1)}), bf16[4,2,36864]{2,1,0:T(2,128)(2,1)}, u32[]{:S(2)}, u32[]{:S(2)}) async-start(bf16[4,2,36864]{2,1,0:T(2,128)(2,1)} %reshape.57), calls=%async_computation | async-start | bytes 1179648 | tf_op jit(solution)/shard_map/all_to_all | solution.py:30
  47.6 9.0 %collective-permute-start = (s32[3]{0:T(128)S(1)}, s32[3]{0:T(128)S(1)}, u32[]{:S(2)}, u32[]{:S(2)}) collective-permute-start(s32[3]{0:T(128)S(1)} %copy-done.2), channel_id=1, source_target_pairs={{0,4},{4,8},{8,12},{1,5},{5,9},{9,13},{2,6},{6,10},{10,14},{3,7},{... | collective-permute-start | bytes 44 | tf_op jit(solution)/shard_map/ppermute | solution.py:17
  56.6 4.3 %collective-permute-start.1 = (s32[3]{0:T(128)S(1)}, s32[3]{0:T(128)S(1)}, u32[]{:S(2)}, u32[]{:S(2)}) collective-permute-start(s32[3]{0:T(128)S(1)} %copy-done.2), channel_id=1, source_target_pairs={{4,0},{8,4},{12,8},{5,1},{9,5},{13,9},{6,2},{10,6},{14,10},{7,3},{... | collective-permute-start | bytes 44 | tf_op jit(solution)/shard_map/ppermute | solution.py:17
where the time goes:
time: 206 us; the launch traced here: 203 us
  local copies, waits for them, and re-layouts  83.7 us (41%)
  starting transfers between devices  30.8 us (15%)
  matrix products  30.1 us (15%)
  loops' own time  18.8 us (9%)
  blocking collectives  15.3 us (7%)
  waiting for transfers between devices  12.6 us (6%)
  other arithmetic  11.1 us (5%)
    while x126, local copies, waits for them, and re-layouts  33.3 us
    another operation x1, loops' own time, body(): results = lax.map(attend, jnp.arange(width * local, dtype=jnp.int32))  18.8 us
    dot_general x9, matrix products, attend(): jnp.einsum('qd,kd->qk', queries, block_keys, preferred_element_type=jnp.f...  18.3 us
    ppermute x6, starting transfers between devices, shifted(): return lax.ppermute(block, axis, route)  17.3 us
    unnamed x16, local copies, waits for them, and re-layouts  15.9 us
    all_to_all x1, blocking collectives, body(): lax.all_to_all(attended, 'head', split_axis=1, concat_axis=2, tiled=True)  15.3 us
    dot_general x9, matrix products, attend(): summed = jnp.dot(rounded, block_values, preferred_element_type=jnp.float32)  11.9 us
    reduce_sum x9, other arithmetic, attend(): total = jnp.sum(weight, axis=-1, keepdims=True)  10.3 us
  transfers between devices with their start and end apart: 9, of which 4 were waited for; matrix products, arithmetic and copies ran while one was open for 13% of the time, Pallas kernels for 0%

commit v1 on v0

v1 whole, which is shorter than its diff:
```python
import functools
import math

import jax
import jax.numpy as jnp
from jax import lax
from jax.experimental import pallas as pl
from jax.experimental.pallas import tpu as pltpu
from jax.sharding import PartitionSpec as P

HEAD_DIM = 128
TILE_H = 8
TILE_W = 8
TIME_TILES = 4
COUNT_ROWS = 16
MASKED = -1e30
VMEM_LIMIT = 48 * 2**20


def in_vmem(count):
    return [pl.BlockSpec(memory_space=pltpu.VMEM)] * count


def anywhere(count):
    return [pl.BlockSpec(memory_space=pl.ANY)] * count


def swap_head(block, bit, devices):
    return lax.ppermute(block, "head", [(i, i ^ bit) for i in range(devices)])


def swap_pairs(block, phase, stride, length, devices):
    route = []
    for i in range(devices):
        place = i // stride % length
        if place % 2 == phase and place + 1 < length:
            route += [(i, i + stride), (i + stride, i)]
    return lax.ppermute(block, "tok", route)


def pack_body(devices, part, me_ref, counts_ref, q_ref, k_ref, v_ref, *rest):
    near_ref, sibling_ref, own_q_ref = rest[:3]
    far_refs, far_q_refs = rest[3 : 1 + devices], rest[1 + devices : 2 * devices - 1]
    counts_buf, sems = rest[2 * devices - 1 :]
    rows = k_ref.shape[0]
    me = me_ref[0]

    def lanes(bit):
        return pl.ds(pl.multiple_of((me ^ bit) * part, HEAD_DIM), part)

    jobs = [
        (k_ref.at[:, lanes(0)], near_ref.at[pl.ds(0, rows)]),
        (v_ref.at[:, lanes(0)], near_ref.at[pl.ds(rows, rows)]),
        (k_ref.at[:, lanes(1)], near_ref.at[pl.ds(2 * rows + COUNT_ROWS, rows)]),
        (v_ref.at[:, lanes(1)], near_ref.at[pl.ds(3 * rows + COUNT_ROWS, rows)]),
        (k_ref.at[:, lanes(1)], sibling_ref.at[pl.ds(0, rows)]),
        (v_ref.at[:, lanes(1)], sibling_ref.at[pl.ds(rows, rows)]),
        (q_ref.at[:, lanes(1)], sibling_ref.at[pl.ds(2 * rows, rows)]),
        (q_ref.at[:, lanes(0)], own_q_ref),
    ]
    for bit in range(2, devices):
        jobs += [
            (k_ref.at[:, lanes(bit)], far_refs[bit - 2].at[pl.ds(0, rows)]),
            (v_ref.at[:, lanes(bit)], far_refs[bit - 2].at[pl.ds(rows, rows)]),
            (q_ref.at[:, lanes(bit)], far_q_refs[bit - 2]),
        ]
    copies = [pltpu.make_async_copy(src, dst, sems.at[i]) for i, (src, dst) in enumerate(jobs)]
    for copy in copies:
        copy.start()
    row = lax.broadcasted_iota(jnp.int32, counts_buf.shape, 0)
    filled = jnp.zeros(counts_buf.shape, jnp.float32)
    for tile in range(counts_ref.shape[0]):
        filled = jnp.where(row == tile, counts_ref[tile].astype(jnp.float32), filled)
    counts_buf[...] = filled.astype(jnp.bfloat16)
    last = pltpu.make_async_copy(
        counts_buf, near_ref.at[pl.ds(2 * rows, COUNT_ROWS)], sems.at[len(jobs)]
    )
    last.start()
    for copy in copies:
        copy.wait()
    last.wait()


def pack(me, counts, query, key, value, devices):
    rows, width = query.shape
    part = width // devices
    far = devices - 2

    def shape(count):
        return jax.ShapeDtypeStruct((count, part), jnp.bfloat16)

    outs = [shape(4 * rows + COUNT_ROWS), shape(3 * rows), shape(rows)]
    outs += [shape(2 * rows)] * far + [shape(rows)] * far
    results = pl.pallas_call(
        functools.partial(pack_body, devices, part),
        out_shape=outs,
        in_specs=[pl.BlockSpec(memory_space=pltpu.SMEM)] * 2 + anywhere(3),
        out_specs=anywhere(len(outs)),
        scratch_shapes=[
            pltpu.VMEM((COUNT_ROWS, part), jnp.bfloat16),
            pltpu.SemaphoreType.DMA((9 + 3 * far,)),
        ],
        cost_estimate=pl.CostEstimate(flops=0, bytes_accessed=4 * query.size * 4, transcendentals=0),
    )(me, counts, query, key, value)
    return results[0], results[1], results[2], results[3 : 3 + far], results[3 + far :]


def attend_body(slots, frames, tiles, tokens, heads, *refs):
    rows = tiles * tokens
    queries = refs[:frames]
    fields = refs[frames : frames + slots * frames]
    outs = refs[frames + slots * frames :]
    scale = math.log2(math.e) / math.sqrt(HEAD_DIM)
    lane = lax.broadcasted_iota(jnp.int32, (1, HEAD_DIM), 1)
    row = (lane // TILE_W % TILE_H).astype(jnp.float32)
    bias = {}
    for slot in range(slots):
        counted = fields[slot * frames][pl.ds(2 * rows, COUNT_ROWS), pl.ds(0, HEAD_DIM)]
        counted = counted.astype(jnp.float32)
        for tile in range(tiles):
            part = jnp.where(row < counted[tile : tile + 1], 0.0, MASKED)
            bias[slot, tile] = jnp.concatenate([part] * (frames * tokens // HEAD_DIM), 1)

    def piece(slot, frame, which, tile, lanes):
        ref = fields[slot * frames + frame]
        base = 2 * rows + COUNT_ROWS if frame == 1 and slot > 0 else 0
        return ref[pl.ds(base + which * rows + tile * tokens, tokens), lanes]

    for head in range(heads):
        lanes = pl.ds(head * HEAD_DIM, HEAD_DIM)
        for tile in range(tiles):
            window = [
                (slot, near)
                for near in range(max(tile - 1, 0), min(tile + 2, tiles))
                for slot in range(slots)
            ]
            members = [(slot, frame, near) for slot, near in window for frame in range(frames)]
            keys = jnp.concatenate([piece(s, f, 0, n, lanes) for s, f, n in members], 0)
            values = jnp.concatenate([piece(s, f, 1, n, lanes) for s, f, n in members], 0)
            asked = jnp.concatenate(
                [ref[pl.ds(tile * tokens, tokens), lanes] for ref in queries], 0
            )
            scores = lax.dot_general(
                asked, keys, (((1,), (1,)), ((), ())), preferred_element_type=jnp.float32
            )
            scores = scores + jnp.concatenate([bias[w] for w in window], 1)
            largest = jnp.max(scores, axis=1, keepdims=True)
            weight = jnp.exp2((scores - largest) * scale)
            total = jnp.sum(weight, axis=1, keepdims=True)
            summed = jnp.dot(
                weight.astype(jnp.bfloat16), values, preferred_element_type=jnp.float32
            )
            result = (summed / total).astype(jnp.bfloat16)
            for frame in range(frames):
                outs[frame][pl.ds(tile * tokens, tokens), lanes] = result[
                    frame * tokens : (frame + 1) * tokens
                ]


def attend(queries, slots, tiles, tokens, heads):
    frames = len(queries)
    fields = [member for slot in slots for member in slot]
    pairs = heads * (3 * tiles - 2) * len(slots) * (frames * tokens) ** 2
    return pl.pallas_call(
        functools.partial(attend_body, len(slots), frames, tiles, tokens, heads),
        out_shape=[jax.ShapeDtypeStruct((tiles * tokens, heads * HEAD_DIM), jnp.bfloat16)] * frames,
        in_specs=in_vmem(frames + len(fields)),
        out_specs=in_vmem(frames),
        compiler_params=pltpu.CompilerParams(vmem_limit_bytes=VMEM_LIMIT),
        cost_estimate=pl.CostEstimate(
            flops=4 * HEAD_DIM * pairs, bytes_accessed=0, transcendentals=pairs
        ),
    )(*queries, *fields)


def join_body(devices, part, me_ref, *rest):
    out_ref, sems = rest[devices], rest[devices + 1]
    me = me_ref[0]
    copies = [
        pltpu.make_async_copy(
            rest[bit],
            out_ref.at[:, pl.ds(pl.multiple_of((me ^ bit) * part, HEAD_DIM), part)],
            sems.at[bit],
        )
        for bit in range(devices)
    ]
    for copy in copies:
        copy.start()
    for copy in copies:
        copy.wait()


def join(me, pieces):
    devices = len(pieces)
    rows, part = pieces[0].shape
    return pl.pallas_call(
        functools.partial(join_body, devices, part),
        out_shape=jax.ShapeDtypeStruct((rows, devices * part), jnp.bfloat16),
        in_specs=[pl.BlockSpec(memory_space=pltpu.SMEM)] + anywhere(devices),
        out_specs=pl.BlockSpec(memory_space=pl.ANY),
        scratch_shapes=[pltpu.SemaphoreType.DMA((devices,))],
    )(me, *pieces)


def body(query, key, value, valid_rows):
    devices = lax.axis_size("head")
    columns = lax.axis_size("tok")
    height = columns // TIME_TILES
    tiles, tokens, width = query.shape
    heads = width // HEAD_DIM // devices
    me = lax.axis_index("head").astype(jnp.int32).reshape(1)
    flat = [field.reshape(tiles * tokens, width) for field in (query, key, value)]
    near, sibling, own_query, far, far_query = pack(me, valid_rows, *flat, devices)

    far = [swap_head(block, bit, devices) for bit, block in enumerate(far, 2)]
    base = [near] + far
    slots = [base]
    if height > 1:
        slots += [[swap_pairs(b, phase, 1, height, columns) for b in base] for phase in (0, 1)]
    slots += [
        [swap_pairs(b, phase, height, TIME_TILES, columns) for b in slot]
        for phase in (0, 1)
        for slot in slots
    ]
    sibling = swap_head(sibling, 1, devices)
    far_query = [swap_head(block, bit, devices) for bit, block in enumerate(far_query, 2)]
    queries = [own_query, sibling[2 * tiles * tokens :], *far_query]
    beside = [sibling] + [swap_head(slot[0], 1, devices) for slot in slots[1:]]
    slots = [[slot[0], other, *slot[1:]] for slot, other in zip(slots, beside)]

    pieces = attend(queries, slots, tiles, tokens, heads)
    pieces = [pieces[0]] + [
        swap_head(piece, bit, devices) for bit, piece in enumerate(pieces[1:], 1)
    ]
    return join(me, pieces).reshape(tiles, tokens, width)


def solution(mesh):
    placed = (
        P(("clips", "tok"), "head", None),
        P(("clips", "tok"), "head", None),
        P(("clips", "tok"), "head", None),
        P(("clips", "tok")),
    )
    return jax.shard_map(
        body,
        mesh=mesh,
        in_specs=placed,
        out_specs=P(("clips", "tok"), "head", None),
        check_vma=False,
    )
```

time: 206 us -> 149 us (0.72); the launches traced: 203 us -> 148 us
  Pallas kernels: 0 us -> 91.7 us
  local copies, waits for them, and re-layouts: 83.7 us -> 3.24 us
  matrix products: 30.1 us -> 0 us
  loops' own time: 18.8 us -> 0 us
  waiting for transfers between devices: 12.6 us -> 31.3 us
  blocking collectives: 15.3 us -> 0 us
  other arithmetic: 11.1 us -> 0 us
  starting transfers between devices: 30.8 us -> 21.7 us
    pallas_call x0 -> x3, Pallas kernels: none -> 91.7 us  [the longest x1 64.4 us: pack(): pl.pallas_call(functools.partial(pack_body, devices, part), out_shape=out...]
    while x126 -> x0, local copies, waits for them, and re-layouts: 33.3 us -> none
    dot_general x18 -> x0, matrix products: 30.1 us -> none  [the longest x9 18.3 us: attend(): jnp.einsum('qd,kd->qk', queries, block_keys, preferred_element_type=jnp.f...]
    ppermute x6 -> x16, waiting for transfers between devices: 6.77 us -> 31.3 us  [the longest x6 17.9 us: swap_pairs(): return lax.ppermute(block, 'tok', route)]
    another operation x1 -> x0, loops' own time: 18.8 us -> none  [body(): results = lax.map(attend, jnp.arange(width * local, dtype=jnp.int32))]
    all_to_all x1 -> x0, blocking collectives: 15.3 us -> none  [body(): lax.all_to_all(attended, 'head', split_axis=1, concat_axis=2, tiled=True)]
    all_to_all x3 -> x0, starting transfers between devices: 13.5 us -> none  [the longest x1 5.11 us: body(): lax.all_to_all(query, 'head', split_axis=2, concat_axis=1, tiled=True)]
    unnamed x16 -> x14, local copies, waits for them, and re-layouts: 15.9 us -> 3.23 us
  transfers between devices with their start and end apart: 9 -> 16, of which waited for: 4 -> 8; matrix products, arithmetic and copies ran while one was open for 13% -> 0% of each run, Pallas kernels for 0% -> 0%
where the time goes in v1:
time: 149 us; the launch traced here: 148 us
  Pallas kernels  91.7 us (62%)
  waiting for transfers between devices  31.3 us (21%)
  starting transfers between devices  21.7 us (15%)
  local copies, waits for them, and re-layouts  3.24 us (2%)
    pallas_call x1, Pallas kernels, pack(): pl.pallas_call(functools.partial(pack_body, devices, part), out_shape=out...  64.4 us
    pallas_call x1, Pallas kernels, join(): pl.pallas_call(functools.partial(join_body, devices, part), out_shape=jax...  19 us
    ppermute x6, waiting for transfers between devices, swap_pairs(): return lax.ppermute(block, 'tok', route)  17.9 us
    ppermute x10, starting transfers between devices, swap_head(): return lax.ppermute(block, 'head', [(i, i ^ bit) for i in range(devices)])  13.9 us
    ppermute x10, waiting for transfers between devices, swap_head(): return lax.ppermute(block, 'head', [(i, i ^ bit) for i in range(devices)])  13.4 us
    pallas_call x1, Pallas kernels, attend(): pl.pallas_call(functools.partial(attend_body, len(slots), frames, tiles,...  8.22 us
    ppermute x6, starting transfers between devices, swap_pairs(): return lax.ppermute(block, 'tok', route)  7.86 us
    unnamed x14, local copies, waits for them, and re-layouts  3.23 us
  transfers between devices with their start and end apart: 16, of which 8 were waited for; matrix products, arithmetic and copies ran while one was open for 0% of the time, Pallas kernels for 0%

profile of v1, /device:TPU:9, one launch (start us, length us, event | category | flops | bytes accessed | tf_op | source)
XLA Modules:
  0.0 148.1 jit_solution(2392029661348941270)
XLA Ops:
  0.0 64.4 %shard_map.46 = (bf16[784,384]{1,0:T(8,128)(2,1)}, bf16[576,384]{1,0:T(8,128)(2,1)}, bf16[192,384]{1,0:T(8,128)(2,1)}, bf16[384,384]{1,0:T(8,128)(2,1)}, bf16[38...) custom-call(s32[1]{0:T(128)} %bitcast.me_ref, s32[3]{0:T(128)} %counts_ref.1, ...), custom_call_target="tpu_custom_call" | custom-call | bytes 4718592 | tf_op jit(solution)/shard_map/pallas_call | solution.py:94
  64.4 3.2 %collective-permute-start.9 = (bf16[784,384]{1,0:T(8,128)(2,1)}, bf16[784,384]{1,0:T(8,128)(2,1)S(1)}, u32[]{:S(2)}, u32[]{:S(2)}) collective-permute-start(bf16[784,384]{1,0:T(8,128)(2,1)} %get-tuple-element.20.refs_4_), channel_id=1, source_target_pairs={{4,8},{8,4},{5,9},{9,5},{6,10},{10,6},{7,11},{11,7},{20,24},{24,20... | collective-permute-start | bytes 1806344 | tf_op jit(solution)/shard_map/ppermute | solution.py:38
  67.7 1.3 collective-permute-start.1
  69.3 2.6 %collective-permute-start.2 = (bf16[192,384]{1,0:T(8,128)(2,1)}, bf16[192,384]{1,0:T(8,128)(2,1)S(1)}, u32[]{:S(2)}, u32[]{:S(2)}) collective-permute-start(bf16[192,384]{1,0:T(8,128)(2,1)} %get-tuple-element.19), channel_id=1, source_target_pairs={{0,3},{1,2},{2,1},{3,0},{4,7},{5,6},{6,5},{7,4},{8,11},{9,10},{10,... | collective-permute-start | bytes 442376 | tf_op jit(solution)/shard_map/ppermute | solution.py:29
  72.4 3.3 %collective-permute-start = (bf16[576,384]{1,0:T(8,128)(2,1)}, bf16[576,384]{1,0:T(8,128)(2,1)S(1)}, u32[]{:S(2)}, u32[]{:S(2)}) collective-permute-start(bf16[576,384]{1,0:T(8,128)(2,1)} %get-tuple-element.17), channel_id=1, source_target_pairs={{0,1},{1,0},{2,3},{3,2},{4,5},{5,4},{6,7},{7,6},{8,9},{9,8},{10,11... | collective-permute-start | bytes 1327112 | tf_op jit(solution)/shard_map/ppermute | solution.py:29
  75.7 5.3 %collective-permute-done.9.refs_12_ = bf16[784,384]{1,0:T(8,128)(2,1)S(1)} collective-permute-done((bf16[784,384]{1,0:T(8,128)(2,1)}, bf16[784,384]{1,0:T(8,128)(2,1)S(1)}, u32[]{:S(2)}, u32[]{:S(2)}) %collective-permute-start.9) | collective-permute-done | bytes 602144 | tf_op jit(solution)/shard_map/ppermute | solution.py:38
  81.0 1.5 %collective-permute-start.10 = (bf16[784,384]{1,0:T(8,128)(2,1)S(1)}, bf16[784,384]{1,0:T(8,128)(2,1)S(1)}, u32[]{:S(2)}, u32[]{:S(2)}) collective-permute-start(bf16[784,384]{1,0:T(8,128)(2,1)S(1)} %collective-permute-done.9.refs_12_), channel_id=1, source_target_pairs={{0,1},{1,0},{2,3},{3,2},{4,5},{5,4},{6,7},{7,6},{8,9},{9,8},{10,11... | collective-permute-start | bytes 1806344 | tf_op jit(solution)/shard_map/ppermute | solution.py:29
  82.6 1.4 collective-permute-start.6
  83.9 1.2 collective-permute-start.4
  85.1 2.3 %collective-permute-start.11 = (bf16[384,384]{1,0:T(8,128)(2,1)S(1)}, bf16[384,384]{1,0:T(8,128)(2,1)S(1)}, u32[]{:S(2)}, u32[]{:S(2)}) collective-permute-start(bf16[384,384]{1,0:T(8,128)(2,1)S(1)} %collective-permute-done.3.refs_6_), channel_id=1, source_target_pairs={{4,8},{8,4},{5,9},{9,5},{6,10},{10,6},{7,11},{11,7},{20,24},{24,20... | collective-permute-start | bytes 884744 | tf_op jit(solution)/shard_map/ppermute | solution.py:38
  87.4 5.8 %collective-permute-done.4.refs_7_ = bf16[384,384]{1,0:T(8,128)(2,1)S(1)} collective-permute-done((bf16[384,384]{1,0:T(8,128)(2,1)}, bf16[384,384]{1,0:T(8,128)(2,1)S(1)}, u32[]{:S(2)}, u32[]{:S(2)}) %collective-permute-start.4) | collective-permute-done | bytes 294944 | tf_op jit(solution)/shard_map/ppermute | solution.py:29
  93.2 2.2 %collective-permute-start.12 = (bf16[384,384]{1,0:T(8,128)(2,1)S(1)}, bf16[384,384]{1,0:T(8,128)(2,1)S(1)}, u32[]{:S(2)}, u32[]{:S(2)}) collective-permute-start(bf16[384,384]{1,0:T(8,128)(2,1)S(1)} %collective-permute-done.4.refs_7_), channel_id=1, source_target_pairs={{4,8},{8,4},{5,9},{9,5},{6,10},{10,6},{7,11},{11,7},{20,24},{24,20... | collective-permute-start | bytes 884744 | tf_op jit(solution)/shard_map/ppermute | solution.py:38
  95.5 6.4 %collective-permute-done.7.refs_10_ = bf16[384,384]{1,0:T(8,128)(2,1)S(1)} collective-permute-done((bf16[384,384]{1,0:T(8,128)(2,1)S(1)}, bf16[384,384]{1,0:T(8,128)(2,1)S(1)}, u32[]{:S(2)}, u32[]{:S(2)}) %collective-permute-start.7) | collective-permute-done | bytes 294944 | tf_op jit(solution)/shard_map/ppermute | solution.py:38
  101.9 1.6 %collective-permute-done.12.refs_15_ = bf16[384,384]{1,0:T(8,128)(2,1)S(1)} collective-permute-done((bf16[384,384]{1,0:T(8,128)(2,1)S(1)}, bf16[384,384]{1,0:T(8,128)(2,1)S(1)}, u32[]{:S(2)}, u32[]{:S(2)}) %collective-permute-start.12) | collective-permute-done | bytes 294944 | tf_op jit(solution)/shard_map/ppermute | solution.py:38
  103.5 4.7 %collective-permute-done.8.refs_11_ = bf16[384,384]{1,0:T(8,128)(2,1)S(1)} collective-permute-done((bf16[384,384]{1,0:T(8,128)(2,1)S(1)}, bf16[384,384]{1,0:T(8,128)(2,1)S(1)}, u32[]{:S(2)}, u32[]{:S(2)}) %collective-permute-start.8) | collective-permute-done | bytes 294944 | tf_op jit(solution)/shard_map/ppermute | solution.py:38
  108.2 0.8 copy-done.6
  109.1 1.1 copy-done.1
  110.1 8.2 %shard_map.47 = (bf16[192,384]{1,0:T(8,128)(2,1)S(1)}, bf16[192,384]{1,0:T(8,128)(2,1)S(1)}, bf16[192,384]{1,0:T(8,128)(2,1)S(1)}, bf16[192,384]{1,0:T(8,128)(2,1)S(1)}) custom-call(bf16[192,384]{1,0:T(8,128)(2,1)S(1)} %copy-done.2, bf16[192,384]{1,0:T(8,128)(2,1)S(1)} %slice.4.refs_1_, bf16[192,384]{1,0:T(8,128)(2,1)S(1)} %collective-permute-done.1.refs_2_, ...), custom_call_target="tpu_custom_call" | custom-call | flops 2113929216 | tf_op jit(solution)/shard_map/pallas_call | solution.py:164
  119.0 0.7 collective-permute-start.13
  119.7 1.2 collective-permute-start.14
  121.3 3.8 %collective-permute-done.14.rest_2_ = bf16[192,384]{1,0:T(8,128)(2,1)S(1)} collective-permute-done((bf16[192,384]{1,0:T(8,128)(2,1)S(1)}, bf16[192,384]{1,0:T(8,128)(2,1)S(1)}, u32[]{:S(2)}, u32[]{:S(2)}) %collective-permute-start.14) | collective-permute-done | bytes 147488 | tf_op jit(solution)/shard_map/ppermute | solution.py:29
  125.2 3.3 %collective-permute-done.15.rest_3_ = bf16[192,384]{1,0:T(8,128)(2,1)S(1)} collective-permute-done((bf16[192,384]{1,0:T(8,128)(2,1)S(1)}, bf16[192,384]{1,0:T(8,128)(2,1)S(1)}, u32[]{:S(2)}, u32[]{:S(2)}) %collective-permute-start.15) | collective-permute-done | bytes 147488 | tf_op jit(solution)/shard_map/ppermute | solution.py:29
  128.4 0.7 copy-done.5
  129.1 19.0 %shard_map.48 = bf16[192,1536]{1,0:T(8,128)(2,1)} custom-call(s32[1]{0:T(128)} %bitcast.me_ref, bf16[192,384]{1,0:T(8,128)(2,1)} %copy-done, bf16[192,384]{1,0:T(8,128)(2,1)} %copy-done.3, bf16[192,384]{1,0:T(8,128)(2,1)} %copy-done.4, bf16[192,384]{1,0:T(8,128)(2,1)} %copy-done.5), custom_call_target="tpu_custom_call" | custom-call | tf_op jit(solution)/shard_map/pallas_call | solution.py:196
  (26 shorter events, 2.1 us)
Async XLA Ops:
  64.4 16.6 %collective-permute-start.9 = (bf16[784,384]{1,0:T(8,128)(2,1)}, bf16[784,384]{1,0:T(8,128)(2,1)S(1)}, u32[]{:S(2)}, u32[]{:S(2)}) collective-permute-start(bf16[784,384]{1,0:T(8,128)(2,1)} %get-tuple-element.20.refs_4_), channel_id=1, source_target_pairs={{4,8},{8,4},{5,9},{9,5},{6,10},{10,6},{7,11},{11,7},{20,24},{24,20... | collective-permute-start | bytes 1806344 | tf_op jit(solution)/shard_map/ppermute | solution.py:38
  67.7 14.9 %collective-permute-start.5 = (bf16[784,384]{1,0:T(8,128)(2,1)}, bf16[784,384]{1,0:T(8,128)(2,1)S(1)}, u32[]{:S(2)}, u32[]{:S(2)}) collective-permute-start(bf16[784,384]{1,0:T(8,128)(2,1)} %get-tuple-element.20.refs_4_), channel_id=1, source_target_pairs={{0,4},{4,0},{8,12},{12,8},{1,5},{5,1},{9,13},{13,9},{2,6},{6,2},{1... | collective-permute-start | bytes 1806344 | tf_op jit(solution)/shard_map/ppermute | solution.py:38
  67.7 4.7 %collective-permute-start.1 = (bf16[192,384]{1,0:T(8,128)(2,1)}, bf16[192,384]{1,0:T(8,128)(2,1)S(1)}, u32[]{:S(2)}, u32[]{:S(2)}) collective-permute-start(bf16[192,384]{1,0:T(8,128)(2,1)} %get-tuple-element.18), channel_id=1, source_target_pairs={{0,2},{1,3},{2,0},{3,1},{4,6},{5,7},{6,4},{7,5},{8,10},{9,11},{10,... | collective-permute-start | bytes 442376 | tf_op jit(solution)/shard_map/ppermute | solution.py:29
  69.0 16.1 %collective-permute-start.3 = (bf16[384,384]{1,0:T(8,128)(2,1)}, bf16[384,384]{1,0:T(8,128)(2,1)S(1)}, u32[]{:S(2)}, u32[]{:S(2)}) collective-permute-start(bf16[384,384]{1,0:T(8,128)(2,1)} %get-tuple-element.21), channel_id=1, source_target_pairs={{0,2},{1,3},{2,0},{3,1},{4,6},{5,7},{6,4},{7,5},{8,10},{9,11},{10,... | collective-permute-start | bytes 884744 | tf_op jit(solution)/shard_map/ppermute | solution.py:29
  69.3 14.7 %collective-permute-start.2 = (bf16[192,384]{1,0:T(8,128)(2,1)}, bf16[192,384]{1,0:T(8,128)(2,1)S(1)}, u32[]{:S(2)}, u32[]{:S(2)}) collective-permute-start(bf16[192,384]{1,0:T(8,128)(2,1)} %get-tuple-element.19), channel_id=1, source_target_pairs={{0,3},{1,2},{2,1},{3,0},{4,7},{5,6},{6,5},{7,4},{8,11},{9,10},{10,... | collective-permute-start | bytes 442376 | tf_op jit(solution)/shard_map/ppermute | solution.py:29
  72.4 20.7 %collective-permute-start = (bf16[576,384]{1,0:T(8,128)(2,1)}, bf16[576,384]{1,0:T(8,128)(2,1)S(1)}, u32[]{:S(2)}, u32[]{:S(2)}) collective-permute-start(bf16[576,384]{1,0:T(8,128)(2,1)} %get-tuple-element.17), channel_id=1, source_target_pairs={{0,1},{1,0},{2,3},{3,2},{4,5},{5,4},{6,7},{7,6},{8,9},{9,8},{10,11... | collective-permute-start | bytes 1327112 | tf_op jit(solution)/shard_map/ppermute | solution.py:29
  81.0 27.2 %collective-permute-start.10 = (bf16[784,384]{1,0:T(8,128)(2,1)S(1)}, bf16[784,384]{1,0:T(8,128)(2,1)S(1)}, u32[]{:S(2)}, u32[]{:S(2)}) collective-permute-start(bf16[784,384]{1,0:T(8,128)(2,1)S(1)} %collective-permute-done.9.refs_12_), channel_id=1, source_target_pairs={{0,1},{1,0},{2,3},{3,2},{4,5},{5,4},{6,7},{7,6},{8,9},{9,8},{10,11... | collective-permute-start | bytes 1806344 | tf_op jit(solution)/shard_map/ppermute | solution.py:29
  82.6 25.6 %collective-permute-start.6 = (bf16[784,384]{1,0:T(8,128)(2,1)S(1)}, bf16[784,384]{1,0:T(8,128)(2,1)S(1)}, u32[]{:S(2)}, u32[]{:S(2)}) collective-permute-start(bf16[784,384]{1,0:T(8,128)(2,1)S(1)} %collective-permute-done.5.refs_8_), channel_id=1, source_target_pairs={{0,1},{1,0},{2,3},{3,2},{4,5},{5,4},{6,7},{7,6},{8,9},{9,8},{10,11... | collective-permute-start | bytes 1806344 | tf_op jit(solution)/shard_map/ppermute | solution.py:29
  83.9 25.1 %copy-start.2 = (bf16[192,384]{1,0:T(8,128)(2,1)S(1)}, bf16[192,384]{1,0:T(8,128)(2,1)}, u32[]{:S(2)}) copy-start(bf16[192,384]{1,0:T(8,128)(2,1)} %get-tuple-element.16.refs_0_) | copy-start | bytes 442372
  83.9 9.2 %collective-permute-start.4 = (bf16[384,384]{1,0:T(8,128)(2,1)}, bf16[384,384]{1,0:T(8,128)(2,1)S(1)}, u32[]{:S(2)}, u32[]{:S(2)}) collective-permute-start(bf16[384,384]{1,0:T(8,128)(2,1)} %get-tuple-element.22), channel_id=1, source_target_pairs={{0,3},{1,2},{2,1},{3,0},{4,7},{5,6},{6,5},{7,4},{8,11},{9,10},{10,... | collective-permute-start | bytes 884744 | tf_op jit(solution)/shard_map/ppermute | solution.py:29
  85.1 10.3 %collective-permute-start.11 = (bf16[384,384]{1,0:T(8,128)(2,1)S(1)}, bf16[384,384]{1,0:T(8,128)(2,1)S(1)}, u32[]{:S(2)}, u32[]{:S(2)}) collective-permute-start(bf16[384,384]{1,0:T(8,128)(2,1)S(1)} %collective-permute-done.3.refs_6_), channel_id=1, source_target_pairs={{4,8},{8,4},{5,9},{9,5},{6,10},{10,6},{7,11},{11,7},{20,24},{24,20... | collective-permute-start | bytes 884744 | tf_op jit(solution)/shard_map/ppermute | solution.py:38
  93.1 8.7 %collective-permute-start.7 = (bf16[384,384]{1,0:T(8,128)(2,1)S(1)}, bf16[384,384]{1,0:T(8,128)(2,1)S(1)}, u32[]{:S(2)}, u32[]{:S(2)}) collective-permute-start(bf16[384,384]{1,0:T(8,128)(2,1)S(1)} %collective-permute-done.3.refs_6_), channel_id=1, source_target_pairs={{0,4},{4,0},{8,12},{12,8},{1,5},{5,1},{9,13},{13,9},{2,6},{6,2},{1... | collective-permute-start | bytes 884744 | tf_op jit(solution)/shard_map/ppermute | solution.py:38
  93.2 10.3 %collective-permute-start.12 = (bf16[384,384]{1,0:T(8,128)(2,1)S(1)}, bf16[384,384]{1,0:T(8,128)(2,1)S(1)}, u32[]{:S(2)}, u32[]{:S(2)}) collective-permute-start(bf16[384,384]{1,0:T(8,128)(2,1)S(1)} %collective-permute-done.4.refs_7_), channel_id=1, source_target_pairs={{4,8},{8,4},{5,9},{9,5},{6,10},{10,6},{7,11},{11,7},{20,24},{24,20... | collective-permute-start | bytes 884744 | tf_op jit(solution)/shard_map/ppermute | solution.py:38
  95.4 12.8 %collective-permute-start.8 = (bf16[384,384]{1,0:T(8,128)(2,1)S(1)}, bf16[384,384]{1,0:T(8,128)(2,1)S(1)}, u32[]{:S(2)}, u32[]{:S(2)}) collective-permute-start(bf16[384,384]{1,0:T(8,128)(2,1)S(1)} %collective-permute-done.4.refs_7_), channel_id=1, source_target_pairs={{0,4},{4,0},{8,12},{12,8},{1,5},{5,1},{9,13},{13,9},{2,6},{6,2},{1... | collective-permute-start | bytes 884744 | tf_op jit(solution)/shard_map/ppermute | solution.py:38
  108.2 0.9 copy-start.6
  109.1 1.1 copy-start.1
  118.3 0.7 copy-start
  119.0 2.3 %collective-permute-start.13 = (bf16[192,384]{1,0:T(8,128)(2,1)S(1)}, bf16[192,384]{1,0:T(8,128)(2,1)S(1)}, u32[]{:S(2)}, u32[]{:S(2)}) collective-permute-start(bf16[192,384]{1,0:T(8,128)(2,1)S(1)} %get-tuple-element.24), channel_id=1, source_target_pairs={{0,1},{1,0},{2,3},{3,2},{4,5},{5,4},{6,7},{7,6},{8,9},{9,8},{10,11... | collective-permute-start | bytes 442376 | tf_op jit(solution)/shard_map/ppermute | solution.py:29
  119.7 5.5 %collective-permute-start.14 = (bf16[192,384]{1,0:T(8,128)(2,1)S(1)}, bf16[192,384]{1,0:T(8,128)(2,1)S(1)}, u32[]{:S(2)}, u32[]{:S(2)}) collective-permute-start(bf16[192,384]{1,0:T(8,128)(2,1)S(1)} %get-tuple-element.25), channel_id=1, source_target_pairs={{0,2},{1,3},{2,0},{3,1},{4,6},{5,7},{6,4},{7,5},{8,10},{9,11},{10,... | collective-permute-start | bytes 442376 | tf_op jit(solution)/shard_map/ppermute | solution.py:29
  120.9 7.5 %collective-permute-start.15 = (bf16[192,384]{1,0:T(8,128)(2,1)S(1)}, bf16[192,384]{1,0:T(8,128)(2,1)S(1)}, u32[]{:S(2)}, u32[]{:S(2)}) collective-permute-start(bf16[192,384]{1,0:T(8,128)(2,1)S(1)} %get-tuple-element.26), channel_id=1, source_target_pairs={{0,3},{1,2},{2,1},{3,0},{4,7},{5,6},{6,5},{7,4},{8,11},{9,10},{10,... | collective-permute-start | bytes 442376 | tf_op jit(solution)/shard_map/ppermute | solution.py:29
  121.3 7.1 %copy-start.3 = (bf16[192,384]{1,0:T(8,128)(2,1)}, bf16[192,384]{1,0:T(8,128)(2,1)S(1)}, u32[]{:S(2)}) copy-start(bf16[192,384]{1,0:T(8,128)(2,1)S(1)} %collective-permute-done.13.rest_1_) | copy-start | bytes 442372
  125.2 3.3 %copy-start.4 = (bf16[192,384]{1,0:T(8,128)(2,1)}, bf16[192,384]{1,0:T(8,128)(2,1)S(1)}, u32[]{:S(2)}) copy-start(bf16[192,384]{1,0:T(8,128)(2,1)S(1)} %collective-permute-done.14.rest_2_) | copy-start | bytes 442372
  128.4 0.7 copy-start.5

commit v2 on v1

v2 whole, which is shorter than its diff:
```python
import functools
import math

import jax
import jax.numpy as jnp
from jax import lax
from jax.experimental import pallas as pl
from jax.experimental.pallas import tpu as pltpu
from jax.sharding import PartitionSpec as P

HEAD_DIM = 128
TILE_H = 8
TILE_W = 8
TIME_TILES = 4
COUNT_ROWS = 16
MASKED = -1e30
VMEM_LIMIT = 24 * 2**20


def in_vmem(count):
    return [pl.BlockSpec(memory_space=pltpu.VMEM)] * count


def swap_head(block, bit, devices):
    return lax.ppermute(block, "head", [(i, i ^ bit) for i in range(devices)])


def swap_pairs(block, phase, stride, length, devices):
    route = []
    for i in range(devices):
        place = i // stride % length
        if place % 2 == phase and place + 1 < length:
            route += [(i, i + stride), (i + stride, i)]
    return lax.ppermute(block, "tok", route)


def pack_body(devices, part, counts_in, me_ref, q_ref, k_ref, v_ref, *rest):
    own_ref, sibling_ref, own_q_ref = rest[:3]
    far_refs, far_q_refs = rest[3 : 1 + devices], rest[1 + devices : 2 * devices - 1]
    counts_ref, count_sem, sems = rest[2 * devices - 1 :]
    rows = k_ref.shape[0]
    me = me_ref[0]

    def lanes(bit):
        return pl.ds(pl.multiple_of((me ^ bit) * part, HEAD_DIM), part)

    count_copy = pltpu.make_async_copy(counts_in, counts_ref, count_sem)
    count_copy.start()
    jobs = []
    for bit, ref in [(1, sibling_ref), *enumerate(far_refs, 2), (0, own_ref)]:
        jobs += [
            (k_ref.at[:, lanes(bit)], ref.at[pl.ds(0, rows)]),
            (v_ref.at[:, lanes(bit)], ref.at[pl.ds(rows, rows)]),
        ]
    jobs += [
        (q_ref.at[:, lanes(1)], sibling_ref.at[pl.ds(2 * rows, rows)]),
        (q_ref.at[:, lanes(0)], own_q_ref),
    ]
    jobs += [(q_ref.at[:, lanes(bit)], ref) for bit, ref in enumerate(far_q_refs, 2)]
    copies = [pltpu.make_async_copy(src, dst, sems.at[i]) for i, (src, dst) in enumerate(jobs)]
    for copy in copies:
        copy.start()
    count_copy.wait()
    shape = (COUNT_ROWS, part)
    row = lax.broadcasted_iota(jnp.int32, shape, 0)
    filled = jnp.zeros(shape, jnp.float32)
    for tile in range(counts_ref.shape[0]):
        filled = jnp.where(row == tile, counts_ref[tile].astype(jnp.float32), filled)
    own_ref[pl.ds(2 * rows, COUNT_ROWS), :] = filled.astype(jnp.bfloat16)
    for copy in copies:
        copy.wait()


def pack(me, counts, query, key, value, devices):
    rows, width = query.shape
    part = width // devices
    far = devices - 2
    sizes = [2 * rows + COUNT_ROWS, 3 * rows, rows] + [2 * rows] * far + [rows] * far
    fields = [pltpu.with_memory_space_constraint(f, pltpu.HBM) for f in (query, key, value)]
    results = pl.pallas_call(
        functools.partial(pack_body, devices, part),
        out_shape=[pltpu.VMEM((size, part), jnp.bfloat16) for size in sizes],
        in_specs=[pl.BlockSpec(memory_space=pltpu.HBM), pl.BlockSpec(memory_space=pltpu.SMEM)]
        + [pl.BlockSpec(memory_space=pltpu.HBM)] * 3,
        out_specs=in_vmem(len(sizes)),
        scratch_shapes=[
            pltpu.SMEM(counts.shape, jnp.int32),
            pltpu.SemaphoreType.DMA,
            pltpu.SemaphoreType.DMA((3 * devices,)),
        ],
        compiler_params=pltpu.CompilerParams(vmem_limit_bytes=VMEM_LIMIT),
        cost_estimate=pl.CostEstimate(flops=0, bytes_accessed=12 * query.size, transcendentals=0),
    )(pltpu.with_memory_space_constraint(counts, pltpu.HBM), me, *fields)
    return results[0], results[1], results[2], results[3 : 3 + far], results[3 + far :]


def stack_body(sizes, *refs):
    blocks, out_ref, sems = refs[:-2], refs[-2], refs[-1]
    copies = [
        pltpu.make_async_copy(
            block.at[pl.ds(0, size)], out_ref.at[pl.ds(sum(sizes[:i]), size)], sems.at[i]
        )
        for i, (block, size) in enumerate(zip(blocks, sizes))
    ]
    for copy in copies:
        copy.start()
    for copy in copies:
        copy.wait()


def stack(blocks, sizes):
    width = blocks[0].shape[1]
    return pl.pallas_call(
        functools.partial(stack_body, sizes),
        out_shape=pltpu.VMEM((sum(sizes), width), jnp.bfloat16),
        in_specs=in_vmem(len(blocks)),
        out_specs=pl.BlockSpec(memory_space=pltpu.VMEM),
        scratch_shapes=[pltpu.SemaphoreType.DMA((len(blocks),))],
        compiler_params=pltpu.CompilerParams(vmem_limit_bytes=VMEM_LIMIT),
        cost_estimate=pl.CostEstimate(
            flops=0, bytes_accessed=sum(sizes) * width, transcendentals=0
        ),
    )(*blocks)


def bias_of(counts, tiles, tokens, copies):
    lane = lax.broadcasted_iota(jnp.int32, (1, HEAD_DIM), 1)
    row = (lane // TILE_W % TILE_H).astype(jnp.float32)
    counted = counts.astype(jnp.float32)
    rows = [jnp.where(row < counted[n : n + 1], 0.0, MASKED) for n in range(tiles)]
    return [jnp.concatenate([r] * (copies * tokens // HEAD_DIM), 1) for r in rows]


def attend_body(groups, operands, frames, tiles, tokens, heads, first, early, *refs):
    rows = tiles * tokens
    refs = list(refs)
    queries = [refs.pop(0) for _ in range(frames)]
    arrays = [refs.pop(0) for _ in range(operands)]
    biases = []
    for counts, fields in groups:
        counted = arrays[counts][pl.ds(2 * rows, COUNT_ROWS), pl.ds(0, HEAD_DIM)]
        biases.append(bias_of(counted, tiles, tokens, len(fields)))
    outs = refs if early else refs[3:]
    scale = math.log2(math.e) / math.sqrt(HEAD_DIM)
    block = frames * tokens

    for head in range(heads):
        lanes = pl.ds((first + head) * HEAD_DIM, HEAD_DIM)
        for tile in range(tiles):
            window = [
                (group, near)
                for near in range(max(tile - 1, 0), min(tile + 2, tiles))
                for group in range(len(groups))
            ]

            def gathered(which):
                return jnp.concatenate(
                    [
                        arrays[i][pl.ds(base + which * rows + near * tokens, tokens), lanes]
                        for group, near in window
                        for i, base in groups[group][1]
                    ],
                    0,
                )

            asked = jnp.concatenate([ref[pl.ds(tile * tokens, tokens), lanes] for ref in queries], 0)
            scores = lax.dot_general(
                asked, gathered(0), (((1,), (1,)), ((), ())), preferred_element_type=jnp.float32
            )
            scores = scores + jnp.concatenate([biases[group][near] for group, near in window], 1)
            largest = jnp.max(scores, axis=1, keepdims=True)
            place = pl.ds(((first + head) * tiles + tile) * block, block)
            if not early:
                before = refs[0][place, :]
                largest = jnp.maximum(before[:, :1], largest)
                shrink = jnp.exp2((before - largest) * scale)
            weight = jnp.exp2((scores - largest) * scale)
            total = jnp.sum(weight, axis=1, keepdims=True)
            summed = jnp.dot(
                weight.astype(jnp.bfloat16), gathered(1), preferred_element_type=jnp.float32
            )
            if early:
                outs[0][place, :] = jnp.broadcast_to(largest, (block, HEAD_DIM))
                outs[1][place, :] = jnp.broadcast_to(total, (block, HEAD_DIM))
                outs[2][place, :] = summed
                continue
            total = total + refs[1][place, :] * shrink
            summed = summed + refs[2][place, :] * shrink
            result = (summed / total).astype(jnp.bfloat16)
            for frame in range(frames):
                outs[frame][pl.ds(tile * tokens, tokens), pl.ds(head * HEAD_DIM, HEAD_DIM)] = result[
                    frame * tokens : (frame + 1) * tokens
                ]


def attend(queries, arrays, groups, tiles, tokens, heads, first=0, state=(), weigh=1):
    frames = len(queries)
    operands = [*queries, *arrays, *state]
    size = sum(len(fields) for _, fields in groups)
    pairs = heads * (3 * tiles - 2) * size * tokens * frames * tokens
    if state:
        outs = [pltpu.VMEM((tiles * tokens, heads * HEAD_DIM), jnp.bfloat16)] * frames
    else:
        left = (heads * tiles * frames * tokens, HEAD_DIM)
        outs = [pltpu.VMEM(left, jnp.float32)] * 3
    return pl.pallas_call(
        functools.partial(
            attend_body, groups, len(arrays), frames, tiles, tokens, heads, first, not state
        ),
        out_shape=outs,
        in_specs=in_vmem(len(operands)),
        out_specs=in_vmem(len(outs)),
        compiler_params=pltpu.CompilerParams(vmem_limit_bytes=VMEM_LIMIT),
        cost_estimate=pl.CostEstimate(
            flops=weigh * 4 * HEAD_DIM * pairs, bytes_accessed=0, transcendentals=weigh * pairs
        ),
    )(*operands)


def join_body(devices, sizes, me_ref, *rest):
    out_ref, sems = rest[-2:]
    me = me_ref[0]
    copies = []
    for part, size in enumerate(sizes):
        for bit in range(devices):
            start = (me ^ bit) * sum(sizes) + sum(sizes[:part])
            copies.append(
                pltpu.make_async_copy(
                    rest[len(copies)],
                    out_ref.at[:, pl.ds(pl.multiple_of(start, HEAD_DIM), size)],
                    sems.at[len(copies)],
                )
            )
    for copy in copies:
        copy.start()
    for copy in copies:
        copy.wait()


def join(me, pieces):
    devices = len(pieces[0])
    rows = pieces[0][0].shape[0]
    sizes = [part[0].shape[1] for part in pieces]
    flat = [block for part in pieces for block in part]
    return pl.pallas_call(
        functools.partial(join_body, devices, sizes),
        out_shape=jax.ShapeDtypeStruct((rows, devices * sum(sizes)), jnp.bfloat16),
        in_specs=[pl.BlockSpec(memory_space=pltpu.SMEM)] + in_vmem(len(flat)),
        out_specs=pl.BlockSpec(memory_space=pl.ANY),
        scratch_shapes=[pltpu.SemaphoreType.DMA((len(flat),))],
        compiler_params=pltpu.CompilerParams(vmem_limit_bytes=VMEM_LIMIT),
    )(me, *flat)


def body(query, key, value, valid_rows):
    devices = lax.axis_size("head")
    columns = lax.axis_size("tok")
    height = columns // TIME_TILES
    tiles, tokens, width = query.shape
    heads = width // HEAD_DIM // devices
    me = lax.axis_index("head").astype(jnp.int32).reshape(1)
    flat = [field.reshape(tiles * tokens, width) for field in (query, key, value)]
    own, sibling, own_query, far, far_query = pack(me, valid_rows, *flat, devices)
    rows = tiles * tokens

    sibling = swap_head(sibling, 1, devices)
    far = [swap_head(b, bit, devices) for bit, b in enumerate(far, 2)]
    far_query = [swap_head(b, bit, devices) for bit, b in enumerate(far_query, 2)]
    queries = [own_query, sibling[2 * rows :], *far_query]
    near = stack([own, sibling], [own.shape[0], 2 * rows])
    across = stack(far, [2 * rows] * len(far))
    slots = [(near, across)]
    if height > 1:
        slots += [
            tuple(swap_pairs(b, phase, 1, height, columns) for b in slots[0]) for phase in (0, 1)
        ]
    slots += [
        tuple(swap_pairs(b, phase, height, TIME_TILES, columns) for b in slot)
        for phase in (0, 1)
        for slot in slots
    ]
    near_rows = [0, own.shape[0]]
    far_rows = [2 * rows * i for i in range(devices - 2)]
    arrays = [across] + [mine for mine, _ in slots]
    groups = [(i, [(i, base) for base in near_rows]) for i in range(1, len(arrays))]
    groups[0][1].extend((0, base) for base in far_rows)
    state = attend(queries, arrays, groups, tiles, tokens, heads)

    arrays = [array for slot in slots[1:] for array in slot]
    groups = [(i, [(i + 1, base) for base in far_rows]) for i in range(0, len(arrays), 2)]
    cut = heads - heads // 3
    pieces = []
    for first, count in ((0, cut), (cut, heads - cut)):
        results = attend(
            queries, arrays, groups, tiles, tokens, count, first, state, weigh=int(first == 0)
        )
        results, state = lax.optimization_barrier((results, state))
        pieces.append(
            [results[0]] + [swap_head(b, bit, devices) for bit, b in enumerate(results[1:], 1)]
        )
    return join(me, pieces).reshape(tiles, tokens, width)


def solution(mesh):
    placed = (
        P(("clips", "tok"), "head", None),
        P(("clips", "tok"), "head", None),
        P(("clips", "tok"), "head", None),
        P(("clips", "tok")),
    )
    return jax.shard_map(
        body,
        mesh=mesh,
        in_specs=placed,
        out_specs=P(("clips", "tok"), "head", None),
        check_vma=False,
    )
```

time: 149 us -> 54.5 us (0.37)
  Pallas kernels: 91.7 us -> 12.5 us
  waiting for transfers between devices: 31.3 us -> 22.1 us
  local copies, waits for them, and re-layouts: 3.24 us -> 0.02 us
  starting transfers between devices: 21.7 us -> 19.6 us
    pallas_call x3 -> x7, Pallas kernels: 91.7 us -> 12.5 us  [the longest x3 9.73 us: attend(): pl.pallas_call(functools.partial(attend_body, groups, len(arrays), frames...]
    ppermute x6 -> x4, waiting for transfers between devices: 17.9 us -> 0.01 us  [swap_pairs(): return lax.ppermute(block, 'tok', route)]
    ppermute x10 -> x11, waiting for transfers between devices: 13.4 us -> 22.1 us  [swap_head(): return lax.ppermute(block, 'head', [(i, i ^ bit) for i in range(devices)])]
    ppermute x10 -> x11, starting transfers between devices: 13.9 us -> 10.5 us  [swap_head(): return lax.ppermute(block, 'head', [(i, i ^ bit) for i in range(devices)])]
    unnamed x14 -> x0, local copies, waits for them, and re-layouts: 3.23 us -> none
    ppermute x6 -> x4, starting transfers between devices: 7.86 us -> 9.09 us  [swap_pairs(): return lax.ppermute(block, 'tok', route)]
  transfers between devices with their start and end apart: 16 -> 15, of which waited for: 8 -> 6; matrix products, arithmetic and copies ran while one was open for 0% -> 0% of each run, Pallas kernels for 0% -> 10%
where the time goes in v2:
time: 54.5 us; the launch traced here: 54.4 us
  waiting for transfers between devices  22.1 us (41%)
  starting transfers between devices  19.6 us (36%)
  Pallas kernels  12.5 us (23%)
    ppermute x11, waiting for transfers between devices, swap_head(): return lax.ppermute(block, 'head', [(i, i ^ bit) for i in range(devices)])  22.1 us
    ppermute x11, starting transfers between devices, swap_head(): return lax.ppermute(block, 'head', [(i, i ^ bit) for i in range(devices)])  10.5 us
    pallas_call x3, Pallas kernels, attend(): pl.pallas_call(functools.partial(attend_body, groups, len(arrays), frames...  9.73 us
    ppermute x4, starting transfers between devices, swap_pairs(): return lax.ppermute(block, 'tok', route)  9.09 us
    pallas_call x1, Pallas kernels, pack(): pl.pallas_call(functools.partial(pack_body, devices, part), out_shape=[pl...  1.64 us
  transfers between devices with their start and end apart: 15, of which 6 were waited for; matrix products, arithmetic and copies ran while one was open for 0% of the time, Pallas kernels for 10%

profile of v2, /device:TPU:9, one launch (start us, length us, event | category | flops | bytes accessed | tf_op | source)
XLA Modules:
  0.0 54.4 jit_solution(9646302467845466722)
XLA Ops:
  0.0 1.6 %shard_map.46 = (bf16[400,384]{1,0:T(8,128)(2,1)S(1)}, bf16[576,384]{1,0:T(8,128)(2,1)S(1)}, bf16[192,384]{1,0:T(8,128)(2,1)S(1)}, bf16[384,384]{1,0:T(8,128)(2,...) custom-call(s32[3]{0:T(128)} %counts_in.1, s32[1]{0:T(128)} %bitcast.me_ref, ...), custom_call_target="tpu_custom_call" | custom-call | bytes 3538944 | tf_op jit(solution)/shard_map/pallas_call | solution.py:80
  1.6 0.7 %collective-permute-start = (bf16[576,384]{1,0:T(8,128)(2,1)S(1)}, bf16[576,384]{1,0:T(8,128)(2,1)S(1)}, u32[]{:S(2)}, u32[]{:S(2)}) collective-permute-start(bf16[576,384]{1,0:T(8,128)(2,1)S(1)} %get-tuple-element.35), channel_id=1, source_target_pairs={{0,1},{1,0},{2,3},{3,2},{4,5},{5,4},{6,7},{7,6},{8,9},{9,8},{10,11... | collective-permute-start | bytes 1327112 | tf_op jit(solution)/shard_map/ppermute | solution.py:25
  2.4 1.2 %collective-permute-start.4 = (bf16[384,384]{1,0:T(8,128)(2,1)S(1)}, bf16[384,384]{1,0:T(8,128)(2,1)S(1)}, u32[]{:S(2)}, u32[]{:S(2)}) collective-permute-start(bf16[384,384]{1,0:T(8,128)(2,1)S(1)} %get-tuple-element.39), channel_id=1, source_target_pairs={{0,2},{1,3},{2,0},{3,1},{4,6},{5,7},{6,4},{7,5},{8,10},{9,11},{10,... | collective-permute-start | bytes 884744 | tf_op jit(solution)/shard_map/ppermute | solution.py:25
  3.6 0.5 collective-permute-start.5
  4.1 0.2 shard_map.47.refs_5_
  4.3 4.5 %collective-permute-start.7 = (bf16[784,384]{1,0:T(8,128)(2,1)S(1)}, bf16[784,384]{1,0:T(8,128)(2,1)S(1)}, u32[]{:S(2)}, u32[]{:S(2)}) collective-permute-start(bf16[784,384]{1,0:T(8,128)(2,1)S(1)} %shard_map.47.refs_5_), channel_id=1, source_target_pairs={{4,8},{8,4},{5,9},{9,5},{6,10},{10,6},{7,11},{11,7},{20,24},{24,20... | collective-permute-start | bytes 1806344 | tf_op jit(solution)/shard_map/ppermute | solution.py:34
  8.8 2.2 %collective-permute-done.4.refs_0_ = bf16[384,384]{1,0:T(8,128)(2,1)S(1)} collective-permute-done((bf16[384,384]{1,0:T(8,128)(2,1)S(1)}, bf16[384,384]{1,0:T(8,128)(2,1)S(1)}, u32[]{:S(2)}, u32[]{:S(2)}) %collective-permute-start.4) | collective-permute-done | bytes 294944 | tf_op jit(solution)/shard_map/ppermute | solution.py:25
  11.0 6.8 %collective-permute-done.5.refs_1_ = bf16[384,384]{1,0:T(8,128)(2,1)S(1)} collective-permute-done((bf16[384,384]{1,0:T(8,128)(2,1)S(1)}, bf16[384,384]{1,0:T(8,128)(2,1)S(1)}, u32[]{:S(2)}, u32[]{:S(2)}) %collective-permute-start.5) | collective-permute-done | bytes 294944 | tf_op jit(solution)/shard_map/ppermute | solution.py:25
  18.0 4.5 %collective-permute-start.8 = (bf16[768,384]{1,0:T(8,128)(2,1)S(1)}, bf16[768,384]{1,0:T(8,128)(2,1)S(1)}, u32[]{:S(2)}, u32[]{:S(2)}) collective-permute-start(bf16[768,384]{1,0:T(8,128)(2,1)S(1)} %shard_map.48.refs_4_), channel_id=1, source_target_pairs={{4,8},{8,4},{5,9},{9,5},{6,10},{10,6},{7,11},{11,7},{20,24},{24,20... | collective-permute-start | bytes 1769480 | tf_op jit(solution)/shard_map/ppermute | solution.py:34
  22.5 1.3 %collective-permute-start.1 = (bf16[192,384]{1,0:T(8,128)(2,1)S(1)}, bf16[192,384]{1,0:T(8,128)(2,1)S(1)}, u32[]{:S(2)}, u32[]{:S(2)}) collective-permute-start(bf16[192,384]{1,0:T(8,128)(2,1)S(1)} %get-tuple-element.36), channel_id=1, source_target_pairs={{0,2},{1,3},{2,0},{3,1},{4,6},{5,7},{6,4},{7,5},{8,10},{9,11},{10,... | collective-permute-start | bytes 442376 | tf_op jit(solution)/shard_map/ppermute | solution.py:25
  23.7 3.7 %collective-permute-done.1.refs_2_ = bf16[192,384]{1,0:T(8,128)(2,1)S(1)} collective-permute-done((bf16[192,384]{1,0:T(8,128)(2,1)S(1)}, bf16[192,384]{1,0:T(8,128)(2,1)S(1)}, u32[]{:S(2)}, u32[]{:S(2)}) %collective-permute-start.1) | collective-permute-done | bytes 147488 | tf_op jit(solution)/shard_map/ppermute | solution.py:25
  27.4 2.4 %collective-permute-start.2 = (bf16[192,384]{1,0:T(8,128)(2,1)S(1)}, bf16[192,384]{1,0:T(8,128)(2,1)S(1)}, u32[]{:S(2)}, u32[]{:S(2)}) collective-permute-start(bf16[192,384]{1,0:T(8,128)(2,1)S(1)} %get-tuple-element.37), channel_id=1, source_target_pairs={{0,3},{1,2},{2,1},{3,0},{4,7},{5,6},{6,5},{7,4},{8,11},{9,10},{10,... | collective-permute-start | bytes 442376 | tf_op jit(solution)/shard_map/ppermute | solution.py:25
  29.9 4.6 %collective-permute-done.2.refs_3_ = bf16[192,384]{1,0:T(8,128)(2,1)S(1)} collective-permute-done((bf16[192,384]{1,0:T(8,128)(2,1)S(1)}, bf16[192,384]{1,0:T(8,128)(2,1)S(1)}, u32[]{:S(2)}, u32[]{:S(2)}) %collective-permute-start.2) | collective-permute-done | bytes 147488 | tf_op jit(solution)/shard_map/ppermute | solution.py:25
  34.5 5.0 %shard_map.49 = (f32[2304,128]{1,0:T(8,128)S(1)}, f32[2304,128]{1,0:T(8,128)S(1)}, f32[2304,128]{1,0:T(8,128)S(1)}) custom-call(bf16[192,384]{1,0:T(8,128)(2,1)S(1)} %get-tuple-element.34.refs_0_, bf16[192,384]{1,0:T(8,128)(2,1)S(1)} %slice.4.refs_1_, bf16[192,384]{1,0:T(8,128)(2,1)S(1)} %collective-permute-done.1.refs_2_, ...), custom_call_target="tpu_custom_call" | custom-call | flops 1409286144 | tf_op jit(solution)/shard_map/pallas_call | solution.py:206
  39.6 3.1 %shard_map.50 = (bf16[192,256]{1,0:T(8,128)(2,1)S(1)}, bf16[192,256]{1,0:T(8,128)(2,1)S(1)}, bf16[192,256]{1,0:T(8,128)(2,1)S(1)}, bf16[192,256]{1,0:T(8,128)(2,1)S(1)}) custom-call(bf16[192,384]{1,0:T(8,128)(2,1)S(1)} %get-tuple-element.34.refs_0_, bf16[192,384]{1,0:T(8,128)(2,1)S(1)} %slice.4.refs_1_, bf16[192,384]{1,0:T(8,128)(2,1)S(1)} %collective-permute-done.1.refs_2_, ...), custom_call_target="tpu_custom_call" | custom-call | flops 469762048 | tf_op jit(solution)/shard_map/pallas_call | solution.py:206
  42.7 1.6 %shard_map.51 = (bf16[192,128]{1,0:T(8,128)(2,1)S(1)}, bf16[192,128]{1,0:T(8,128)(2,1)S(1)}, bf16[192,128]{1,0:T(8,128)(2,1)S(1)}, bf16[192,128]{1,0:T(8,128)(2,1)S(1)}) custom-call(bf16[192,384]{1,0:T(8,128)(2,1)S(1)} %get-tuple-element.34.refs_0_, bf16[192,384]{1,0:T(8,128)(2,1)S(1)} %slice.4.refs_1_, bf16[192,384]{1,0:T(8,128)(2,1)S(1)} %collective-permute-done.1.refs_2_, ...), custom_call_target="tpu_custom_call" | custom-call | tf_op jit(solution)/shard_map/pallas_call | solution.py:206
  44.3 0.4 collective-permute-start.12
  44.7 0.6 %collective-permute-start.10 = (bf16[192,256]{1,0:T(8,128)(2,1)S(1)}, bf16[192,256]{1,0:T(8,128)(2,1)S(1)}, u32[]{:S(2)}, u32[]{:S(2)}) collective-permute-start(bf16[192,256]{1,0:T(8,128)(2,1)S(1)} %get-tuple-element.50), channel_id=1, source_target_pairs={{0,2},{1,3},{2,0},{3,1},{4,6},{5,7},{6,4},{7,5},{8,10},{9,11},{10,... | collective-permute-start | bytes 294920 | tf_op jit(solution)/shard_map/ppermute | solution.py:25
  45.4 1.2 %collective-permute-start.11 = (bf16[192,256]{1,0:T(8,128)(2,1)S(1)}, bf16[192,256]{1,0:T(8,128)(2,1)S(1)}, u32[]{:S(2)}, u32[]{:S(2)}) collective-permute-start(bf16[192,256]{1,0:T(8,128)(2,1)S(1)} %get-tuple-element.51), channel_id=1, source_target_pairs={{0,3},{1,2},{2,1},{3,0},{4,7},{5,6},{6,5},{7,4},{8,11},{9,10},{10,... | collective-permute-start | bytes 294920 | tf_op jit(solution)/shard_map/ppermute | solution.py:25
  46.6 0.6 %collective-permute-start.13 = (bf16[192,128]{1,0:T(8,128)(2,1)S(1)}, bf16[192,128]{1,0:T(8,128)(2,1)S(1)}, u32[]{:S(2)}, u32[]{:S(2)}) collective-permute-start(bf16[192,128]{1,0:T(8,128)(2,1)S(1)} %get-tuple-element.61), channel_id=1, source_target_pairs={{0,2},{1,3},{2,0},{3,1},{4,6},{5,7},{6,4},{7,5},{8,10},{9,11},{10,... | collective-permute-start | bytes 147464 | tf_op jit(solution)/shard_map/ppermute | solution.py:25
  47.2 1.5 %collective-permute-start.14 = (bf16[192,128]{1,0:T(8,128)(2,1)S(1)}, bf16[192,128]{1,0:T(8,128)(2,1)S(1)}, u32[]{:S(2)}, u32[]{:S(2)}) collective-permute-start(bf16[192,128]{1,0:T(8,128)(2,1)S(1)} %get-tuple-element.62), channel_id=1, source_target_pairs={{0,3},{1,2},{2,1},{3,0},{4,7},{5,6},{6,5},{7,4},{8,11},{9,10},{10,... | collective-permute-start | bytes 147464 | tf_op jit(solution)/shard_map/ppermute | solution.py:25
  48.7 3.2 %collective-permute-done.13.rest_6_ = bf16[192,128]{1,0:T(8,128)(2,1)S(1)} collective-permute-done((bf16[192,128]{1,0:T(8,128)(2,1)S(1)}, bf16[192,128]{1,0:T(8,128)(2,1)S(1)}, u32[]{:S(2)}, u32[]{:S(2)}) %collective-permute-start.13) | collective-permute-done | bytes 49184 | tf_op jit(solution)/shard_map/ppermute | solution.py:25
  51.9 1.6 %collective-permute-done.14.rest_7_ = bf16[192,128]{1,0:T(8,128)(2,1)S(1)} collective-permute-done((bf16[192,128]{1,0:T(8,128)(2,1)S(1)}, bf16[192,128]{1,0:T(8,128)(2,1)S(1)}, u32[]{:S(2)}, u32[]{:S(2)}) %collective-permute-start.14) | collective-permute-done | bytes 49184 | tf_op jit(solution)/shard_map/ppermute | solution.py:25
  53.5 0.9 %shard_map.52 = bf16[192,1536]{1,0:T(8,128)(2,1)} custom-call(s32[1]{0:T(128)} %bitcast.me_ref, bf16[192,256]{1,0:T(8,128)(2,1)S(1)} %get-tuple-element.48.rest_0_, bf16[192,256]{1,0:T(8,128)(2,1)S(1)} %collective-permute-done.9.rest_1_, bf16[192,256]{1,0:T(8,128)(2,1)S(1)} %collective-permute-done.10.rest_2_, ...), custom_call_target="tpu_custom_call" | custom-call | tf_op jit(solution)/shard_map/pallas_call | solution.py:245
  (14 shorter events, 0.4 us)
Async XLA Ops:
  1.6 2.5 %collective-permute-start = (bf16[576,384]{1,0:T(8,128)(2,1)S(1)}, bf16[576,384]{1,0:T(8,128)(2,1)S(1)}, u32[]{:S(2)}, u32[]{:S(2)}) collective-permute-start(bf16[576,384]{1,0:T(8,128)(2,1)S(1)} %get-tuple-element.35), channel_id=1, source_target_pairs={{0,1},{1,0},{2,3},{3,2},{4,5},{5,4},{6,7},{7,6},{8,9},{9,8},{10,11... | collective-permute-start | bytes 1327112 | tf_op jit(solution)/shard_map/ppermute | solution.py:25
  2.4 8.6 %collective-permute-start.4 = (bf16[384,384]{1,0:T(8,128)(2,1)S(1)}, bf16[384,384]{1,0:T(8,128)(2,1)S(1)}, u32[]{:S(2)}, u32[]{:S(2)}) collective-permute-start(bf16[384,384]{1,0:T(8,128)(2,1)S(1)} %get-tuple-element.39), channel_id=1, source_target_pairs={{0,2},{1,3},{2,0},{3,1},{4,6},{5,7},{6,4},{7,5},{8,10},{9,11},{10,... | collective-permute-start | bytes 884744 | tf_op jit(solution)/shard_map/ppermute | solution.py:25
  3.6 14.1 %collective-permute-start.5 = (bf16[384,384]{1,0:T(8,128)(2,1)S(1)}, bf16[384,384]{1,0:T(8,128)(2,1)S(1)}, u32[]{:S(2)}, u32[]{:S(2)}) collective-permute-start(bf16[384,384]{1,0:T(8,128)(2,1)S(1)} %get-tuple-element.40), channel_id=1, source_target_pairs={{0,3},{1,2},{2,1},{3,0},{4,7},{5,6},{6,5},{7,4},{8,11},{9,10},{10,... | collective-permute-start | bytes 884744 | tf_op jit(solution)/shard_map/ppermute | solution.py:25
  4.3 30.3 %collective-permute-start.3 = (bf16[784,384]{1,0:T(8,128)(2,1)S(1)}, bf16[784,384]{1,0:T(8,128)(2,1)S(1)}, u32[]{:S(2)}, u32[]{:S(2)}) collective-permute-start(bf16[784,384]{1,0:T(8,128)(2,1)S(1)} %shard_map.47.refs_5_), channel_id=1, source_target_pairs={{0,4},{4,0},{8,12},{12,8},{1,5},{5,1},{9,13},{13,9},{2,6},{6,2},{1... | collective-permute-start | bytes 1806344 | tf_op jit(solution)/shard_map/ppermute | solution.py:34
  4.3 30.2 %collective-permute-start.7 = (bf16[784,384]{1,0:T(8,128)(2,1)S(1)}, bf16[784,384]{1,0:T(8,128)(2,1)S(1)}, u32[]{:S(2)}, u32[]{:S(2)}) collective-permute-start(bf16[784,384]{1,0:T(8,128)(2,1)S(1)} %shard_map.47.refs_5_), channel_id=1, source_target_pairs={{4,8},{8,4},{5,9},{9,5},{6,10},{10,6},{7,11},{11,7},{20,24},{24,20... | collective-permute-start | bytes 1806344 | tf_op jit(solution)/shard_map/ppermute | solution.py:34
  17.9 21.7 %collective-permute-start.6 = (bf16[768,384]{1,0:T(8,128)(2,1)S(1)}, bf16[768,384]{1,0:T(8,128)(2,1)S(1)}, u32[]{:S(2)}, u32[]{:S(2)}) collective-permute-start(bf16[768,384]{1,0:T(8,128)(2,1)S(1)} %shard_map.48.refs_4_), channel_id=1, source_target_pairs={{0,4},{4,0},{8,12},{12,8},{1,5},{5,1},{9,13},{13,9},{2,6},{6,2},{1... | collective-permute-start | bytes 1769480 | tf_op jit(solution)/shard_map/ppermute | solution.py:34
  18.0 21.6 %collective-permute-start.8 = (bf16[768,384]{1,0:T(8,128)(2,1)S(1)}, bf16[768,384]{1,0:T(8,128)(2,1)S(1)}, u32[]{:S(2)}, u32[]{:S(2)}) collective-permute-start(bf16[768,384]{1,0:T(8,128)(2,1)S(1)} %shard_map.48.refs_4_), channel_id=1, source_target_pairs={{4,8},{8,4},{5,9},{9,5},{6,10},{10,6},{7,11},{11,7},{20,24},{24,20... | collective-permute-start | bytes 1769480 | tf_op jit(solution)/shard_map/ppermute | solution.py:34
  22.5 5.0 %collective-permute-start.1 = (bf16[192,384]{1,0:T(8,128)(2,1)S(1)}, bf16[192,384]{1,0:T(8,128)(2,1)S(1)}, u32[]{:S(2)}, u32[]{:S(2)}) collective-permute-start(bf16[192,384]{1,0:T(8,128)(2,1)S(1)} %get-tuple-element.36), channel_id=1, source_target_pairs={{0,2},{1,3},{2,0},{3,1},{4,6},{5,7},{6,4},{7,5},{8,10},{9,11},{10,... | collective-permute-start | bytes 442376 | tf_op jit(solution)/shard_map/ppermute | solution.py:25
  27.4 7.1 %collective-permute-start.2 = (bf16[192,384]{1,0:T(8,128)(2,1)S(1)}, bf16[192,384]{1,0:T(8,128)(2,1)S(1)}, u32[]{:S(2)}, u32[]{:S(2)}) collective-permute-start(bf16[192,384]{1,0:T(8,128)(2,1)S(1)} %get-tuple-element.37), channel_id=1, source_target_pairs={{0,3},{1,2},{2,1},{3,0},{4,7},{5,6},{6,5},{7,4},{8,11},{9,10},{10,... | collective-permute-start | bytes 442376 | tf_op jit(solution)/shard_map/ppermute | solution.py:25
  44.3 2.9 %collective-permute-start.12 = (bf16[192,128]{1,0:T(8,128)(2,1)S(1)}, bf16[192,128]{1,0:T(8,128)(2,1)S(1)}, u32[]{:S(2)}, u32[]{:S(2)}) collective-permute-start(bf16[192,128]{1,0:T(8,128)(2,1)S(1)} %get-tuple-element.60), channel_id=1, source_target_pairs={{0,1},{1,0},{2,3},{3,2},{4,5},{5,4},{6,7},{7,6},{8,9},{9,8},{10,11... | collective-permute-start | bytes 147464 | tf_op jit(solution)/shard_map/ppermute | solution.py:25
  44.7 8.7 %collective-permute-start.10 = (bf16[192,256]{1,0:T(8,128)(2,1)S(1)}, bf16[192,256]{1,0:T(8,128)(2,1)S(1)}, u32[]{:S(2)}, u32[]{:S(2)}) collective-permute-start(bf16[192,256]{1,0:T(8,128)(2,1)S(1)} %get-tuple-element.50), channel_id=1, source_target_pairs={{0,2},{1,3},{2,0},{3,1},{4,6},{5,7},{6,4},{7,5},{8,10},{9,11},{10,... | collective-permute-start | bytes 294920 | tf_op jit(solution)/shard_map/ppermute | solution.py:25
  45.4 8.1 %collective-permute-start.11 = (bf16[192,256]{1,0:T(8,128)(2,1)S(1)}, bf16[192,256]{1,0:T(8,128)(2,1)S(1)}, u32[]{:S(2)}, u32[]{:S(2)}) collective-permute-start(bf16[192,256]{1,0:T(8,128)(2,1)S(1)} %get-tuple-element.51), channel_id=1, source_target_pairs={{0,3},{1,2},{2,1},{3,0},{4,7},{5,6},{6,5},{7,4},{8,11},{9,10},{10,... | collective-permute-start | bytes 294920 | tf_op jit(solution)/shard_map/ppermute | solution.py:25
  46.5 7.0 %collective-permute-start.9 = (bf16[192,256]{1,0:T(8,128)(2,1)S(1)}, bf16[192,256]{1,0:T(8,128)(2,1)S(1)}, u32[]{:S(2)}, u32[]{:S(2)}) collective-permute-start(bf16[192,256]{1,0:T(8,128)(2,1)S(1)} %get-tuple-element.49), channel_id=1, source_target_pairs={{0,1},{1,0},{2,3},{3,2},{4,5},{5,4},{6,7},{7,6},{8,9},{9,8},{10,11... | collective-permute-start | bytes 294920 | tf_op jit(solution)/shard_map/ppermute | solution.py:25
  46.6 5.3 %collective-permute-start.13 = (bf16[192,128]{1,0:T(8,128)(2,1)S(1)}, bf16[192,128]{1,0:T(8,128)(2,1)S(1)}, u32[]{:S(2)}, u32[]{:S(2)}) collective-permute-start(bf16[192,128]{1,0:T(8,128)(2,1)S(1)} %get-tuple-element.61), channel_id=1, source_target_pairs={{0,2},{1,3},{2,0},{3,1},{4,6},{5,7},{6,4},{7,5},{8,10},{9,11},{10,... | collective-permute-start | bytes 147464 | tf_op jit(solution)/shard_map/ppermute | solution.py:25
  47.2 6.3 %collective-permute-start.14 = (bf16[192,128]{1,0:T(8,128)(2,1)S(1)}, bf16[192,128]{1,0:T(8,128)(2,1)S(1)}, u32[]{:S(2)}, u32[]{:S(2)}) collective-permute-start(bf16[192,128]{1,0:T(8,128)(2,1)S(1)} %get-tuple-element.62), channel_id=1, source_target_pairs={{0,3},{1,2},{2,1},{3,0},{4,7},{5,6},{6,5},{7,4},{8,11},{9,10},{10,... | collective-permute-start | bytes 147464 | tf_op jit(solution)/shard_map/ppermute | solution.py:25

commit v3 on v2

v3 whole, which is shorter than its diff:
```python
import functools
import math

import jax
import jax.numpy as jnp
from jax import lax
from jax.experimental import pallas as pl
from jax.experimental.pallas import tpu as pltpu
from jax.sharding import PartitionSpec as P

HEAD_DIM = 128
TILE_H = 8
TILE_W = 8
TIME_TILES = 4
COUNT_ROWS = 16
MASKED = -1e30
LARGEST_TOTAL = 2.0**100
SCALE = math.log2(math.e) / math.sqrt(HEAD_DIM)
VMEM_LIMIT = 24 * 2**20
WHOLE = False


def in_vmem(count):
    return [pl.BlockSpec(memory_space=pltpu.VMEM)] * count


def swap_head(block, bit, devices):
    return lax.ppermute(block, "head", [(i, i ^ bit) for i in range(devices)])


def swap_pairs(block, phase, stride, length, devices):
    route = []
    for i in range(devices):
        place = i // stride % length
        if place % 2 == phase and place + 1 < length:
            route += [(i, i + stride), (i + stride, i)]
    return lax.ppermute(block, "tok", route)


def pack_body(devices, part, counts_in, me_ref, q_ref, k_ref, v_ref, *rest):
    own_ref, sibling_ref, own_q_ref = rest[:3]
    far_refs, far_q_refs = rest[3 : 1 + devices], rest[1 + devices : -3]
    counts_ref, count_sem, sems = rest[-3:]
    rows = k_ref.shape[0]
    me = me_ref[0]

    def lanes(bit):
        return pl.ds(pl.multiple_of((me ^ bit) * part, HEAD_DIM), part)

    count_copy = pltpu.make_async_copy(counts_in, counts_ref, count_sem)
    count_copy.start()
    jobs = []
    targets = [(1, sibling_ref, 0)]
    targets += [(bit, far_refs[bit - 2], 0) for bit in range(2, devices)]
    for bit, ref, base in [*targets, (0, own_ref, 0)]:
        jobs += [
            (k_ref.at[:, lanes(bit)], ref.at[pl.ds(base, rows)]),
            (v_ref.at[:, lanes(bit)], ref.at[pl.ds(base + rows, rows)]),
        ]
    jobs += [
        (q_ref.at[:, lanes(1)], sibling_ref.at[pl.ds(2 * rows, rows)]),
        (q_ref.at[:, lanes(0)], own_q_ref),
    ]
    jobs += [
        (q_ref.at[:, lanes(bit)], far_q_refs[bit // 2 - 1].at[pl.ds(bit % 2 * rows, rows)])
        for bit in range(2, devices)
    ]
    copies = [pltpu.make_async_copy(src, dst, sems.at[i]) for i, (src, dst) in enumerate(jobs)]
    for copy in copies:
        copy.start()
    count_copy.wait()
    shape = (COUNT_ROWS, part)
    row = lax.broadcasted_iota(jnp.int32, shape, 0)
    filled = jnp.zeros(shape, jnp.float32)
    for tile in range(counts_ref.shape[0]):
        filled = jnp.where(row == tile, counts_ref[tile].astype(jnp.float32), filled)
    own_ref[pl.ds(2 * rows, COUNT_ROWS), :] = filled.astype(jnp.bfloat16)
    for copy in copies:
        copy.wait()


def pack(me, counts, query, key, value, devices):
    rows, width = query.shape
    part = width // devices
    far = devices - 2
    sizes = [2 * rows + COUNT_ROWS, 3 * rows, rows] + [2 * rows] * far + [2 * rows] * (far // 2)
    fields = [pltpu.with_memory_space_constraint(f, pltpu.HBM) for f in (query, key, value)]
    results = pl.pallas_call(
        functools.partial(pack_body, devices, part),
        out_shape=[pltpu.VMEM((size, part), jnp.bfloat16) for size in sizes],
        in_specs=[pl.BlockSpec(memory_space=pltpu.HBM), pl.BlockSpec(memory_space=pltpu.SMEM)]
        + [pl.BlockSpec(memory_space=pltpu.HBM)] * 3,
        out_specs=in_vmem(len(sizes)),
        scratch_shapes=[
            pltpu.SMEM(counts.shape, jnp.int32),
            pltpu.SemaphoreType.DMA,
            pltpu.SemaphoreType.DMA((3 * devices,)),
        ],
        compiler_params=pltpu.CompilerParams(vmem_limit_bytes=VMEM_LIMIT),
        cost_estimate=pl.CostEstimate(flops=0, bytes_accessed=12 * query.size, transcendentals=0),
    )(pltpu.with_memory_space_constraint(counts, pltpu.HBM), me, *fields)
    return results[0], results[1], results[2], results[3 : 3 + far], results[3 + far :]


def stack_body(jobs, *refs):
    blocks, out_ref, sems = refs[:-2], refs[-2], refs[-1]
    copies, base = [], 0
    for i, (size, lanes) in enumerate(jobs):
        source = blocks[i].at[pl.ds(0, size), lanes]
        copies.append(
            pltpu.make_async_copy(source, out_ref.at[pl.ds(base, size)], sems.at[i])
        )
        base += size
    for copy in copies:
        copy.start()
    for copy in copies:
        copy.wait()


def stack(blocks, sizes, start, width):
    jobs = [(size, pl.ds(start, width)) for size in sizes]
    return pl.pallas_call(
        functools.partial(stack_body, jobs),
        out_shape=pltpu.VMEM((sum(sizes), width), jnp.bfloat16),
        in_specs=in_vmem(len(blocks)),
        out_specs=pl.BlockSpec(memory_space=pltpu.VMEM),
        scratch_shapes=[pltpu.SemaphoreType.DMA((len(blocks),))],
        compiler_params=pltpu.CompilerParams(vmem_limit_bytes=VMEM_LIMIT),
        cost_estimate=pl.CostEstimate(
            flops=0, bytes_accessed=sum(sizes) * width, transcendentals=0
        ),
    )(*blocks)


def features(head):
    start = head * HEAD_DIM
    return pl.ds(start if isinstance(head, int) else pl.multiple_of(start, HEAD_DIM), HEAD_DIM)


def window_of(tile, tiles, groups):
    near = range(max(tile - 1, 0), min(tile + 2, tiles))
    return [(group, other) for other in near for group in range(len(groups))]


def gather(arrays, groups, window, start, tokens, lanes):
    return jnp.concatenate(
        [
            arrays[i][pl.ds(base + start + other * tokens, tokens), lanes]
            for group, other in window
            for i, base in groups[group][1]
        ],
        0,
    )


def counts_of(arrays, groups, rows):
    counts = [arrays[i][pl.ds(2 * rows, COUNT_ROWS), pl.ds(0, HEAD_DIM)] for i, _ in groups]
    return [count.astype(jnp.float32) for count in counts]


def bias_of(counts, groups, window, tokens):
    lane = lax.broadcasted_iota(jnp.int32, (1, HEAD_DIM), 1)
    row = (lane // TILE_W % TILE_H).astype(jnp.float32)
    parts = []
    for group, other in window:
        part = jnp.where(row < counts[group][other : other + 1], 0.0, MASKED)
        parts += [part] * (len(groups[group][1]) * tokens // HEAD_DIM)
    return jnp.concatenate(parts, 1)


def products(queries, keys):
    return lax.dot_general(
        queries, keys, (((1,), (1,)), ((), ())), preferred_element_type=jnp.float32
    )


def early_body(groups, operands, frames, tiles, tokens, heads, *refs):
    rows = tiles * tokens
    queries, arrays = refs[:frames], refs[frames : frames + operands]
    max_ref, total_ref, sum_ref = refs[frames + operands :]
    counts = counts_of(arrays, groups, rows)
    windows = [window_of(tile, tiles, groups) for tile in range(tiles)]
    biases = [bias_of(counts, groups, window, tokens) for window in windows]
    block = frames * tokens

    def scored(head, tile):
        lanes = features(head)
        asked = jnp.concatenate([ref[pl.ds(tile * tokens, tokens), lanes] for ref in queries], 0)
        scores = products(asked, gather(arrays, groups, windows[tile], 0, tokens, lanes))
        scores = scores + biases[tile]
        return scores, jnp.max(scores, axis=1, keepdims=True)

    steps = [(head, tile) for head in range(heads) for tile in range(tiles)]
    ahead = scored(*steps[0])
    for i, (head, tile) in enumerate(steps):
        scores, largest = ahead
        if i + 1 < len(steps):
            ahead = scored(*steps[i + 1])
        weight = jnp.exp2((scores - largest) * SCALE).astype(jnp.bfloat16)
        values = gather(arrays, groups, windows[tile], rows, tokens, features(head))
        values = jnp.concatenate([values, jnp.ones_like(values)], 1)
        summed = jnp.dot(weight, values, preferred_element_type=jnp.float32)
        place = pl.ds((head * tiles + tile) * block, block)
        max_ref[place, :] = jnp.broadcast_to(largest, (block, HEAD_DIM))
        sum_ref[place, :] = summed[:, :HEAD_DIM]
        total_ref[place, :] = summed[:, HEAD_DIM:]


def late_body(groups, operands, frames, tiles, tokens, heads, first, lane, *refs):
    rows = tiles * tokens
    queries, arrays = refs[:frames], refs[frames : frames + operands]
    max_ref, total_ref, sum_ref = refs[frames + operands : frames + operands + 3]
    outs = refs[frames + operands + 3 :]
    counts = counts_of(arrays, groups, rows)
    windows = [window_of(tile, tiles, groups) for tile in range(tiles)]
    block = frames * tokens

    def asked(head, tile):
        return jnp.concatenate(
            [ref[pl.ds(tile * tokens, tokens), features(first + head)] for ref in queries], 0
        )

    def place(head, tile):
        start = ((first + head) * tiles + tile) * block
        return pl.ds(start if isinstance(start, int) else pl.multiple_of(start, block), block)

    def write(head, tile, result):
        for frame in range(frames):
            outs[frame][pl.ds(tile * tokens, tokens), features(head)] = result[
                frame * tokens : (frame + 1) * tokens
            ]

    token = lax.broadcasted_iota(jnp.int32, (tokens, HEAD_DIM), 0)
    row = (token // TILE_W % TILE_H).astype(jnp.float32)
    real = [
        [jnp.where(row < count[n : n + 1], 1.0, 0.0).astype(jnp.bfloat16) for n in range(tiles)]
        for count in counts
    ]
    worst = jnp.zeros((block, HEAD_DIM), jnp.float32)
    for head in range(heads):
        lanes = features(lane + head)
        for tile, window in enumerate(windows):
            at = place(head, tile)
            scores = products(
                asked(head, tile), gather(arrays, groups, window, 0, tokens, lanes)
            )
            before = jnp.concatenate([max_ref[at, :]] * (scores.shape[1] // HEAD_DIM), 1)
            weight = jnp.exp2((scores - before) * SCALE).astype(jnp.bfloat16)
            kept = jnp.concatenate(
                [real[group][n] for group, n in window for _ in groups[group][1]], 0
            )
            values = gather(arrays, groups, window, rows, tokens, lanes) * kept
            summed = jnp.dot(
                weight,
                jnp.concatenate([values, kept], 1),
                preferred_element_type=jnp.float32,
            )
            total = total_ref[at, :] + summed[:, HEAD_DIM:]
            worst = jnp.where(total < LARGEST_TOTAL, worst, 1.0)
            result = (sum_ref[at, :] + summed[:, :HEAD_DIM]) / total
            write(head, tile, result.astype(jnp.bfloat16))

    @pl.when(jnp.max(worst) > 0.0)
    def _():
        def one_head(head, _):
            lanes = features(lane + head)
            for tile, window in enumerate(windows):
                at = place(head, tile)
                scores = products(
                    asked(head, tile), gather(arrays, groups, window, 0, tokens, lanes)
                )
                scores = scores + bias_of(counts, groups, window, tokens)
                before = max_ref[at, :]
                largest = jnp.maximum(before[:, :1], jnp.max(scores, axis=1, keepdims=True))
                shrink = jnp.exp2((before - largest) * SCALE)
                weight = jnp.exp2((scores - largest) * SCALE)
                total = jnp.sum(weight, axis=1, keepdims=True) + total_ref[at, :] * shrink
                summed = jnp.dot(
                    weight.astype(jnp.bfloat16),
                    gather(arrays, groups, window, rows, tokens, lanes),
                    preferred_element_type=jnp.float32,
                )
                result = (summed + sum_ref[at, :] * shrink) / total
                write(head, tile, result.astype(jnp.bfloat16))
            return 0

        lax.fori_loop(0, heads, one_head, 0)


def attend(queries, arrays, groups, tiles, tokens, heads, first=0, base=0, state=(), weigh=1):
    frames = len(queries)
    operands = [*queries, *arrays, *state]
    size = sum(len(fields) for _, fields in groups)
    pairs = heads * (3 * tiles - 2) * size * tokens * frames * tokens
    shape = (groups, len(arrays), frames, tiles, tokens, heads)
    if state:
        outs = [pltpu.VMEM((tiles * tokens, heads * HEAD_DIM), jnp.bfloat16)] * frames
        kernel = functools.partial(late_body, *shape, first, base)
    else:
        outs = [pltpu.VMEM((heads * tiles * frames * tokens, HEAD_DIM), jnp.float32)] * 3
        kernel = functools.partial(early_body, *shape)
    return pl.pallas_call(
        kernel,
        out_shape=outs,
        in_specs=in_vmem(len(operands)),
        out_specs=in_vmem(len(outs)),
        compiler_params=pltpu.CompilerParams(vmem_limit_bytes=VMEM_LIMIT),
        cost_estimate=pl.CostEstimate(
            flops=weigh * 4 * HEAD_DIM * pairs, bytes_accessed=0, transcendentals=weigh * pairs
        ),
    )(*operands)


def join_body(jobs, part, me_ref, *rest):
    out_ref, sems = rest[-2:]
    me = me_ref[0]
    copies = []
    for i, (bit, base) in enumerate(jobs):
        lanes = pl.ds(pl.multiple_of((me ^ bit) * part + base, HEAD_DIM), rest[i].shape[1])
        copies.append(pltpu.make_async_copy(rest[i], out_ref.at[:, lanes], sems.at[i]))
    for copy in copies:
        copy.start()
    for copy in copies:
        copy.wait()


def join(me, pieces, rows, part, devices):
    jobs = [piece[:2] for piece in pieces]
    return pl.pallas_call(
        functools.partial(join_body, jobs, part),
        out_shape=jax.ShapeDtypeStruct((rows, devices * part), jnp.bfloat16),
        in_specs=[pl.BlockSpec(memory_space=pltpu.SMEM)] + in_vmem(len(pieces)),
        out_specs=pl.BlockSpec(memory_space=pl.ANY),
        scratch_shapes=[pltpu.SemaphoreType.DMA((len(pieces),))],
        compiler_params=pltpu.CompilerParams(vmem_limit_bytes=VMEM_LIMIT),
    )(me, *(piece[2] for piece in pieces))


def body(query, key, value, valid_rows):
    devices = lax.axis_size("head")
    columns = lax.axis_size("tok")
    height = columns // TIME_TILES
    tiles, tokens, width = query.shape
    heads = width // HEAD_DIM // devices
    me = lax.axis_index("head").astype(jnp.int32).reshape(1)
    flat = [field.reshape(tiles * tokens, width) for field in (query, key, value)]
    own, sibling, own_query, far, far_query = pack(me, valid_rows, *flat, devices)
    rows = tiles * tokens

    part = heads * HEAD_DIM

    def by_height(block):
        if height == 1:
            return [block]
        return [block] + [swap_pairs(block, phase, 1, height, columns) for phase in (0, 1)]

    def by_time(blocks):
        return [
            swap_pairs(b, phase, height, TIME_TILES, columns) for phase in (0, 1) for b in blocks
        ]

    sibling = swap_head(sibling, 1, devices)
    far = [swap_head(b, bit, devices) for bit, b in enumerate(far, 2)]
    far_query = [swap_head(b, 2 * i + 2, devices) for i, b in enumerate(far_query)]
    near = by_height(stack([own, sibling], [own.shape[0], 2 * rows], 0, part))
    near = near + by_time(near)

    queries = [own_query, sibling[2 * rows :]]
    for block in far_query:
        queries += [block[:rows], swap_head(block[rows:], 1, devices)]

    cut = heads - heads // 3
    parts = [(0, heads)] if WHOLE else [(0, cut), (cut, heads - cut)]
    across = []
    for first, count in parts:
        block = stack(far, [2 * rows] * len(far), first * HEAD_DIM, count * HEAD_DIM)
        if first:
            block, *near = lax.optimization_barrier((block, *near))
        block = by_height(block)
        across.append(block[1:] + by_time(block))
    parts = [(0, cut), (cut, heads - cut)]

    near_rows = [0, own.shape[0]]
    far_rows = [2 * rows * i for i in range(devices - 2)]
    arrays = near + far
    groups = [(i, [(i, base) for base in near_rows]) for i in range(len(near))]
    groups[0][1].extend((len(near) + i, 0) for i in range(len(far)))
    state = attend(queries, arrays, groups, tiles, tokens, heads)

    pieces = []
    for i, (first, count) in enumerate(parts):
        others = across[min(i, len(across) - 1)]
        groups = [
            (i, [(len(others) + i, base) for base in far_rows]) for i in range(len(others))
        ]
        base = first if WHOLE else 0
        results = attend(
            queries, near[1:] + others, groups, tiles, tokens, count, first, base, state
        )
        results = list(results)
        results[1] = swap_head(results[1], 1, devices)
        if i == 0:
            *state, results[1] = lax.optimization_barrier((*state, results[1]))
        pieces += [
            (bit, first * HEAD_DIM, swap_head(b, bit, devices) if bit > 1 else b)
            for bit, b in enumerate(results)
        ]
    return join(me, pieces, rows, part, devices).reshape(tiles, tokens, width)


def solution(mesh):
    placed = (
        P(("clips", "tok"), "head", None),
        P(("clips", "tok"), "head", None),
        P(("clips", "tok"), "head", None),
        P(("clips", "tok")),
    )
    return jax.shard_map(
        body,
        mesh=mesh,
        in_specs=placed,
        out_specs=P(("clips", "tok"), "head", None),
        check_vma=False,
    )
```

time: 54.5 us -> 45.2 us (0.83)
  waiting for transfers between devices: 22.1 us -> 12.9 us
  Pallas kernels: 12.5 us -> 9.1 us
  starting transfers between devices: 19.6 us -> 22.8 us
    ppermute x11, waiting for transfers between devices: 22.1 us -> 12.9 us  [swap_head(): return lax.ppermute(block, 'head', [(i, i ^ bit) for i in range(devices)])]
    ppermute x4 -> x6, starting transfers between devices: 9.09 us -> 13.6 us  [swap_pairs(): return lax.ppermute(block, 'tok', route)]
    pallas_call x6 -> x7, Pallas kernels: 10.9 us -> 7.46 us  [the longest x3 6.34 us: attend(): pl.pallas_call(kernel, out_shape=outs, in_specs=in_vmem(len(operands)), o...]
    ppermute x11, starting transfers between devices: 10.5 us -> 9.13 us  [swap_head(): return lax.ppermute(block, 'head', [(i, i ^ bit) for i in range(devices)])]
  transfers between devices with their start and end apart: 15 -> 17, of which waited for: 6 -> 6; matrix products, arithmetic and copies ran while one was open for 0% -> 0% of each run, Pallas kernels for 10% -> 15%
where the time goes in v3:
time: 45.2 us; the launch traced here: 45 us
  starting transfers between devices  22.8 us (50%)
  waiting for transfers between devices  12.9 us (29%)
  Pallas kernels  9.1 us (20%)
    ppermute x6, starting transfers between devices, swap_pairs(): return lax.ppermute(block, 'tok', route)  13.6 us
    ppermute x11, waiting for transfers between devices, swap_head(): return lax.ppermute(block, 'head', [(i, i ^ bit) for i in range(devices)])  12.9 us
    ppermute x11, starting transfers between devices, swap_head(): return lax.ppermute(block, 'head', [(i, i ^ bit) for i in range(devices)])  9.13 us
    pallas_call x3, Pallas kernels, attend(): pl.pallas_call(kernel, out_shape=outs, in_specs=in_vmem(len(operands)), o...  6.34 us
    pallas_call x1, Pallas kernels, pack(): pl.pallas_call(functools.partial(pack_body, devices, part), out_shape=[pl...  1.64 us
  transfers between devices with their start and end apart: 17, of which 6 were waited for; matrix products, arithmetic and copies ran while one was open for 0% of the time, Pallas kernels for 15%

profile of v3, /device:TPU:9, one launch (start us, length us, event | category | flops | bytes accessed | tf_op | source)
XLA Modules:
  0.0 45.0 jit_solution(10772608530145661098)
XLA Ops:
  0.0 1.6 %shard_map.46 = (bf16[400,384]{1,0:T(8,128)(2,1)S(1)}, bf16[576,384]{1,0:T(8,128)(2,1)S(1)}, bf16[192,384]{1,0:T(8,128)(2,1)S(1)}, bf16[384,384]{1,0:T(8,128)(2,...) custom-call(s32[3]{0:T(128)} %counts_in.1, s32[1]{0:T(128)} %bitcast.me_ref, ...), custom_call_target="tpu_custom_call" | custom-call | bytes 3538944 | tf_op jit(solution)/shard_map/pallas_call | solution.py:88
  1.6 0.7 %collective-permute-start = (bf16[576,384]{1,0:T(8,128)(2,1)S(1)}, bf16[576,384]{1,0:T(8,128)(2,1)S(1)}, u32[]{:S(2)}, u32[]{:S(2)}) collective-permute-start(bf16[576,384]{1,0:T(8,128)(2,1)S(1)} %get-tuple-element.31), channel_id=1, source_target_pairs={{0,1},{1,0},{2,3},{3,2},{4,5},{5,4},{6,7},{7,6},{8,9},{9,8},{10,11... | collective-permute-start | bytes 1327112 | tf_op jit(solution)/shard_map/ppermute | solution.py:28
  2.4 1.2 %collective-permute-start.3 = (bf16[384,384]{1,0:T(8,128)(2,1)S(1)}, bf16[384,384]{1,0:T(8,128)(2,1)S(1)}, u32[]{:S(2)}, u32[]{:S(2)}) collective-permute-start(bf16[384,384]{1,0:T(8,128)(2,1)S(1)} %get-tuple-element.33), channel_id=1, source_target_pairs={{0,2},{1,3},{2,0},{3,1},{4,6},{5,7},{6,4},{7,5},{8,10},{9,11},{10,... | collective-permute-start | bytes 884744 | tf_op jit(solution)/shard_map/ppermute | solution.py:28
  3.6 0.5 %collective-permute-start.4 = (bf16[384,384]{1,0:T(8,128)(2,1)S(1)}, bf16[384,384]{1,0:T(8,128)(2,1)S(1)}, u32[]{:S(2)}, u32[]{:S(2)}) collective-permute-start(bf16[384,384]{1,0:T(8,128)(2,1)S(1)} %get-tuple-element.34), channel_id=1, source_target_pairs={{0,3},{1,2},{2,1},{3,0},{4,7},{5,6},{6,5},{7,4},{8,11},{9,10},{10,... | collective-permute-start | bytes 884744 | tf_op jit(solution)/shard_map/ppermute | solution.py:28
  4.1 1.2 %collective-permute-start.1 = (bf16[384,384]{1,0:T(8,128)(2,1)S(1)}, bf16[384,384]{1,0:T(8,128)(2,1)S(1)}, u32[]{:S(2)}, u32[]{:S(2)}) collective-permute-start(bf16[384,384]{1,0:T(8,128)(2,1)S(1)} %get-tuple-element.32), channel_id=1, source_target_pairs={{0,2},{1,3},{2,0},{3,1},{4,6},{5,7},{6,4},{7,5},{8,10},{9,11},{10,... | collective-permute-start | bytes 884744 | tf_op jit(solution)/shard_map/ppermute | solution.py:28
  5.7 4.3 %collective-permute-start.6 = (bf16[784,384]{1,0:T(8,128)(2,1)S(1)}, bf16[784,384]{1,0:T(8,128)(2,1)S(1)}, u32[]{:S(2)}, u32[]{:S(2)}) collective-permute-start(bf16[784,384]{1,0:T(8,128)(2,1)S(1)} %shard_map.48.refs_4_), channel_id=1, source_target_pairs={{4,8},{8,4},{5,9},{9,5},{6,10},{10,6},{7,11},{11,7},{20,24},{24,20... | collective-permute-start | bytes 1806344 | tf_op jit(solution)/shard_map/ppermute | solution.py:37
  10.0 0.9 %collective-permute-done.3.refs_0_.refs_7_ = bf16[384,384]{1,0:T(8,128)(2,1)S(1)} collective-permute-done((bf16[384,384]{1,0:T(8,128)(2,1)S(1)}, bf16[384,384]{1,0:T(8,128)(2,1)S(1)}, u32[]{:S(2)}, u32[]{:S(2)}) %collective-permute-start.3) | collective-permute-done | bytes 294944 | tf_op jit(solution)/shard_map/ppermute | solution.py:28
  11.0 7.2 %collective-permute-done.4.refs_1_.refs_8_ = bf16[384,384]{1,0:T(8,128)(2,1)S(1)} collective-permute-done((bf16[384,384]{1,0:T(8,128)(2,1)S(1)}, bf16[384,384]{1,0:T(8,128)(2,1)S(1)}, u32[]{:S(2)}, u32[]{:S(2)}) %collective-permute-start.4) | collective-permute-done | bytes 294944 | tf_op jit(solution)/shard_map/ppermute | solution.py:28
  18.3 4.5 %collective-permute-start.8 = (bf16[768,256]{1,0:T(8,128)(2,1)S(1)}, bf16[768,256]{1,0:T(8,128)(2,1)S(1)}, u32[]{:S(2)}, u32[]{:S(2)}) collective-permute-start(bf16[768,256]{1,0:T(8,128)(2,1)S(1)} %shard_map.49), channel_id=1, source_target_pairs={{4,8},{8,4},{5,9},{9,5},{6,10},{10,6},{7,11},{11,7},{20,24},{24,20... | collective-permute-start | bytes 1179656 | tf_op jit(solution)/shard_map/ppermute | solution.py:37
  22.8 0.8 %collective-permute-done.1 = bf16[384,384]{1,0:T(8,128)(2,1)S(1)} collective-permute-done((bf16[384,384]{1,0:T(8,128)(2,1)S(1)}, bf16[384,384]{1,0:T(8,128)(2,1)S(1)}, u32[]{:S(2)}, u32[]{:S(2)}) %collective-permute-start.1) | collective-permute-done | bytes 294944 | tf_op jit(solution)/shard_map/ppermute | solution.py:28
  23.7 0.9 %collective-permute-start.2 = (bf16[192,384]{1,0:T(8,128)(2,1)S(1)}, bf16[192,384]{1,0:T(8,128)(2,1)S(1)}, u32[]{:S(2)}, u32[]{:S(2)}) collective-permute-start(bf16[192,384]{1,0:T(8,128)(2,1)S(1)} %get-tuple-element.55), channel_id=1, source_target_pairs={{0,1},{1,0},{2,3},{3,2},{4,5},{5,4},{6,7},{7,6},{8,9},{9,8},{10,11... | collective-permute-start | bytes 442376 | tf_op jit(solution)/shard_map/ppermute | solution.py:28
  24.8 4.5 %collective-permute-start.13 = (bf16[768,128]{1,0:T(8,128)(2,1)S(1)}, bf16[768,128]{1,0:T(8,128)(2,1)S(1)}, u32[]{:S(2)}, u32[]{:S(2)}) collective-permute-start(bf16[768,128]{1,0:T(8,128)(2,1)S(1)} %shard_map.47), channel_id=1, source_target_pairs={{4,8},{8,4},{5,9},{9,5},{6,10},{10,6},{7,11},{11,7},{20,24},{24,20... | collective-permute-start | bytes 589832 | tf_op jit(solution)/shard_map/ppermute | solution.py:37
  29.3 4.0 %shard_map.50 = (f32[2304,128]{1,0:T(8,128)S(1)}, f32[2304,128]{1,0:T(8,128)S(1)}, f32[2304,128]{1,0:T(8,128)S(1)}) custom-call(bf16[192,384]{1,0:T(8,128)(2,1)S(1)} %get-tuple-element.30.refs_0_, bf16[192,384]{1,0:T(8,128)(2,1)S(1)} %slice.12.refs_1_, bf16[192,384]{1,0:T(8,128)(2,1)S(1)} %get-tuple-element.56.refs_2_, ...), custom_call_target="tpu_custom_call" | custom-call | flops 1409286144 | tf_op jit(solution)/shard_map/pallas_call | solution.py:302
  33.3 1.4 %shard_map.51 = (bf16[192,256]{1,0:T(8,128)(2,1)S(1)}, bf16[192,256]{1,0:T(8,128)(2,1)S(1)}, bf16[192,256]{1,0:T(8,128)(2,1)S(1)}, bf16[192,256]{1,0:T(8,128)(2,1)S(1)}) custom-call(bf16[192,384]{1,0:T(8,128)(2,1)S(1)} %get-tuple-element.30.refs_0_, bf16[192,384]{1,0:T(8,128)(2,1)S(1)} %slice.12.refs_1_, bf16[192,384]{1,0:T(8,128)(2,1)S(1)} %get-tuple-element.56.refs_2_, ...), custom_call_target="tpu_custom_call" | custom-call | flops 469762048 | tf_op jit(solution)/shard_map/pallas_call | solution.py:302
  34.7 0.6 %collective-permute-start.9 = (bf16[192,256]{1,0:T(8,128)(2,1)S(1)}, bf16[192,256]{1,0:T(8,128)(2,1)S(1)}, u32[]{:S(2)}, u32[]{:S(2)}) collective-permute-start(bf16[192,256]{1,0:T(8,128)(2,1)S(1)} %get-tuple-element.43), channel_id=1, source_target_pairs={{0,1},{1,0},{2,3},{3,2},{4,5},{5,4},{6,7},{7,6},{8,9},{9,8},{10,11... | collective-permute-start | bytes 294920 | tf_op jit(solution)/shard_map/ppermute | solution.py:28
  35.4 1.2 %collective-permute-start.10 = (bf16[192,256]{1,0:T(8,128)(2,1)S(1)}, bf16[192,256]{1,0:T(8,128)(2,1)S(1)}, u32[]{:S(2)}, u32[]{:S(2)}) collective-permute-start(bf16[192,256]{1,0:T(8,128)(2,1)S(1)} %get-tuple-element.45), channel_id=1, source_target_pairs={{0,2},{1,3},{2,0},{3,1},{4,6},{5,7},{6,4},{7,5},{8,10},{9,11},{10,... | collective-permute-start | bytes 294920 | tf_op jit(solution)/shard_map/ppermute | solution.py:28
  36.6 0.5 %collective-permute-start.11 = (bf16[192,256]{1,0:T(8,128)(2,1)S(1)}, bf16[192,256]{1,0:T(8,128)(2,1)S(1)}, u32[]{:S(2)}, u32[]{:S(2)}) collective-permute-start(bf16[192,256]{1,0:T(8,128)(2,1)S(1)} %get-tuple-element.46), channel_id=1, source_target_pairs={{0,3},{1,2},{2,1},{3,0},{4,7},{5,6},{6,5},{7,4},{8,11},{9,10},{10,... | collective-permute-start | bytes 294920 | tf_op jit(solution)/shard_map/ppermute | solution.py:28
  37.1 0.9 %shard_map.52 = (bf16[192,128]{1,0:T(8,128)(2,1)S(1)}, bf16[192,128]{1,0:T(8,128)(2,1)S(1)}, bf16[192,128]{1,0:T(8,128)(2,1)S(1)}, bf16[192,128]{1,0:T(8,128)(2,1)S(1)}) custom-call(bf16[192,384]{1,0:T(8,128)(2,1)S(1)} %get-tuple-element.30.refs_0_, bf16[192,384]{1,0:T(8,128)(2,1)S(1)} %slice.12.refs_1_, bf16[192,384]{1,0:T(8,128)(2,1)S(1)} %get-tuple-element.56.refs_2_, ...), custom_call_target="tpu_custom_call" | custom-call | flops 234881024 | tf_op jit(solution)/shard_map/pallas_call | solution.py:302
  38.2 1.2 %collective-permute-start.15 = (bf16[192,128]{1,0:T(8,128)(2,1)S(1)}, bf16[192,128]{1,0:T(8,128)(2,1)S(1)}, u32[]{:S(2)}, u32[]{:S(2)}) collective-permute-start(bf16[192,128]{1,0:T(8,128)(2,1)S(1)} %get-tuple-element.53), channel_id=1, source_target_pairs={{0,2},{1,3},{2,0},{3,1},{4,6},{5,7},{6,4},{7,5},{8,10},{9,11},{10,... | collective-permute-start | bytes 147464 | tf_op jit(solution)/shard_map/ppermute | solution.py:28
  39.4 0.8 %collective-permute-start.16 = (bf16[192,128]{1,0:T(8,128)(2,1)S(1)}, bf16[192,128]{1,0:T(8,128)(2,1)S(1)}, u32[]{:S(2)}, u32[]{:S(2)}) collective-permute-start(bf16[192,128]{1,0:T(8,128)(2,1)S(1)} %get-tuple-element.54), channel_id=1, source_target_pairs={{0,3},{1,2},{2,1},{3,0},{4,7},{5,6},{6,5},{7,4},{8,11},{9,10},{10,... | collective-permute-start | bytes 147464 | tf_op jit(solution)/shard_map/ppermute | solution.py:28
  40.2 2.2 %collective-permute-done.11.rest_3_ = bf16[192,256]{1,0:T(8,128)(2,1)S(1)} collective-permute-done((bf16[192,256]{1,0:T(8,128)(2,1)S(1)}, bf16[192,256]{1,0:T(8,128)(2,1)S(1)}, u32[]{:S(2)}, u32[]{:S(2)}) %collective-permute-start.11) | collective-permute-done | bytes 98336 | tf_op jit(solution)/shard_map/ppermute | solution.py:28
  42.5 0.4 collective-permute-done.15.rest_6_
  42.9 1.2 %collective-permute-done.16.rest_7_ = bf16[192,128]{1,0:T(8,128)(2,1)S(1)} collective-permute-done((bf16[192,128]{1,0:T(8,128)(2,1)S(1)}, bf16[192,128]{1,0:T(8,128)(2,1)S(1)}, u32[]{:S(2)}, u32[]{:S(2)}) %collective-permute-start.16) | collective-permute-done | bytes 49184 | tf_op jit(solution)/shard_map/ppermute | solution.py:28
  44.1 0.9 %shard_map.53 = bf16[192,1536]{1,0:T(8,128)(2,1)} custom-call(s32[1]{0:T(128)} %bitcast.me_ref, bf16[192,256]{1,0:T(8,128)(2,1)S(1)} %get-tuple-element.42.rest_0_, bf16[192,256]{1,0:T(8,128)(2,1)S(1)} %collective-permute-done.9.rest_1_, bf16[192,256]{1,0:T(8,128)(2,1)S(1)} %collective-permute-done.10.rest_2_, ...), custom_call_target="tpu_custom_call" | custom-call | tf_op jit(solution)/shard_map/pallas_call | solution.py:329
  (20 shorter events, 0.9 us)
Async XLA Ops:
  1.6 3.7 %collective-permute-start = (bf16[576,384]{1,0:T(8,128)(2,1)S(1)}, bf16[576,384]{1,0:T(8,128)(2,1)S(1)}, u32[]{:S(2)}, u32[]{:S(2)}) collective-permute-start(bf16[576,384]{1,0:T(8,128)(2,1)S(1)} %get-tuple-element.31), channel_id=1, source_target_pairs={{0,1},{1,0},{2,3},{3,2},{4,5},{5,4},{6,7},{7,6},{8,9},{9,8},{10,11... | collective-permute-start | bytes 1327112 | tf_op jit(solution)/shard_map/ppermute | solution.py:28
  2.4 8.6 %collective-permute-start.3 = (bf16[384,384]{1,0:T(8,128)(2,1)S(1)}, bf16[384,384]{1,0:T(8,128)(2,1)S(1)}, u32[]{:S(2)}, u32[]{:S(2)}) collective-permute-start(bf16[384,384]{1,0:T(8,128)(2,1)S(1)} %get-tuple-element.33), channel_id=1, source_target_pairs={{0,2},{1,3},{2,0},{3,1},{4,6},{5,7},{6,4},{7,5},{8,10},{9,11},{10,... | collective-permute-start | bytes 884744 | tf_op jit(solution)/shard_map/ppermute | solution.py:28
  3.6 14.6 %collective-permute-start.4 = (bf16[384,384]{1,0:T(8,128)(2,1)S(1)}, bf16[384,384]{1,0:T(8,128)(2,1)S(1)}, u32[]{:S(2)}, u32[]{:S(2)}) collective-permute-start(bf16[384,384]{1,0:T(8,128)(2,1)S(1)} %get-tuple-element.34), channel_id=1, source_target_pairs={{0,3},{1,2},{2,1},{3,0},{4,7},{5,6},{6,5},{7,4},{8,11},{9,10},{10,... | collective-permute-start | bytes 884744 | tf_op jit(solution)/shard_map/ppermute | solution.py:28
  4.1 19.5 %collective-permute-start.1 = (bf16[384,384]{1,0:T(8,128)(2,1)S(1)}, bf16[384,384]{1,0:T(8,128)(2,1)S(1)}, u32[]{:S(2)}, u32[]{:S(2)}) collective-permute-start(bf16[384,384]{1,0:T(8,128)(2,1)S(1)} %get-tuple-element.32), channel_id=1, source_target_pairs={{0,2},{1,3},{2,0},{3,1},{4,6},{5,7},{6,4},{7,5},{8,10},{9,11},{10,... | collective-permute-start | bytes 884744 | tf_op jit(solution)/shard_map/ppermute | solution.py:28
  5.5 19.2 %collective-permute-start.5 = (bf16[784,384]{1,0:T(8,128)(2,1)S(1)}, bf16[784,384]{1,0:T(8,128)(2,1)S(1)}, u32[]{:S(2)}, u32[]{:S(2)}) collective-permute-start(bf16[784,384]{1,0:T(8,128)(2,1)S(1)} %shard_map.48.refs_4_), channel_id=1, source_target_pairs={{0,4},{4,0},{8,12},{12,8},{1,5},{5,1},{9,13},{13,9},{2,6},{6,2},{1... | collective-permute-start | bytes 1806344 | tf_op jit(solution)/shard_map/ppermute | solution.py:37
  5.7 19.0 %collective-permute-start.6 = (bf16[784,384]{1,0:T(8,128)(2,1)S(1)}, bf16[784,384]{1,0:T(8,128)(2,1)S(1)}, u32[]{:S(2)}, u32[]{:S(2)}) collective-permute-start(bf16[784,384]{1,0:T(8,128)(2,1)S(1)} %shard_map.48.refs_4_), channel_id=1, source_target_pairs={{4,8},{8,4},{5,9},{9,5},{6,10},{10,6},{7,11},{11,7},{20,24},{24,20... | collective-permute-start | bytes 1806344 | tf_op jit(solution)/shard_map/ppermute | solution.py:37
  18.3 15.0 %collective-permute-start.7 = (bf16[768,256]{1,0:T(8,128)(2,1)S(1)}, bf16[768,256]{1,0:T(8,128)(2,1)S(1)}, u32[]{:S(2)}, u32[]{:S(2)}) collective-permute-start(bf16[768,256]{1,0:T(8,128)(2,1)S(1)} %shard_map.49), channel_id=1, source_target_pairs={{0,4},{4,0},{8,12},{12,8},{1,5},{5,1},{9,13},{13,9},{2,6},{6,2},{1... | collective-permute-start | bytes 1179656 | tf_op jit(solution)/shard_map/ppermute | solution.py:37
  18.3 15.0 %collective-permute-start.8 = (bf16[768,256]{1,0:T(8,128)(2,1)S(1)}, bf16[768,256]{1,0:T(8,128)(2,1)S(1)}, u32[]{:S(2)}, u32[]{:S(2)}) collective-permute-start(bf16[768,256]{1,0:T(8,128)(2,1)S(1)} %shard_map.49), channel_id=1, source_target_pairs={{4,8},{8,4},{5,9},{9,5},{6,10},{10,6},{7,11},{11,7},{20,24},{24,20... | collective-permute-start | bytes 1179656 | tf_op jit(solution)/shard_map/ppermute | solution.py:37
  23.7 5.6 %collective-permute-start.2 = (bf16[192,384]{1,0:T(8,128)(2,1)S(1)}, bf16[192,384]{1,0:T(8,128)(2,1)S(1)}, u32[]{:S(2)}, u32[]{:S(2)}) collective-permute-start(bf16[192,384]{1,0:T(8,128)(2,1)S(1)} %get-tuple-element.55), channel_id=1, source_target_pairs={{0,1},{1,0},{2,3},{3,2},{4,5},{5,4},{6,7},{7,6},{8,9},{9,8},{10,11... | collective-permute-start | bytes 442376 | tf_op jit(solution)/shard_map/ppermute | solution.py:28
  24.7 12.4 %collective-permute-start.12 = (bf16[768,128]{1,0:T(8,128)(2,1)S(1)}, bf16[768,128]{1,0:T(8,128)(2,1)S(1)}, u32[]{:S(2)}, u32[]{:S(2)}) collective-permute-start(bf16[768,128]{1,0:T(8,128)(2,1)S(1)} %shard_map.47), channel_id=1, source_target_pairs={{0,4},{4,0},{8,12},{12,8},{1,5},{5,1},{9,13},{13,9},{2,6},{6,2},{1... | collective-permute-start | bytes 589832 | tf_op jit(solution)/shard_map/ppermute | solution.py:37
  24.8 12.3 %collective-permute-start.13 = (bf16[768,128]{1,0:T(8,128)(2,1)S(1)}, bf16[768,128]{1,0:T(8,128)(2,1)S(1)}, u32[]{:S(2)}, u32[]{:S(2)}) collective-permute-start(bf16[768,128]{1,0:T(8,128)(2,1)S(1)} %shard_map.47), channel_id=1, source_target_pairs={{4,8},{8,4},{5,9},{9,5},{6,10},{10,6},{7,11},{11,7},{20,24},{24,20... | collective-permute-start | bytes 589832 | tf_op jit(solution)/shard_map/ppermute | solution.py:37
  34.7 2.4 %collective-permute-start.9 = (bf16[192,256]{1,0:T(8,128)(2,1)S(1)}, bf16[192,256]{1,0:T(8,128)(2,1)S(1)}, u32[]{:S(2)}, u32[]{:S(2)}) collective-permute-start(bf16[192,256]{1,0:T(8,128)(2,1)S(1)} %get-tuple-element.43), channel_id=1, source_target_pairs={{0,1},{1,0},{2,3},{3,2},{4,5},{5,4},{6,7},{7,6},{8,9},{9,8},{10,11... | collective-permute-start | bytes 294920 | tf_op jit(solution)/shard_map/ppermute | solution.py:28
  35.4 4.8 %collective-permute-start.10 = (bf16[192,256]{1,0:T(8,128)(2,1)S(1)}, bf16[192,256]{1,0:T(8,128)(2,1)S(1)}, u32[]{:S(2)}, u32[]{:S(2)}) collective-permute-start(bf16[192,256]{1,0:T(8,128)(2,1)S(1)} %get-tuple-element.45), channel_id=1, source_target_pairs={{0,2},{1,3},{2,0},{3,1},{4,6},{5,7},{6,4},{7,5},{8,10},{9,11},{10,... | collective-permute-start | bytes 294920 | tf_op jit(solution)/shard_map/ppermute | solution.py:28
  36.6 5.9 %collective-permute-start.11 = (bf16[192,256]{1,0:T(8,128)(2,1)S(1)}, bf16[192,256]{1,0:T(8,128)(2,1)S(1)}, u32[]{:S(2)}, u32[]{:S(2)}) collective-permute-start(bf16[192,256]{1,0:T(8,128)(2,1)S(1)} %get-tuple-element.46), channel_id=1, source_target_pairs={{0,3},{1,2},{2,1},{3,0},{4,7},{5,6},{6,5},{7,4},{8,11},{9,10},{10,... | collective-permute-start | bytes 294920 | tf_op jit(solution)/shard_map/ppermute | solution.py:28
  38.0 4.5 %collective-permute-start.14 = (bf16[192,128]{1,0:T(8,128)(2,1)S(1)}, bf16[192,128]{1,0:T(8,128)(2,1)S(1)}, u32[]{:S(2)}, u32[]{:S(2)}) collective-permute-start(bf16[192,128]{1,0:T(8,128)(2,1)S(1)} %get-tuple-element.52), channel_id=1, source_target_pairs={{0,1},{1,0},{2,3},{3,2},{4,5},{5,4},{6,7},{7,6},{8,9},{9,8},{10,11... | collective-permute-start | bytes 147464 | tf_op jit(solution)/shard_map/ppermute | solution.py:28
  38.2 4.7 %collective-permute-start.15 = (bf16[192,128]{1,0:T(8,128)(2,1)S(1)}, bf16[192,128]{1,0:T(8,128)(2,1)S(1)}, u32[]{:S(2)}, u32[]{:S(2)}) collective-permute-start(bf16[192,128]{1,0:T(8,128)(2,1)S(1)} %get-tuple-element.53), channel_id=1, source_target_pairs={{0,2},{1,3},{2,0},{3,1},{4,6},{5,7},{6,4},{7,5},{8,10},{9,11},{10,... | collective-permute-start | bytes 147464 | tf_op jit(solution)/shard_map/ppermute | solution.py:28
  39.4 4.7 %collective-permute-start.16 = (bf16[192,128]{1,0:T(8,128)(2,1)S(1)}, bf16[192,128]{1,0:T(8,128)(2,1)S(1)}, u32[]{:S(2)}, u32[]{:S(2)}) collective-permute-start(bf16[192,128]{1,0:T(8,128)(2,1)S(1)} %get-tuple-element.54), channel_id=1, source_target_pairs={{0,3},{1,2},{2,1},{3,0},{4,7},{5,6},{6,5},{7,4},{8,11},{9,10},{10,... | collective-permute-start | bytes 147464 | tf_op jit(solution)/shard_map/ppermute | solution.py:28

commit v4 on v3

--- a/solution.py
+++ b/solution.py
@@ -61,10 +61,9 @@
         (q_ref.at[:, lanes(1)], sibling_ref.at[pl.ds(2 * rows, rows)]),
         (q_ref.at[:, lanes(0)], own_q_ref),
     ]
-    jobs += [
-        (q_ref.at[:, lanes(bit)], far_q_refs[bit // 2 - 1].at[pl.ds(bit % 2 * rows, rows)])
-        for bit in range(2, devices)
-    ]
+    for i, ref in enumerate(far_q_refs):
+        passed = sibling_ref.at[pl.ds((3 + i) * rows, rows)]
+        jobs += [(q_ref.at[:, lanes(2 * i + 2)], ref), (q_ref.at[:, lanes(2 * i + 3)], passed)]
     copies = [pltpu.make_async_copy(src, dst, sems.at[i]) for i, (src, dst) in enumerate(jobs)]
     for copy in copies:
         copy.start()
@@ -83,7 +82,8 @@
     rows, width = query.shape
     part = width // devices
     far = devices - 2
-    sizes = [2 * rows + COUNT_ROWS, 3 * rows, rows] + [2 * rows] * far + [2 * rows] * (far // 2)
+    sizes = [2 * rows + COUNT_ROWS, (3 + far // 2) * rows, rows]
+    sizes += [2 * rows] * far + [rows] * (far // 2)
     fields = [pltpu.with_memory_space_constraint(f, pltpu.HBM) for f in (query, key, value)]
     results = pl.pallas_call(
         functools.partial(pack_body, devices, part),
@@ -105,8 +105,8 @@
 def stack_body(jobs, *refs):
     blocks, out_ref, sems = refs[:-2], refs[-2], refs[-1]
     copies, base = [], 0
-    for i, (size, lanes) in enumerate(jobs):
-        source = blocks[i].at[pl.ds(0, size), lanes]
+    for i, (first, size, lanes) in enumerate(jobs):
+        source = blocks[i].at[pl.ds(first, size), lanes]
         copies.append(
             pltpu.make_async_copy(source, out_ref.at[pl.ds(base, size)], sems.at[i])
         )
@@ -117,17 +117,18 @@
         copy.wait()
 
 
-def stack(blocks, sizes, start, width):
-    jobs = [(size, pl.ds(start, width)) for size in sizes]
+def stack(blocks, spans, start, width, flops=0, pad=0):
+    jobs = [(first, size, pl.ds(start, width)) for first, size in spans]
+    rows = sum(size for _, size in spans)
     return pl.pallas_call(
         functools.partial(stack_body, jobs),
-        out_shape=pltpu.VMEM((sum(sizes), width), jnp.bfloat16),
+        out_shape=pltpu.VMEM((rows + pad, width), jnp.bfloat16),
         in_specs=in_vmem(len(blocks)),
         out_specs=pl.BlockSpec(memory_space=pltpu.VMEM),
         scratch_shapes=[pltpu.SemaphoreType.DMA((len(blocks),))],
         compiler_params=pltpu.CompilerParams(vmem_limit_bytes=VMEM_LIMIT),
         cost_estimate=pl.CostEstimate(
-            flops=0, bytes_accessed=sum(sizes) * width, transcendentals=0
+            flops=flops, bytes_accessed=rows * width, transcendentals=0
         ),
     )(*blocks)
 
@@ -206,23 +207,25 @@
         total_ref[place, :] = summed[:, HEAD_DIM:]
 
 
-def late_body(groups, operands, frames, tiles, tokens, heads, first, lane, *refs):
+def late_body(groups, operands, frames, tiles, tokens, heads, states, first, lane, *refs):
     rows = tiles * tokens
     queries, arrays = refs[:frames], refs[frames : frames + operands]
-    max_ref, total_ref, sum_ref = refs[frames + operands : frames + operands + 3]
-    outs = refs[frames + operands + 3 :]
+    left = refs[frames + operands : frames + operands + 3 * states]
+    outs = refs[frames + operands + 3 * states :]
     counts = counts_of(arrays, groups, rows)
     windows = [window_of(tile, tiles, groups) for tile in range(tiles)]
     block = frames * tokens
+    share = block // states
 
     def asked(head, tile):
         return jnp.concatenate(
             [ref[pl.ds(tile * tokens, tokens), features(first + head)] for ref in queries], 0
         )
 
-    def place(head, tile):
-        start = ((first + head) * tiles + tile) * block
-        return pl.ds(start if isinstance(start, int) else pl.multiple_of(start, block), block)
+    def early(head, tile):
+        start = ((first + head) * tiles + tile) * share
+        at = pl.ds(start if isinstance(start, int) else pl.multiple_of(start, share), share)
+        return [jnp.concatenate([ref[at, :] for ref in left[which::3]], 0) for which in range(3)]
 
     def write(head, tile, result):
         for frame in range(frames):
@@ -240,24 +243,24 @@
     for head in range(heads):
         lanes = features(lane + head)
         for tile, window in enumerate(windows):
-            at = place(head, tile)
+            largest, total, summed = early(head, tile)
             scores = products(
                 asked(head, tile), gather(arrays, groups, window, 0, tokens, lanes)
             )
-            before = jnp.concatenate([max_ref[at, :]] * (scores.shape[1] // HEAD_DIM), 1)
-            weight = jnp.exp2((scores - before) * SCALE).astype(jnp.bfloat16)
+            largest = jnp.concatenate([largest] * (scores.shape[1] // HEAD_DIM), 1)
+            weight = jnp.exp2((scores - largest) * SCALE).astype(jnp.bfloat16)
             kept = jnp.concatenate(
                 [real[group][n] for group, n in window for _ in groups[group][1]], 0
             )
             values = gather(arrays, groups, window, rows, tokens, lanes) * kept
-            summed = jnp.dot(
+            added = jnp.dot(
                 weight,
                 jnp.concatenate([values, kept], 1),
                 preferred_element_type=jnp.float32,
             )
-            total = total_ref[at, :] + summed[:, HEAD_DIM:]
+            total = total + added[:, HEAD_DIM:]
             worst = jnp.where(total < LARGEST_TOTAL, worst, 1.0)
-            result = (sum_ref[at, :] + summed[:, :HEAD_DIM]) / total
+            result = (summed + added[:, :HEAD_DIM]) / total
             write(head, tile, result.astype(jnp.bfloat16))
 
     @pl.when(jnp.max(worst) > 0.0)
@@ -265,29 +268,29 @@
         def one_head(head, _):
             lanes = features(lane + head)
             for tile, window in enumerate(windows):
-                at = place(head, tile)
+                before, total, summed = early(head, tile)
                 scores = products(
                     asked(head, tile), gather(arrays, groups, window, 0, tokens, lanes)
                 )
                 scores = scores + bias_of(counts, groups, window, tokens)
-                before = max_ref[at, :]
                 largest = jnp.maximum(before[:, :1], jnp.max(scores, axis=1, keepdims=True))
                 shrink = jnp.exp2((before - largest) * SCALE)
                 weight = jnp.exp2((scores - largest) * SCALE)
-                total = jnp.sum(weight, axis=1, keepdims=True) + total_ref[at, :] * shrink
-                summed = jnp.dot(
+                total = jnp.sum(weight, axis=1, keepdims=True) + total * shrink
+                added = jnp.dot(
                     weight.astype(jnp.bfloat16),
                     gather(arrays, groups, window, rows, tokens, lanes),
                     preferred_element_type=jnp.float32,
                 )
-                result = (summed + sum_ref[at, :] * shrink) / total
+                result = (added + summed * shrink) / total
                 write(head, tile, result.astype(jnp.bfloat16))
             return 0
 
         lax.fori_loop(0, heads, one_head, 0)
 
 
-def attend(queries, arrays, groups, tiles, tokens, heads, first=0, base=0, state=(), weigh=1):
+def attend(queries, arrays, groups, tiles, tokens, heads, first=0, base=0, state=(), weigh=0):
+    weigh = 0 if state else 0
     frames = len(queries)
     operands = [*queries, *arrays, *state]
     size = sum(len(fields) for _, fields in groups)
@@ -295,7 +298,7 @@
     shape = (groups, len(arrays), frames, tiles, tokens, heads)
     if state:
         outs = [pltpu.VMEM((tiles * tokens, heads * HEAD_DIM), jnp.bfloat16)] * frames
-        kernel = functools.partial(late_body, *shape, first, base)
+        kernel = functools.partial(late_body, *shape, len(state) // 3, first, base)
     else:
         outs = [pltpu.VMEM((heads * tiles * frames * tokens, HEAD_DIM), jnp.float32)] * 3
         kernel = functools.partial(early_body, *shape)
@@ -361,19 +364,31 @@
 
     sibling = swap_head(sibling, 1, devices)
     far = [swap_head(b, bit, devices) for bit, b in enumerate(far, 2)]
-    far_query = [swap_head(b, 2 * i + 2, devices) for i, b in enumerate(far_query)]
-    near = by_height(stack([own, sibling], [own.shape[0], 2 * rows], 0, part))
+    far_query = [
+        swap_head(
+            stack([b, sibling], [(0, rows), ((3 + i) * rows, rows)], 0, part, 0, 0), 2 * i + 2, devices
+        )
+        for i, b in enumerate(far_query)
+    ]
+    near = by_height(stack([own, sibling], [(0, own.shape[0]), (0, 2 * rows)], 0, part))
     near = near + by_time(near)
 
-    queries = [own_query, sibling[2 * rows :]]
+    queries = [own_query, sibling[2 * rows : 3 * rows]]
     for block in far_query:
-        queries += [block[:rows], swap_head(block[rows:], 1, devices)]
+        queries += [block[:rows], block[rows : 2 * rows]]
 
     cut = heads - heads // 3
     parts = [(0, heads)] if WHOLE else [(0, cut), (cut, heads - cut)]
     across = []
     for first, count in parts:
-        block = stack(far, [2 * rows] * len(far), first * HEAD_DIM, count * HEAD_DIM)
+        block = stack(
+            far,
+            [(0, 2 * rows)] * len(far),
+            first * HEAD_DIM,
+            count * HEAD_DIM,
+            0 if first else 2000000000,
+            0 if first else 0,
+        )
         if first:
             block, *near = lax.optimization_barrier((block, *near))
         block = by_height(block)
@@ -385,7 +400,11 @@
     arrays = near + far
     groups = [(i, [(i, base) for base in near_rows]) for i in range(len(near))]
     groups[0][1].extend((len(near) + i, 0) for i in range(len(far)))
-    state = attend(queries, arrays, groups, tiles, tokens, heads)
+    state = [
+        left
+        for part in (queries,)
+        for left in attend(part, arrays, groups, tiles, tokens, heads)
+    ]
 
     pieces = []
     for i, (first, count) in enumerate(parts):

time: 45.2 us -> 44.5 us (0.985)
  starting transfers between devices: 22.8 us -> 19.3 us
  waiting for transfers between devices: 12.9 us -> 15.2 us
    ppermute x6, waiting for transfers between devices: 0.02 us -> 3.9 us  [swap_pairs(): return lax.ppermute(block, 'tok', route)]
    ppermute x6, starting transfers between devices: 13.6 us -> 11.4 us  [swap_pairs(): return lax.ppermute(block, 'tok', route)]
    ppermute x11 -> x10, waiting for transfers between devices: 12.9 us -> 11.3 us  [swap_head(): return lax.ppermute(block, 'head', [(i, i ^ bit) for i in range(devices)])]
    ppermute x11 -> x10, starting transfers between devices: 9.13 us -> 7.86 us  [swap_head(): return lax.ppermute(block, 'head', [(i, i ^ bit) for i in range(devices)])]
  transfers between devices with their start and end apart: 17 -> 16, of which waited for: 6 -> 8; matrix products, arithmetic and copies ran while one was open for 0% -> 0% of each run, Pallas kernels for 15% -> 16%
where the time goes in v4:
time: 44.5 us; the launch traced here: 44.1 us
  starting transfers between devices  19.3 us (43%)
  waiting for transfers between devices  15.2 us (34%)
  Pallas kernels  9.47 us (21%)
    ppermute x6, starting transfers between devices, swap_pairs(): return lax.ppermute(block, 'tok', route)  11.4 us
    ppermute x10, waiting for transfers between devices, swap_head(): return lax.ppermute(block, 'head', [(i, i ^ bit) for i in range(devices)])  11.3 us
    ppermute x10, starting transfers between devices, swap_head(): return lax.ppermute(block, 'head', [(i, i ^ bit) for i in range(devices)])  7.86 us
    pallas_call x3, Pallas kernels, attend(): pl.pallas_call(kernel, out_shape=outs, in_specs=in_vmem(len(operands)), o...  6.3 us
    ppermute x6, waiting for transfers between devices, swap_pairs(): return lax.ppermute(block, 'tok', route)  3.9 us
    pallas_call x1, Pallas kernels, pack(): pl.pallas_call(functools.partial(pack_body, devices, part), out_shape=[pl...  1.64 us
  transfers between devices with their start and end apart: 16, of which 8 were waited for; matrix products, arithmetic and copies ran while one was open for 0% of the time, Pallas kernels for 16%

profile of v4, /device:TPU:9, one launch (start us, length us, event | category | flops | bytes accessed | tf_op | source)
XLA Modules:
  0.0 44.1 jit_solution(693402084577173359)
XLA Ops:
  0.0 1.6 %shard_map.46 = (bf16[400,384]{1,0:T(8,128)(2,1)S(1)}, bf16[768,384]{1,0:T(8,128)(2,1)S(1)}, bf16[192,384]{1,0:T(8,128)(2,1)S(1)}, bf16[384,384]{1,0:T(8,128)(2,...) custom-call(s32[3]{0:T(128)} %counts_in.1, s32[1]{0:T(128)} %bitcast.me_ref, ...), custom_call_target="tpu_custom_call" | custom-call | bytes 3538944 | tf_op jit(solution)/shard_map/pallas_call | solution.py:88
  1.6 0.7 %collective-permute-start = (bf16[768,384]{1,0:T(8,128)(2,1)S(1)}, bf16[768,384]{1,0:T(8,128)(2,1)S(1)}, u32[]{:S(2)}, u32[]{:S(2)}) collective-permute-start(bf16[768,384]{1,0:T(8,128)(2,1)S(1)} %get-tuple-element.31), channel_id=1, source_target_pairs={{0,1},{1,0},{2,3},{3,2},{4,5},{5,4},{6,7},{7,6},{8,9},{9,8},{10,11... | collective-permute-start | bytes 1769480 | tf_op jit(solution)/shard_map/ppermute | solution.py:28
  2.4 1.2 %collective-permute-start.2 = (bf16[384,384]{1,0:T(8,128)(2,1)S(1)}, bf16[384,384]{1,0:T(8,128)(2,1)S(1)}, u32[]{:S(2)}, u32[]{:S(2)}) collective-permute-start(bf16[384,384]{1,0:T(8,128)(2,1)S(1)} %get-tuple-element.33), channel_id=1, source_target_pairs={{0,2},{1,3},{2,0},{3,1},{4,6},{5,7},{6,4},{7,5},{8,10},{9,11},{10,... | collective-permute-start | bytes 884744 | tf_op jit(solution)/shard_map/ppermute | solution.py:28
  3.6 0.5 %collective-permute-start.3 = (bf16[384,384]{1,0:T(8,128)(2,1)S(1)}, bf16[384,384]{1,0:T(8,128)(2,1)S(1)}, u32[]{:S(2)}, u32[]{:S(2)}) collective-permute-start(bf16[384,384]{1,0:T(8,128)(2,1)S(1)} %get-tuple-element.34), channel_id=1, source_target_pairs={{0,3},{1,2},{2,1},{3,0},{4,7},{5,6},{6,5},{7,4},{8,11},{9,10},{10,... | collective-permute-start | bytes 884744 | tf_op jit(solution)/shard_map/ppermute | solution.py:28
  4.3 4.5 %collective-permute-start.5 = (bf16[784,384]{1,0:T(8,128)(2,1)S(1)}, bf16[784,384]{1,0:T(8,128)(2,1)S(1)}, u32[]{:S(2)}, u32[]{:S(2)}) collective-permute-start(bf16[784,384]{1,0:T(8,128)(2,1)S(1)} %shard_map.49.refs_4_), channel_id=1, source_target_pairs={{4,8},{8,4},{5,9},{9,5},{6,10},{10,6},{7,11},{11,7},{20,24},{24,20... | collective-permute-start | bytes 1806344 | tf_op jit(solution)/shard_map/ppermute | solution.py:37
  8.8 0.4 shard_map.47
  9.2 1.3 %collective-permute-start.1 = (bf16[384,384]{1,0:T(8,128)(2,1)S(1)}, bf16[384,384]{1,0:T(8,128)(2,1)S(1)}, u32[]{:S(2)}, u32[]{:S(2)}) collective-permute-start(bf16[384,384]{1,0:T(8,128)(2,1)S(1)} %shard_map.47), channel_id=1, source_target_pairs={{0,2},{1,3},{2,0},{3,1},{4,6},{5,7},{6,4},{7,5},{8,10},{9,11},{10,... | collective-permute-start | bytes 884744 | tf_op jit(solution)/shard_map/ppermute | solution.py:28
  10.5 0.5 %collective-permute-done.2.refs_0_.refs_7_ = bf16[384,384]{1,0:T(8,128)(2,1)S(1)} collective-permute-done((bf16[384,384]{1,0:T(8,128)(2,1)S(1)}, bf16[384,384]{1,0:T(8,128)(2,1)S(1)}, u32[]{:S(2)}, u32[]{:S(2)}) %collective-permute-start.2) | collective-permute-done | bytes 294944 | tf_op jit(solution)/shard_map/ppermute | solution.py:28
  11.0 7.2 %collective-permute-done.3.refs_1_.refs_8_ = bf16[384,384]{1,0:T(8,128)(2,1)S(1)} collective-permute-done((bf16[384,384]{1,0:T(8,128)(2,1)S(1)}, bf16[384,384]{1,0:T(8,128)(2,1)S(1)}, u32[]{:S(2)}, u32[]{:S(2)}) %collective-permute-start.3) | collective-permute-done | bytes 294944 | tf_op jit(solution)/shard_map/ppermute | solution.py:28
  18.3 4.5 %collective-permute-start.7 = (bf16[768,256]{1,0:T(8,128)(2,1)S(1)}, bf16[768,256]{1,0:T(8,128)(2,1)S(1)}, u32[]{:S(2)}, u32[]{:S(2)}) collective-permute-start(bf16[768,256]{1,0:T(8,128)(2,1)S(1)} %shard_map.50), channel_id=1, source_target_pairs={{4,8},{8,4},{5,9},{9,5},{6,10},{10,6},{7,11},{11,7},{20,24},{24,20... | collective-permute-start | bytes 1179656 | tf_op jit(solution)/shard_map/ppermute | solution.py:37
  23.0 2.3 %collective-permute-start.12 = (bf16[768,128]{1,0:T(8,128)(2,1)S(1)}, bf16[768,128]{1,0:T(8,128)(2,1)S(1)}, u32[]{:S(2)}, u32[]{:S(2)}) collective-permute-start(bf16[768,128]{1,0:T(8,128)(2,1)S(1)} %shard_map.48), channel_id=1, source_target_pairs={{4,8},{8,4},{5,9},{9,5},{6,10},{10,6},{7,11},{11,7},{20,24},{24,20... | collective-permute-start | bytes 589832 | tf_op jit(solution)/shard_map/ppermute | solution.py:37
  25.3 4.0 %shard_map.51 = (f32[2304,128]{1,0:T(8,128)S(1)}, f32[2304,128]{1,0:T(8,128)S(1)}, f32[2304,128]{1,0:T(8,128)S(1)}) custom-call(bf16[192,384]{1,0:T(8,128)(2,1)S(1)} %get-tuple-element.30.refs_0_, bf16[192,384]{1,0:T(8,128)(2,1)S(1)} %slice.12.refs_1_, bf16[192,384]{1,0:T(8,128)(2,1)S(1)} %get-tuple-element.56.refs_2_, ...), custom_call_target="tpu_custom_call" | custom-call | tf_op jit(solution)/shard_map/pallas_call | solution.py:305
  29.5 3.0 %collective-permute-done.7.refs_7_ = bf16[768,256]{1,0:T(8,128)(2,1)S(1)} collective-permute-done((bf16[768,256]{1,0:T(8,128)(2,1)S(1)}, bf16[768,256]{1,0:T(8,128)(2,1)S(1)}, u32[]{:S(2)}, u32[]{:S(2)}) %collective-permute-start.7) | collective-permute-done | bytes 393248 | tf_op jit(solution)/shard_map/ppermute | solution.py:37
  32.5 1.4 %shard_map.52 = (bf16[192,256]{1,0:T(8,128)(2,1)S(1)}, bf16[192,256]{1,0:T(8,128)(2,1)S(1)}, bf16[192,256]{1,0:T(8,128)(2,1)S(1)}, bf16[192,256]{1,0:T(8,128)(2,1)S(1)}) custom-call(bf16[192,384]{1,0:T(8,128)(2,1)S(1)} %get-tuple-element.30.refs_0_, bf16[192,384]{1,0:T(8,128)(2,1)S(1)} %slice.12.refs_1_, bf16[192,384]{1,0:T(8,128)(2,1)S(1)} %get-tuple-element.56.refs_2_, ...), custom_call_target="tpu_custom_call" | custom-call | tf_op jit(solution)/shard_map/pallas_call | solution.py:305
  34.2 1.3 %collective-permute-start.10 = (bf16[192,256]{1,0:T(8,128)(2,1)S(1)}, bf16[192,256]{1,0:T(8,128)(2,1)S(1)}, u32[]{:S(2)}, u32[]{:S(2)}) collective-permute-start(bf16[192,256]{1,0:T(8,128)(2,1)S(1)} %get-tuple-element.46), channel_id=1, source_target_pairs={{0,3},{1,2},{2,1},{3,0},{4,7},{5,6},{6,5},{7,4},{8,11},{9,10},{10,... | collective-permute-start | bytes 294920 | tf_op jit(solution)/shard_map/ppermute | solution.py:28
  35.8 0.8 %collective-permute-done.12.refs_7_ = bf16[768,128]{1,0:T(8,128)(2,1)S(1)} collective-permute-done((bf16[768,128]{1,0:T(8,128)(2,1)S(1)}, bf16[768,128]{1,0:T(8,128)(2,1)S(1)}, u32[]{:S(2)}, u32[]{:S(2)}) %collective-permute-start.12) | collective-permute-done | bytes 196640 | tf_op jit(solution)/shard_map/ppermute | solution.py:37
  36.6 0.9 %shard_map.53 = (bf16[192,128]{1,0:T(8,128)(2,1)S(1)}, bf16[192,128]{1,0:T(8,128)(2,1)S(1)}, bf16[192,128]{1,0:T(8,128)(2,1)S(1)}, bf16[192,128]{1,0:T(8,128)(2,1)S(1)}) custom-call(bf16[192,384]{1,0:T(8,128)(2,1)S(1)} %get-tuple-element.30.refs_0_, bf16[192,384]{1,0:T(8,128)(2,1)S(1)} %slice.12.refs_1_, bf16[192,384]{1,0:T(8,128)(2,1)S(1)} %get-tuple-element.56.refs_2_, ...), custom_call_target="tpu_custom_call" | custom-call | tf_op jit(solution)/shard_map/pallas_call | solution.py:305
  37.5 0.5 %collective-permute-start.13 = (bf16[192,128]{1,0:T(8,128)(2,1)S(1)}, bf16[192,128]{1,0:T(8,128)(2,1)S(1)}, u32[]{:S(2)}, u32[]{:S(2)}) collective-permute-start(bf16[192,128]{1,0:T(8,128)(2,1)S(1)} %get-tuple-element.52), channel_id=1, source_target_pairs={{0,1},{1,0},{2,3},{3,2},{4,5},{5,4},{6,7},{7,6},{8,9},{9,8},{10,11... | collective-permute-start | bytes 147464 | tf_op jit(solution)/shard_map/ppermute | solution.py:28
  38.0 1.2 %collective-permute-start.14 = (bf16[192,128]{1,0:T(8,128)(2,1)S(1)}, bf16[192,128]{1,0:T(8,128)(2,1)S(1)}, u32[]{:S(2)}, u32[]{:S(2)}) collective-permute-start(bf16[192,128]{1,0:T(8,128)(2,1)S(1)} %get-tuple-element.53), channel_id=1, source_target_pairs={{0,2},{1,3},{2,0},{3,1},{4,6},{5,7},{6,4},{7,5},{8,10},{9,11},{10,... | collective-permute-start | bytes 147464 | tf_op jit(solution)/shard_map/ppermute | solution.py:28
  39.2 0.5 %collective-permute-start.15 = (bf16[192,128]{1,0:T(8,128)(2,1)S(1)}, bf16[192,128]{1,0:T(8,128)(2,1)S(1)}, u32[]{:S(2)}, u32[]{:S(2)}) collective-permute-start(bf16[192,128]{1,0:T(8,128)(2,1)S(1)} %get-tuple-element.54), channel_id=1, source_target_pairs={{0,3},{1,2},{2,1},{3,0},{4,7},{5,6},{6,5},{7,4},{8,11},{9,10},{10,... | collective-permute-start | bytes 147464 | tf_op jit(solution)/shard_map/ppermute | solution.py:28
  39.7 1.2 %collective-permute-done.9.rest_2_ = bf16[192,256]{1,0:T(8,128)(2,1)S(1)} collective-permute-done((bf16[192,256]{1,0:T(8,128)(2,1)S(1)}, bf16[192,256]{1,0:T(8,128)(2,1)S(1)}, u32[]{:S(2)}, u32[]{:S(2)}) %collective-permute-start.9) | collective-permute-done | bytes 98336 | tf_op jit(solution)/shard_map/ppermute | solution.py:28
  40.9 1.1 %collective-permute-done.14.rest_6_ = bf16[192,128]{1,0:T(8,128)(2,1)S(1)} collective-permute-done((bf16[192,128]{1,0:T(8,128)(2,1)S(1)}, bf16[192,128]{1,0:T(8,128)(2,1)S(1)}, u32[]{:S(2)}, u32[]{:S(2)}) %collective-permute-start.14) | collective-permute-done | bytes 49184 | tf_op jit(solution)/shard_map/ppermute | solution.py:28
  41.9 1.3 %collective-permute-done.15.rest_7_ = bf16[192,128]{1,0:T(8,128)(2,1)S(1)} collective-permute-done((bf16[192,128]{1,0:T(8,128)(2,1)S(1)}, bf16[192,128]{1,0:T(8,128)(2,1)S(1)}, u32[]{:S(2)}, u32[]{:S(2)}) %collective-permute-start.15) | collective-permute-done | bytes 49184 | tf_op jit(solution)/shard_map/ppermute | solution.py:28
  43.3 0.9 %shard_map.54 = bf16[192,1536]{1,0:T(8,128)(2,1)} custom-call(s32[1]{0:T(128)} %bitcast.me_ref, bf16[192,256]{1,0:T(8,128)(2,1)S(1)} %get-tuple-element.42.rest_0_, bf16[192,256]{1,0:T(8,128)(2,1)S(1)} %collective-permute-done.8.rest_1_, bf16[192,256]{1,0:T(8,128)(2,1)S(1)} %collective-permute-done.9.rest_2_, ...), custom_call_target="tpu_custom_call" | custom-call | tf_op jit(solution)/shard_map/pallas_call | solution.py:332
  (19 shorter events, 1.3 us)
Async XLA Ops:
  1.6 2.5 %collective-permute-start = (bf16[768,384]{1,0:T(8,128)(2,1)S(1)}, bf16[768,384]{1,0:T(8,128)(2,1)S(1)}, u32[]{:S(2)}, u32[]{:S(2)}) collective-permute-start(bf16[768,384]{1,0:T(8,128)(2,1)S(1)} %get-tuple-element.31), channel_id=1, source_target_pairs={{0,1},{1,0},{2,3},{3,2},{4,5},{5,4},{6,7},{7,6},{8,9},{9,8},{10,11... | collective-permute-start | bytes 1769480 | tf_op jit(solution)/shard_map/ppermute | solution.py:28
  2.4 8.6 %collective-permute-start.2 = (bf16[384,384]{1,0:T(8,128)(2,1)S(1)}, bf16[384,384]{1,0:T(8,128)(2,1)S(1)}, u32[]{:S(2)}, u32[]{:S(2)}) collective-permute-start(bf16[384,384]{1,0:T(8,128)(2,1)S(1)} %get-tuple-element.33), channel_id=1, source_target_pairs={{0,2},{1,3},{2,0},{3,1},{4,6},{5,7},{6,4},{7,5},{8,10},{9,11},{10,... | collective-permute-start | bytes 884744 | tf_op jit(solution)/shard_map/ppermute | solution.py:28
  3.6 14.6 %collective-permute-start.3 = (bf16[384,384]{1,0:T(8,128)(2,1)S(1)}, bf16[384,384]{1,0:T(8,128)(2,1)S(1)}, u32[]{:S(2)}, u32[]{:S(2)}) collective-permute-start(bf16[384,384]{1,0:T(8,128)(2,1)S(1)} %get-tuple-element.34), channel_id=1, source_target_pairs={{0,3},{1,2},{2,1},{3,0},{4,7},{5,6},{6,5},{7,4},{8,11},{9,10},{10,... | collective-permute-start | bytes 884744 | tf_op jit(solution)/shard_map/ppermute | solution.py:28
  4.3 18.7 %collective-permute-start.4 = (bf16[784,384]{1,0:T(8,128)(2,1)S(1)}, bf16[784,384]{1,0:T(8,128)(2,1)S(1)}, u32[]{:S(2)}, u32[]{:S(2)}) collective-permute-start(bf16[784,384]{1,0:T(8,128)(2,1)S(1)} %shard_map.49.refs_4_), channel_id=1, source_target_pairs={{0,4},{4,0},{8,12},{12,8},{1,5},{5,1},{9,13},{13,9},{2,6},{6,2},{1... | collective-permute-start | bytes 1806344 | tf_op jit(solution)/shard_map/ppermute | solution.py:37
  4.3 18.6 %collective-permute-start.5 = (bf16[784,384]{1,0:T(8,128)(2,1)S(1)}, bf16[784,384]{1,0:T(8,128)(2,1)S(1)}, u32[]{:S(2)}, u32[]{:S(2)}) collective-permute-start(bf16[784,384]{1,0:T(8,128)(2,1)S(1)} %shard_map.49.refs_4_), channel_id=1, source_target_pairs={{4,8},{8,4},{5,9},{9,5},{6,10},{10,6},{7,11},{11,7},{20,24},{24,20... | collective-permute-start | bytes 1806344 | tf_op jit(solution)/shard_map/ppermute | solution.py:37
  9.2 16.1 %collective-permute-start.1 = (bf16[384,384]{1,0:T(8,128)(2,1)S(1)}, bf16[384,384]{1,0:T(8,128)(2,1)S(1)}, u32[]{:S(2)}, u32[]{:S(2)}) collective-permute-start(bf16[384,384]{1,0:T(8,128)(2,1)S(1)} %shard_map.47), channel_id=1, source_target_pairs={{0,2},{1,3},{2,0},{3,1},{4,6},{5,7},{6,4},{7,5},{8,10},{9,11},{10,... | collective-permute-start | bytes 884744 | tf_op jit(solution)/shard_map/ppermute | solution.py:28
  18.3 11.2 %collective-permute-start.6 = (bf16[768,256]{1,0:T(8,128)(2,1)S(1)}, bf16[768,256]{1,0:T(8,128)(2,1)S(1)}, u32[]{:S(2)}, u32[]{:S(2)}) collective-permute-start(bf16[768,256]{1,0:T(8,128)(2,1)S(1)} %shard_map.50), channel_id=1, source_target_pairs={{0,4},{4,0},{8,12},{12,8},{1,5},{5,1},{9,13},{13,9},{2,6},{6,2},{1... | collective-permute-start | bytes 1179656 | tf_op jit(solution)/shard_map/ppermute | solution.py:37
  18.3 14.1 %collective-permute-start.7 = (bf16[768,256]{1,0:T(8,128)(2,1)S(1)}, bf16[768,256]{1,0:T(8,128)(2,1)S(1)}, u32[]{:S(2)}, u32[]{:S(2)}) collective-permute-start(bf16[768,256]{1,0:T(8,128)(2,1)S(1)} %shard_map.50), channel_id=1, source_target_pairs={{4,8},{8,4},{5,9},{9,5},{6,10},{10,6},{7,11},{11,7},{20,24},{24,20... | collective-permute-start | bytes 1179656 | tf_op jit(solution)/shard_map/ppermute | solution.py:37
  22.9 12.9 %collective-permute-start.11 = (bf16[768,128]{1,0:T(8,128)(2,1)S(1)}, bf16[768,128]{1,0:T(8,128)(2,1)S(1)}, u32[]{:S(2)}, u32[]{:S(2)}) collective-permute-start(bf16[768,128]{1,0:T(8,128)(2,1)S(1)} %shard_map.48), channel_id=1, source_target_pairs={{0,4},{4,0},{8,12},{12,8},{1,5},{5,1},{9,13},{13,9},{2,6},{6,2},{1... | collective-permute-start | bytes 589832 | tf_op jit(solution)/shard_map/ppermute | solution.py:37
  23.0 13.6 %collective-permute-start.12 = (bf16[768,128]{1,0:T(8,128)(2,1)S(1)}, bf16[768,128]{1,0:T(8,128)(2,1)S(1)}, u32[]{:S(2)}, u32[]{:S(2)}) collective-permute-start(bf16[768,128]{1,0:T(8,128)(2,1)S(1)} %shard_map.48), channel_id=1, source_target_pairs={{4,8},{8,4},{5,9},{9,5},{6,10},{10,6},{7,11},{11,7},{20,24},{24,20... | collective-permute-start | bytes 589832 | tf_op jit(solution)/shard_map/ppermute | solution.py:37
  33.9 1.9 %collective-permute-start.8 = (bf16[192,256]{1,0:T(8,128)(2,1)S(1)}, bf16[192,256]{1,0:T(8,128)(2,1)S(1)}, u32[]{:S(2)}, u32[]{:S(2)}) collective-permute-start(bf16[192,256]{1,0:T(8,128)(2,1)S(1)} %get-tuple-element.43), channel_id=1, source_target_pairs={{0,1},{1,0},{2,3},{3,2},{4,5},{5,4},{6,7},{7,6},{8,9},{9,8},{10,11... | collective-permute-start | bytes 294920 | tf_op jit(solution)/shard_map/ppermute | solution.py:28
  34.2 5.5 %collective-permute-start.10 = (bf16[192,256]{1,0:T(8,128)(2,1)S(1)}, bf16[192,256]{1,0:T(8,128)(2,1)S(1)}, u32[]{:S(2)}, u32[]{:S(2)}) collective-permute-start(bf16[192,256]{1,0:T(8,128)(2,1)S(1)} %get-tuple-element.46), channel_id=1, source_target_pairs={{0,3},{1,2},{2,1},{3,0},{4,7},{5,6},{6,5},{7,4},{8,11},{9,10},{10,... | collective-permute-start | bytes 294920 | tf_op jit(solution)/shard_map/ppermute | solution.py:28
  35.6 5.3 %collective-permute-start.9 = (bf16[192,256]{1,0:T(8,128)(2,1)S(1)}, bf16[192,256]{1,0:T(8,128)(2,1)S(1)}, u32[]{:S(2)}, u32[]{:S(2)}) collective-permute-start(bf16[192,256]{1,0:T(8,128)(2,1)S(1)} %get-tuple-element.45), channel_id=1, source_target_pairs={{0,2},{1,3},{2,0},{3,1},{4,6},{5,7},{6,4},{7,5},{8,10},{9,11},{10,... | collective-permute-start | bytes 294920 | tf_op jit(solution)/shard_map/ppermute | solution.py:28
  37.5 3.4 %collective-permute-start.13 = (bf16[192,128]{1,0:T(8,128)(2,1)S(1)}, bf16[192,128]{1,0:T(8,128)(2,1)S(1)}, u32[]{:S(2)}, u32[]{:S(2)}) collective-permute-start(bf16[192,128]{1,0:T(8,128)(2,1)S(1)} %get-tuple-element.52), channel_id=1, source_target_pairs={{0,1},{1,0},{2,3},{3,2},{4,5},{5,4},{6,7},{7,6},{8,9},{9,8},{10,11... | collective-permute-start | bytes 147464 | tf_op jit(solution)/shard_map/ppermute | solution.py:28
  38.0 4.0 %collective-permute-start.14 = (bf16[192,128]{1,0:T(8,128)(2,1)S(1)}, bf16[192,128]{1,0:T(8,128)(2,1)S(1)}, u32[]{:S(2)}, u32[]{:S(2)}) collective-permute-start(bf16[192,128]{1,0:T(8,128)(2,1)S(1)} %get-tuple-element.53), channel_id=1, source_target_pairs={{0,2},{1,3},{2,0},{3,1},{4,6},{5,7},{6,4},{7,5},{8,10},{9,11},{10,... | collective-permute-start | bytes 147464 | tf_op jit(solution)/shard_map/ppermute | solution.py:28
  39.2 4.1 %collective-permute-start.15 = (bf16[192,128]{1,0:T(8,128)(2,1)S(1)}, bf16[192,128]{1,0:T(8,128)(2,1)S(1)}, u32[]{:S(2)}, u32[]{:S(2)}) collective-permute-start(bf16[192,128]{1,0:T(8,128)(2,1)S(1)} %get-tuple-element.54), channel_id=1, source_target_pairs={{0,3},{1,2},{2,1},{3,0},{4,7},{5,6},{6,5},{7,4},{8,11},{9,10},{10,... | collective-permute-start | bytes 147464 | tf_op jit(solution)/shard_map/ppermute | solution.py:28

commit v5 on v4

v5 whole, which is shorter than its diff:
```python
import functools
import math

import jax
import jax.numpy as jnp
from jax import lax
from jax.experimental import pallas as pl
from jax.experimental.pallas import tpu as pltpu
from jax.sharding import PartitionSpec as P

HEAD_DIM = 128
TILE_H = 8
TILE_W = 8
TIME_TILES = 4
COUNT_ROWS = 16
MASKED = -1e30
LARGEST_TOTAL = 2.0**100
SCALE = math.log2(math.e) / math.sqrt(HEAD_DIM)
VMEM_LIMIT = 24 * 2**20
FIRST_FLOPS = 2500000000
EARLY_FLOPS = 0


def in_vmem(count):
    return [pl.BlockSpec(memory_space=pltpu.VMEM)] * count


def swap_head(block, bit, devices):
    return lax.ppermute(block, "head", [(i, i ^ bit) for i in range(devices)])


def swap_pairs(block, phase, stride, length, devices):
    route = []
    for i in range(devices):
        place = i // stride % length
        if place % 2 == phase and place + 1 < length:
            route += [(i, i + stride), (i + stride, i)]
    return lax.ppermute(block, "tok", route)


def pack_body(devices, heads, counts_in, me_ref, q_ref, k_ref, v_ref, *rest):
    far = devices - 2
    own_ref, sibling_ref, passed_ref, own_q_ref = rest[:4]
    far_refs, last_refs = rest[4 : 4 + far], rest[4 + far : -3]
    counts_ref, count_sem, sems = rest[-3:]
    rows = k_ref.shape[0]
    me = me_ref[0]

    def lanes(bit, first=0, count=heads):
        start = ((me ^ bit) * heads + first) * HEAD_DIM
        return pl.ds(pl.multiple_of(start, HEAD_DIM), count * HEAD_DIM)

    count_copy = pltpu.make_async_copy(counts_in, counts_ref, count_sem)
    count_copy.start()
    jobs = [
        (k_ref.at[:, lanes(1)], sibling_ref.at[pl.ds(0, rows)]),
        (v_ref.at[:, lanes(1)], sibling_ref.at[pl.ds(rows, rows)]),
        (q_ref.at[:, lanes(1)], sibling_ref.at[pl.ds(2 * rows, rows)]),
    ]
    for bit, ref in enumerate(far_refs, 2):
        jobs += [
            (k_ref.at[:, lanes(bit, 0, heads - 1)], ref.at[pl.ds(0, rows)]),
            (v_ref.at[:, lanes(bit, 0, heads - 1)], ref.at[pl.ds(rows, rows)]),
        ]
    jobs += [
        (k_ref.at[:, lanes(0)], own_ref.at[pl.ds(0, rows)]),
        (v_ref.at[:, lanes(0)], own_ref.at[pl.ds(rows, rows)]),
        (q_ref.at[:, lanes(0)], own_q_ref),
    ]
    for bit in range(2, devices):
        pair = bit // 2 - 1
        ref, base = (passed_ref, pair * (heads + 2)) if bit % 2 else (last_refs[pair], 0)
        sources = [q_ref.at[:, lanes(bit, head, 1)] for head in range(heads)]
        sources += [k_ref.at[:, lanes(bit, heads - 1, 1)], v_ref.at[:, lanes(bit, heads - 1, 1)]]
        jobs += [
            (source, ref.at[pl.ds((base + i) * rows, rows)]) for i, source in enumerate(sources)
        ]
    copies = [pltpu.make_async_copy(src, dst, sems.at[i]) for i, (src, dst) in enumerate(jobs)]
    for copy in copies:
        copy.start()
    count_copy.wait()
    shape = (COUNT_ROWS, own_ref.shape[1])
    row = lax.broadcasted_iota(jnp.int32, shape, 0)
    filled = jnp.zeros(shape, jnp.float32)
    for tile in range(counts_ref.shape[0]):
        filled = jnp.where(row == tile, counts_ref[tile].astype(jnp.float32), filled)
    own_ref[pl.ds(2 * rows, COUNT_ROWS), :] = filled.astype(jnp.bfloat16)
    for copy in copies:
        copy.wait()


def pack(me, counts, query, key, value, devices):
    rows, width = query.shape
    part = width // devices
    heads = part // HEAD_DIM
    far = devices - 2
    shapes = [(2 * rows + COUNT_ROWS, part), (3 * rows, part)]
    shapes += [(far // 2 * (heads + 2) * rows, HEAD_DIM), (rows, part)]
    shapes += [(2 * rows, part - HEAD_DIM)] * far + [((heads + 2) * rows, HEAD_DIM)] * (far // 2)
    fields = [pltpu.with_memory_space_constraint(f, pltpu.HBM) for f in (query, key, value)]
    results = pl.pallas_call(
        functools.partial(pack_body, devices, heads),
        out_shape=[pltpu.VMEM(shape, jnp.bfloat16) for shape in shapes],
        in_specs=[pl.BlockSpec(memory_space=pltpu.HBM), pl.BlockSpec(memory_space=pltpu.SMEM)]
        + [pl.BlockSpec(memory_space=pltpu.HBM)] * 3,
        out_specs=in_vmem(len(shapes)),
        scratch_shapes=[
            pltpu.SMEM(counts.shape, jnp.int32),
            pltpu.SemaphoreType.DMA,
            pltpu.SemaphoreType.DMA((6 + far * (heads + 4),)),
        ],
        compiler_params=pltpu.CompilerParams(vmem_limit_bytes=VMEM_LIMIT),
        cost_estimate=pl.CostEstimate(flops=0, bytes_accessed=12 * query.size, transcendentals=0),
    )(pltpu.with_memory_space_constraint(counts, pltpu.HBM), me, *fields)
    return (*results[:4], results[4 : 4 + far], results[4 + far :])


def stack_body(jobs, after, *refs):
    blocks, out_ref, sems = refs[: -2 - after], refs[-2], refs[-1]
    copies, base = [], 0
    for i, (first, size) in enumerate(jobs):
        source = blocks[i].at[pl.ds(first, size)]
        copies.append(
            pltpu.make_async_copy(source, out_ref.at[pl.ds(base, size)], sems.at[i])
        )
        base += size
    for copy in copies:
        copy.start()
    for copy in copies:
        copy.wait()


def stack(blocks, spans, flops=0, after=()):
    width = blocks[0].shape[1]
    rows = sum(size for _, size in spans)
    return pl.pallas_call(
        functools.partial(stack_body, spans, len(after)),
        out_shape=pltpu.VMEM((rows, width), jnp.bfloat16),
        in_specs=in_vmem(len(blocks) + len(after)),
        out_specs=pl.BlockSpec(memory_space=pltpu.VMEM),
        scratch_shapes=[pltpu.SemaphoreType.DMA((len(blocks),))],
        compiler_params=pltpu.CompilerParams(vmem_limit_bytes=VMEM_LIMIT),
        cost_estimate=pl.CostEstimate(
            flops=flops, bytes_accessed=rows * width, transcendentals=0
        ),
    )(*blocks, *after)


def features(head):
    return pl.ds(aligned(head * HEAD_DIM, HEAD_DIM), HEAD_DIM)


def window_of(tile, tiles, groups):
    near = range(max(tile - 1, 0), min(tile + 2, tiles))
    return [(group, other) for other in near for group in range(len(groups))]


def aligned(start, unit):
    return start if isinstance(start, int) else pl.multiple_of(start, unit)


def gather(arrays, groups, window, start, tokens, head):
    blocks = []
    for group, other in window:
        for field in groups[group][1]:
            index, base, first = field[0]
            for segment in field[1:]:
                if head >= segment[2]:
                    index, base, first = segment
            rows = pl.ds(base + start + other * tokens, tokens)
            blocks.append(arrays[index][rows, features(head - first)])
    return jnp.concatenate(blocks, 0)


def asked_of(queries, layout, head, tile, tokens, rows):
    blocks = []
    for index, base, by_rows in layout:
        if by_rows:
            at = pl.ds(aligned(base + head * rows + tile * tokens, tokens), tokens)
            blocks.append(queries[index][at, :])
        else:
            blocks.append(queries[index][pl.ds(base + tile * tokens, tokens), features(head)])
    return jnp.concatenate(blocks, 0)


def counts_of(arrays, groups, rows):
    counts = [arrays[i][pl.ds(2 * rows, COUNT_ROWS), pl.ds(0, HEAD_DIM)] for i, _ in groups]
    return [count.astype(jnp.float32) for count in counts]


def bias_of(counts, groups, window, tokens):
    lane = lax.broadcasted_iota(jnp.int32, (1, HEAD_DIM), 1)
    row = (lane // TILE_W % TILE_H).astype(jnp.float32)
    parts = []
    for group, other in window:
        part = jnp.where(row < counts[group][other : other + 1], 0.0, MASKED)
        parts += [part] * (len(groups[group][1]) * tokens // HEAD_DIM)
    return jnp.concatenate(parts, 1)


def products(queries, keys):
    return lax.dot_general(
        queries, keys, (((1,), (1,)), ((), ())), preferred_element_type=jnp.float32
    )


def early_body(groups, operands, jobs, asked, tiles, tokens, *refs):
    rows = tiles * tokens
    queries, arrays = refs[:asked], refs[asked : asked + operands]
    outs = refs[asked + operands :]
    counts = counts_of(arrays, groups, rows)
    windows = [window_of(tile, tiles, groups) for tile in range(tiles)]
    biases = [bias_of(counts, groups, window, tokens) for window in windows]

    def scored(job, head, tile):
        scores = products(
            asked_of(queries, jobs[job][0], head, tile, tokens, rows),
            gather(arrays, groups, windows[tile], 0, tokens, head),
        )
        scores = scores + biases[tile]
        return scores, jnp.max(scores, axis=1, keepdims=True)

    steps = [
        (job, head, tile)
        for job, (_, heads) in enumerate(jobs)
        for head in heads
        for tile in range(tiles)
    ]
    ahead = scored(*steps[0])
    for i, (job, head, tile) in enumerate(steps):
        scores, largest = ahead
        if i + 1 < len(steps):
            ahead = scored(*steps[i + 1])
        weight = jnp.exp2((scores - largest) * SCALE).astype(jnp.bfloat16)
        values = gather(arrays, groups, windows[tile], rows, tokens, head)
        values = jnp.concatenate([values, jnp.ones_like(values)], 1)
        summed = jnp.dot(weight, values, preferred_element_type=jnp.float32)
        layout, heads = jobs[job]
        block = len(layout) * tokens
        place = pl.ds(((head - heads[0]) * tiles + tile) * block, block)
        max_ref, total_ref, sum_ref = outs[3 * job : 3 * job + 3]
        max_ref[place, :] = jnp.broadcast_to(largest, (block, HEAD_DIM))
        sum_ref[place, :] = summed[:, :HEAD_DIM]
        total_ref[place, :] = summed[:, HEAD_DIM:]


def late_body(groups, operands, layout, asked, tiles, tokens, heads, first, parts, *refs):
    rows = tiles * tokens
    queries, arrays = refs[:asked], refs[asked : asked + operands]
    left = refs[asked + operands : asked + operands + 3 * parts]
    outs = refs[asked + operands + 3 * parts :]
    counts = counts_of(arrays, groups, rows)
    windows = [window_of(tile, tiles, groups) for tile in range(tiles)]
    block = len(layout) * tokens

    def scored(head, tile):
        return products(
            asked_of(queries, layout, first + head, tile, tokens, rows),
            gather(arrays, groups, windows[tile], 0, tokens, head),
        )

    def early(head, tile):
        share = block // parts
        at = pl.ds(aligned((head * tiles + tile) * share, share), share)
        return [jnp.concatenate([ref[at, :] for ref in left[which::3]], 0) for which in range(3)]

    def write(head, tile, result):
        for frame in range(len(layout)):
            outs[frame][pl.ds(tile * tokens, tokens), features(head)] = result[
                frame * tokens : (frame + 1) * tokens
            ]

    token = lax.broadcasted_iota(jnp.int32, (tokens, HEAD_DIM), 0)
    row = (token // TILE_W % TILE_H).astype(jnp.float32)
    real = [
        [jnp.where(row < count[n : n + 1], 1.0, 0.0).astype(jnp.bfloat16) for n in range(tiles)]
        for count in counts
    ]
    worst = jnp.zeros((block, HEAD_DIM), jnp.float32)
    for head in range(heads):
        for tile, window in enumerate(windows):
            largest, total, summed = early(head, tile)
            scores = scored(head, tile)
            largest = jnp.concatenate([largest] * (scores.shape[1] // HEAD_DIM), 1)
            weight = jnp.exp2((scores - largest) * SCALE).astype(jnp.bfloat16)
            kept = jnp.concatenate(
                [real[group][n] for group, n in window for _ in groups[group][1]], 0
            )
            values = gather(arrays, groups, window, rows, tokens, head) * kept
            added = jnp.dot(
                weight,
                jnp.concatenate([values, kept], 1),
                preferred_element_type=jnp.float32,
            )
            total = total + added[:, HEAD_DIM:]
            worst = jnp.where(total < LARGEST_TOTAL, worst, 1.0)
            result = (summed + added[:, :HEAD_DIM]) / total
            write(head, tile, result.astype(jnp.bfloat16))

    @pl.when(jnp.max(worst) > 0.0)
    def _():
        def one_head(head, _):
            for tile, window in enumerate(windows):
                before, total, summed = early(head, tile)
                scores = scored(head, tile) + bias_of(counts, groups, window, tokens)
                largest = jnp.maximum(before[:, :1], jnp.max(scores, axis=1, keepdims=True))
                shrink = jnp.exp2((before - largest) * SCALE)
                weight = jnp.exp2((scores - largest) * SCALE)
                total = jnp.sum(weight, axis=1, keepdims=True) + total * shrink
                added = jnp.dot(
                    weight.astype(jnp.bfloat16),
                    gather(arrays, groups, window, rows, tokens, head),
                    preferred_element_type=jnp.float32,
                )
                result = (added + summed * shrink) / total
                write(head, tile, result.astype(jnp.bfloat16))
            return 0

        lax.fori_loop(0, heads, one_head, 0)


def attend(kernel, operands, outs, flops=0):
    return pl.pallas_call(
        kernel,
        out_shape=outs,
        in_specs=in_vmem(len(operands)),
        out_specs=in_vmem(len(outs)),
        compiler_params=pltpu.CompilerParams(vmem_limit_bytes=VMEM_LIMIT),
        cost_estimate=pl.CostEstimate(flops=flops, bytes_accessed=0, transcendentals=0),
    )(*operands)


def attend_early(queries, jobs, arrays, groups, tiles, tokens):
    outs = [
        pltpu.VMEM((len(heads) * tiles * len(layout) * tokens, HEAD_DIM), jnp.float32)
        for layout, heads in jobs
        for _ in range(3)
    ]
    kernel = functools.partial(
        early_body, groups, len(arrays), jobs, len(queries), tiles, tokens
    )
    return attend(kernel, [*queries, *arrays], outs, EARLY_FLOPS)


def attend_late(queries, layout, arrays, groups, tiles, tokens, heads, first, left):
    outs = [pltpu.VMEM((tiles * tokens, heads * HEAD_DIM), jnp.bfloat16)] * len(layout)
    kernel = functools.partial(
        late_body, groups, len(arrays), layout, len(queries), tiles, tokens, heads, first, len(left) // 3
    )
    return attend(kernel, [*queries, *arrays, *left], outs)


def join_body(jobs, part, me_ref, *rest):
    out_ref, sems = rest[-2:]
    me = me_ref[0]
    copies = []
    for i, (bit, base) in enumerate(jobs):
        lanes = pl.ds(pl.multiple_of((me ^ bit) * part + base, HEAD_DIM), rest[i].shape[1])
        copies.append(pltpu.make_async_copy(rest[i], out_ref.at[:, lanes], sems.at[i]))
    for copy in copies:
        copy.start()
    for copy in copies:
        copy.wait()


def join(me, pieces, rows, part, devices):
    jobs = [piece[:2] for piece in pieces]
    return pl.pallas_call(
        functools.partial(join_body, jobs, part),
        out_shape=jax.ShapeDtypeStruct((rows, devices * part), jnp.bfloat16),
        in_specs=[pl.BlockSpec(memory_space=pltpu.SMEM)] + in_vmem(len(pieces)),
        out_specs=pl.BlockSpec(memory_space=pl.ANY),
        scratch_shapes=[pltpu.SemaphoreType.DMA((len(pieces),))],
        compiler_params=pltpu.CompilerParams(vmem_limit_bytes=VMEM_LIMIT),
    )(me, *(piece[2] for piece in pieces))


def body(query, key, value, valid_rows):
    devices = lax.axis_size("head")
    columns = lax.axis_size("tok")
    height = columns // TIME_TILES
    tiles, tokens, width = query.shape
    heads = width // HEAD_DIM // devices
    me = lax.axis_index("head").astype(jnp.int32).reshape(1)
    flat = [field.reshape(tiles * tokens, width) for field in (query, key, value)]
    own, sibling, passed, own_query, far, last = pack(me, valid_rows, *flat, devices)
    rows = tiles * tokens

    def by_height(block):
        if height == 1:
            return [block]
        return [block] + [swap_pairs(block, phase, 1, height, columns) for phase in (0, 1)]

    def by_time(blocks):
        return [
            swap_pairs(b, phase, height, TIME_TILES, columns) for phase in (0, 1) for b in blocks
        ]

    sibling = swap_head(sibling, 1, devices)
    passed = swap_head(passed, 1, devices)
    far = [swap_head(b, bit, devices) for bit, b in enumerate(far, 2)]
    near = by_height(stack([own, sibling], [(0, own.shape[0]), (0, 2 * rows)]))
    near = near + by_time(near)

    unit = (heads + 2) * rows
    last = [
        swap_head(stack([b, passed], [(0, unit), (i * unit, unit)]), 2 * i + 2, devices)
        for i, b in enumerate(last)
    ]
    queries = [own_query, sibling, *last]
    layout = [(0, 0, False), (1, 2 * rows, False)]
    layout += [(2 + bit // 2, bit % 2 * unit, True) for bit in range(devices - 2)]

    ends = [(bit // 2, bit % 2 * unit + heads * rows) for bit in range(devices - 2)]
    def sent(block):
        block = by_height(block)
        return block[1:] + by_time(block)

    first_heads, last_head = tuple(range(heads - 1)), (heads - 1,)
    across = sent(stack(far, [(0, 2 * rows)] * len(far), FIRST_FLOPS))
    near_groups = [(i, [[(i, 0, 0)], [(i, own.shape[0], 0)]]) for i in range(len(near))]
    own_fields = [[(len(near) + bit, 0, 0)] for bit in range(len(far))]
    groups = [(0, near_groups[0][1] + own_fields), *near_groups[1:]]
    close = attend_early(
        queries[:2], [(layout[:2], first_heads)], near + far, groups, tiles, tokens
    )

    spans = [(base, 2 * rows) for _, base in ends]
    across_last = sent(stack([last[i] for i, _ in ends], spans, after=close[:1]))
    for field, (i, base) in zip(own_fields, ends):
        field.append((len(near) + len(far) + i, base, heads - 1))
    jobs = [(layout[2:], first_heads), (layout, last_head)]
    groups = [(0, near_groups[0][1] + own_fields), *near_groups[1:]]
    left = attend_early(queries, jobs, near + far + last, groups, tiles, tokens)
    left = [[*close, *left[:3]], left[3:]]

    pieces = []
    for others, heads_now in ((across, first_heads), (across_last, last_head)):
        first = heads_now[0]
        groups = [
            (i, [[(len(others) + i, 2 * rows * bit, 0)] for bit in range(devices - 2)])
            for i in range(len(others))
        ]
        results = attend_late(
            queries,
            layout,
            near[1:] + others,
            groups,
            tiles,
            tokens,
            len(heads_now),
            first,
            left[len(pieces) > 0],
        )
        results = list(results)
        results[1] = swap_head(results[1], 1, devices)
        if not pieces:
            results[1], *left[1] = lax.optimization_barrier((results[1], *left[1]))
        pieces += [
            (bit, first * HEAD_DIM, swap_head(b, bit, devices) if bit > 1 else b)
            for bit, b in enumerate(results)
        ]
    return join(me, pieces, rows, heads * HEAD_DIM, devices).reshape(tiles, tokens, width)


def solution(mesh):
    placed = (
        P(("clips", "tok"), "head", None),
        P(("clips", "tok"), "head", None),
        P(("clips", "tok"), "head", None),
        P(("clips", "tok")),
    )
    return jax.shard_map(
        body,
        mesh=mesh,
        in_specs=placed,
        out_specs=P(("clips", "tok"), "head", None),
        check_vma=False,
    )
```

time: 44.5 us -> 44.2 us (level)
  waiting for transfers between devices: 15.2 us -> 11.2 us
  starting transfers between devices: 19.3 us -> 21.7 us
  Pallas kernels: 9.47 us -> 10.6 us
    ppermute x10 -> x11, waiting for transfers between devices: 11.3 us -> 7.05 us  [swap_head(): return lax.ppermute(block, 'head', [(i, i ^ bit) for i in range(devices)])]
    ppermute x10 -> x11, starting transfers between devices: 7.86 us -> 9.44 us  [swap_head(): return lax.ppermute(block, 'head', [(i, i ^ bit) for i in range(devices)])]
    pallas_call x5, Pallas kernels: 2.3 us -> 3.21 us  [the longest x1 1.63 us: pack(): pl.pallas_call(functools.partial(pack_body, devices, heads), out_shape=[p...]
    ppermute x6, starting transfers between devices: 11.4 us -> 12.3 us  [swap_pairs(): return lax.ppermute(block, 'tok', route)]
    pallas_call x3 -> x4, Pallas kernels: 6.3 us -> 6.56 us  [attend(): pl.pallas_call(kernel, out_shape=outs, in_specs=in_vmem(len(operands)), o...]
  transfers between devices with their start and end apart: 16 -> 17, of which waited for: 8 -> 7; matrix products, arithmetic and copies ran while one was open for 0% -> 0% of each run, Pallas kernels for 16% -> 19%
where the time goes in v5:
time: 44.2 us; the launch traced here: 43.7 us
  starting transfers between devices  21.7 us (49%)
  waiting for transfers between devices  11.2 us (25%)
  Pallas kernels  10.6 us (24%)
    ppermute x6, starting transfers between devices, swap_pairs(): return lax.ppermute(block, 'tok', route)  12.3 us
    ppermute x11, starting transfers between devices, swap_head(): return lax.ppermute(block, 'head', [(i, i ^ bit) for i in range(devices)])  9.44 us
    ppermute x11, waiting for transfers between devices, swap_head(): return lax.ppermute(block, 'head', [(i, i ^ bit) for i in range(devices)])  7.05 us
    pallas_call x4, Pallas kernels, attend(): pl.pallas_call(kernel, out_shape=outs, in_specs=in_vmem(len(operands)), o...  6.56 us
    ppermute x6, waiting for transfers between devices, swap_pairs(): return lax.ppermute(block, 'tok', route)  4.18 us
    pallas_call x1, Pallas kernels, pack(): pl.pallas_call(functools.partial(pack_body, devices, heads), out_shape=[p...  1.63 us
    pallas_call x4, Pallas kernels, stack(): pl.pallas_call(functools.partial(stack_body, spans, len(after)), out_shap...  1.58 us
  transfers between devices with their start and end apart: 17, of which 7 were waited for; matrix products, arithmetic and copies ran while one was open for 0% of the time, Pallas kernels for 19%

profile of v5, /device:TPU:9, one launch (start us, length us, event | category | flops | bytes accessed | tf_op | source)
XLA Modules:
  0.0 43.7 jit_solution(16190618689264423979)
XLA Ops:
  0.0 1.6 %shard_map.46 = (bf16[400,384]{1,0:T(8,128)(2,1)S(1)}, bf16[576,384]{1,0:T(8,128)(2,1)S(1)}, bf16[960,128]{1,0:T(8,128)(2,1)S(1)}, bf16[192,384]{1,0:T(8,128)(2,...) custom-call(s32[3]{0:T(128)} %counts_in.1, s32[1]{0:T(128)} %bitcast.me_ref, ...), custom_call_target="tpu_custom_call" | custom-call | bytes 3538944 | tf_op jit(solution)/shard_map/pallas_call | solution.py:101
  1.6 0.7 %collective-permute-start = (bf16[576,384]{1,0:T(8,128)(2,1)S(1)}, bf16[576,384]{1,0:T(8,128)(2,1)S(1)}, u32[]{:S(2)}, u32[]{:S(2)}) collective-permute-start(bf16[576,384]{1,0:T(8,128)(2,1)S(1)} %get-tuple-element.34), channel_id=1, source_target_pairs={{0,1},{1,0},{2,3},{3,2},{4,5},{5,4},{6,7},{7,6},{8,9},{9,8},{10,11... | collective-permute-start | bytes 1327112 | tf_op jit(solution)/shard_map/ppermute | solution.py:29
  2.5 1.2 %collective-permute-start.5 = (bf16[384,256]{1,0:T(8,128)(2,1)S(1)}, bf16[384,256]{1,0:T(8,128)(2,1)S(1)}, u32[]{:S(2)}, u32[]{:S(2)}) collective-permute-start(bf16[384,256]{1,0:T(8,128)(2,1)S(1)} %get-tuple-element.38), channel_id=1, source_target_pairs={{0,2},{1,3},{2,0},{3,1},{4,6},{5,7},{6,4},{7,5},{8,10},{9,11},{10,... | collective-permute-start | bytes 589832 | tf_op jit(solution)/shard_map/ppermute | solution.py:29
  3.7 0.9 %collective-permute-start.6 = (bf16[384,256]{1,0:T(8,128)(2,1)S(1)}, bf16[384,256]{1,0:T(8,128)(2,1)S(1)}, u32[]{:S(2)}, u32[]{:S(2)}) collective-permute-start(bf16[384,256]{1,0:T(8,128)(2,1)S(1)} %get-tuple-element.39), channel_id=1, source_target_pairs={{0,3},{1,2},{2,1},{3,0},{4,7},{5,6},{6,5},{7,4},{8,11},{9,10},{10,... | collective-permute-start | bytes 589832 | tf_op jit(solution)/shard_map/ppermute | solution.py:29
  4.8 4.5 %collective-permute-start.4 = (bf16[784,384]{1,0:T(8,128)(2,1)S(1)}, bf16[784,384]{1,0:T(8,128)(2,1)S(1)}, u32[]{:S(2)}, u32[]{:S(2)}) collective-permute-start(bf16[784,384]{1,0:T(8,128)(2,1)S(1)} %shard_map.48.refs_2_.refs_3_), channel_id=1, source_target_pairs={{4,8},{8,4},{5,9},{9,5},{6,10},{10,6},{7,11},{11,7},{20,24},{24,20... | collective-permute-start | bytes 1806344 | tf_op jit(solution)/shard_map/ppermute | solution.py:38
  9.3 0.7 %shard_map.47 = bf16[1920,128]{1,0:T(8,128)(2,1)S(1)} custom-call(bf16[960,128]{1,0:T(8,128)(2,1)S(1)} %get-tuple-element.35.refs_0_, bf16[960,128]{1,0:T(8,128)(2,1)S(1)} %collective-permute-done.1.refs_1_), custom_call_target="tpu_custom_call" | custom-call | bytes 245760 | tf_op jit(solution)/shard_map/pallas_call | solution.py:136
  9.9 1.3 %collective-permute-start.2 = (bf16[1920,128]{1,0:T(8,128)(2,1)S(1)}, bf16[1920,128]{1,0:T(8,128)(2,1)S(1)}, u32[]{:S(2)}, u32[]{:S(2)}) collective-permute-start(bf16[1920,128]{1,0:T(8,128)(2,1)S(1)} %shard_map.47), channel_id=1, source_target_pairs={{0,2},{1,3},{2,0},{3,1},{4,6},{5,7},{6,4},{7,5},{8,10},{9,11},{10,... | collective-permute-start | bytes 1474568 | tf_op jit(solution)/shard_map/ppermute | solution.py:29
  11.2 3.2 %collective-permute-done.6.refs_1_.refs_6_.refs_7_ = bf16[384,256]{1,0:T(8,128)(2,1)S(1)} collective-permute-done((bf16[384,256]{1,0:T(8,128)(2,1)S(1)}, bf16[384,256]{1,0:T(8,128)(2,1)S(1)}, u32[]{:S(2)}, u32[]{:S(2)}) %collective-permute-start.6) | collective-permute-done | bytes 196640 | tf_op jit(solution)/shard_map/ppermute | solution.py:29
  15.0 4.5 %collective-permute-start.8 = (bf16[768,256]{1,0:T(8,128)(2,1)S(1)}, bf16[768,256]{1,0:T(8,128)(2,1)S(1)}, u32[]{:S(2)}, u32[]{:S(2)}) collective-permute-start(bf16[768,256]{1,0:T(8,128)(2,1)S(1)} %shard_map.49), channel_id=1, source_target_pairs={{4,8},{8,4},{5,9},{9,5},{6,10},{10,6},{7,11},{11,7},{20,24},{24,20... | collective-permute-start | bytes 1179656 | tf_op jit(solution)/shard_map/ppermute | solution.py:38
  19.5 0.5 %collective-permute-done.3.refs_3_.refs_4_ = bf16[784,384]{1,0:T(8,128)(2,1)S(1)} collective-permute-done((bf16[784,384]{1,0:T(8,128)(2,1)S(1)}, bf16[784,384]{1,0:T(8,128)(2,1)S(1)}, u32[]{:S(2)}, u32[]{:S(2)}) %collective-permute-start.3) | collective-permute-done | bytes 602144 | tf_op jit(solution)/shard_map/ppermute | solution.py:38
  20.0 3.0 %collective-permute-done.4.refs_4_.refs_5_ = bf16[784,384]{1,0:T(8,128)(2,1)S(1)} collective-permute-done((bf16[784,384]{1,0:T(8,128)(2,1)S(1)}, bf16[784,384]{1,0:T(8,128)(2,1)S(1)}, u32[]{:S(2)}, u32[]{:S(2)}) %collective-permute-start.4) | collective-permute-done | bytes 602144 | tf_op jit(solution)/shard_map/ppermute | solution.py:38
  23.1 1.5 %shard_map.50 = (f32[768,128]{1,0:T(8,128)S(1)}, f32[768,128]{1,0:T(8,128)S(1)}, f32[768,128]{1,0:T(8,128)S(1)}) custom-call(bf16[192,384]{1,0:T(8,128)(2,1)S(1)} %get-tuple-element.33.refs_0_, bf16[576,384]{1,0:T(8,128)(2,1)S(1)} %collective-permute-done.refs_1_, bf16[784,384]{1,0:T(8,128)(2,1)S(1)} %shard_map.48.refs_2_.refs_3_, ...), custom_call_target="tpu_custom_call" | custom-call | tf_op jit(solution)/shard_map/pallas_call | solution.py:323
  25.0 3.1 %collective-permute-start.13 = (bf16[768,128]{1,0:T(8,128)(2,1)S(1)}, bf16[768,128]{1,0:T(8,128)(2,1)S(1)}, u32[]{:S(2)}, u32[]{:S(2)}) collective-permute-start(bf16[768,128]{1,0:T(8,128)(2,1)S(1)} %shard_map.53), channel_id=1, source_target_pairs={{4,8},{8,4},{5,9},{9,5},{6,10},{10,6},{7,11},{11,7},{20,24},{24,20... | collective-permute-start | bytes 589832 | tf_op jit(solution)/shard_map/ppermute | solution.py:38
  28.1 2.7 %shard_map.51 = (f32[768,128]{1,0:T(8,128)S(1)}, f32[768,128]{1,0:T(8,128)S(1)}, f32[768,128]{1,0:T(8,128)S(1)}, f32[768,128]{1,0:T(8,128)S(1)}, f32[768,128]{1,0:T(8,128)S(1)}, /*index=5*/f32[768,128]{1,0:T(8,128)S(1)}) custom-call(bf16[192,384]{1,0:T(8,128)(2,1)S(1)} %get-tuple-element.33.refs_0_, bf16[576,384]{1,0:T(8,128)(2,1)S(1)} %collective-permute-done.refs_1_, ...), custom_call_target="tpu_custom_call" | custom-call | tf_op jit(solution)/shard_map/pallas_call | solution.py:323
  30.8 0.6 %collective-permute-done.8.refs_6_ = bf16[768,256]{1,0:T(8,128)(2,1)S(1)} collective-permute-done((bf16[768,256]{1,0:T(8,128)(2,1)S(1)}, bf16[768,256]{1,0:T(8,128)(2,1)S(1)}, u32[]{:S(2)}, u32[]{:S(2)}) %collective-permute-start.8) | collective-permute-done | bytes 393248 | tf_op jit(solution)/shard_map/ppermute | solution.py:38
  31.5 1.4 %shard_map.52 = (bf16[192,256]{1,0:T(8,128)(2,1)S(1)}, bf16[192,256]{1,0:T(8,128)(2,1)S(1)}, bf16[192,256]{1,0:T(8,128)(2,1)S(1)}, bf16[192,256]{1,0:T(8,128)(2,1)S(1)}) custom-call(bf16[192,384]{1,0:T(8,128)(2,1)S(1)} %get-tuple-element.33.refs_0_, bf16[576,384]{1,0:T(8,128)(2,1)S(1)} %collective-permute-done.refs_1_, ...), custom_call_target="tpu_custom_call" | custom-call | tf_op jit(solution)/shard_map/pallas_call | solution.py:323
  32.9 1.2 %collective-permute-start.9 = (bf16[192,256]{1,0:T(8,128)(2,1)S(1)}, bf16[192,256]{1,0:T(8,128)(2,1)S(1)}, u32[]{:S(2)}, u32[]{:S(2)}) collective-permute-start(bf16[192,256]{1,0:T(8,128)(2,1)S(1)} %get-tuple-element.47), channel_id=1, source_target_pairs={{0,1},{1,0},{2,3},{3,2},{4,5},{5,4},{6,7},{7,6},{8,9},{9,8},{10,11... | collective-permute-start | bytes 294920 | tf_op jit(solution)/shard_map/ppermute | solution.py:29
  34.1 1.2 %collective-permute-start.10 = (bf16[192,256]{1,0:T(8,128)(2,1)S(1)}, bf16[192,256]{1,0:T(8,128)(2,1)S(1)}, u32[]{:S(2)}, u32[]{:S(2)}) collective-permute-start(bf16[192,256]{1,0:T(8,128)(2,1)S(1)} %get-tuple-element.52), channel_id=1, source_target_pairs={{0,2},{1,3},{2,0},{3,1},{4,6},{5,7},{6,4},{7,5},{8,10},{9,11},{10,... | collective-permute-start | bytes 294920 | tf_op jit(solution)/shard_map/ppermute | solution.py:29
  35.9 0.9 %shard_map.54 = (bf16[192,128]{1,0:T(8,128)(2,1)S(1)}, bf16[192,128]{1,0:T(8,128)(2,1)S(1)}, bf16[192,128]{1,0:T(8,128)(2,1)S(1)}, bf16[192,128]{1,0:T(8,128)(2,1)S(1)}) custom-call(bf16[192,384]{1,0:T(8,128)(2,1)S(1)} %get-tuple-element.33.refs_0_, bf16[576,384]{1,0:T(8,128)(2,1)S(1)} %collective-permute-done.refs_1_, ...), custom_call_target="tpu_custom_call" | custom-call | tf_op jit(solution)/shard_map/pallas_call | solution.py:323
  36.8 0.6 %collective-permute-start.14 = (bf16[192,128]{1,0:T(8,128)(2,1)S(1)}, bf16[192,128]{1,0:T(8,128)(2,1)S(1)}, u32[]{:S(2)}, u32[]{:S(2)}) collective-permute-start(bf16[192,128]{1,0:T(8,128)(2,1)S(1)} %get-tuple-element.58), channel_id=1, source_target_pairs={{0,1},{1,0},{2,3},{3,2},{4,5},{5,4},{6,7},{7,6},{8,9},{9,8},{10,11... | collective-permute-start | bytes 147464 | tf_op jit(solution)/shard_map/ppermute | solution.py:29
  37.4 1.2 %collective-permute-start.15 = (bf16[192,128]{1,0:T(8,128)(2,1)S(1)}, bf16[192,128]{1,0:T(8,128)(2,1)S(1)}, u32[]{:S(2)}, u32[]{:S(2)}) collective-permute-start(bf16[192,128]{1,0:T(8,128)(2,1)S(1)} %get-tuple-element.59), channel_id=1, source_target_pairs={{0,2},{1,3},{2,0},{3,1},{4,6},{5,7},{6,4},{7,5},{8,10},{9,11},{10,... | collective-permute-start | bytes 147464 | tf_op jit(solution)/shard_map/ppermute | solution.py:29
  39.1 2.1 %collective-permute-done.11.rest_3_ = bf16[192,256]{1,0:T(8,128)(2,1)S(1)} collective-permute-done((bf16[192,256]{1,0:T(8,128)(2,1)S(1)}, bf16[192,256]{1,0:T(8,128)(2,1)S(1)}, u32[]{:S(2)}, u32[]{:S(2)}) %collective-permute-start.11) | collective-permute-done | bytes 98336 | tf_op jit(solution)/shard_map/ppermute | solution.py:29
  41.7 1.2 %collective-permute-done.16.rest_7_ = bf16[192,128]{1,0:T(8,128)(2,1)S(1)} collective-permute-done((bf16[192,128]{1,0:T(8,128)(2,1)S(1)}, bf16[192,128]{1,0:T(8,128)(2,1)S(1)}, u32[]{:S(2)}, u32[]{:S(2)}) %collective-permute-start.16) | collective-permute-done | bytes 49184 | tf_op jit(solution)/shard_map/ppermute | solution.py:29
  42.9 0.9 %shard_map.55 = bf16[192,1536]{1,0:T(8,128)(2,1)} custom-call(s32[1]{0:T(128)} %bitcast.me_ref, bf16[192,256]{1,0:T(8,128)(2,1)S(1)} %get-tuple-element.46.rest_0_, bf16[192,256]{1,0:T(8,128)(2,1)S(1)} %collective-permute-done.9.rest_1_, bf16[192,256]{1,0:T(8,128)(2,1)S(1)} %collective-permute-done.10.rest_2_, ...), custom_call_target="tpu_custom_call" | custom-call | tf_op jit(solution)/shard_map/pallas_call | solution.py:368
  (20 shorter events, 2.7 us)
Async XLA Ops:
  1.6 2.9 %collective-permute-start = (bf16[576,384]{1,0:T(8,128)(2,1)S(1)}, bf16[576,384]{1,0:T(8,128)(2,1)S(1)}, u32[]{:S(2)}, u32[]{:S(2)}) collective-permute-start(bf16[576,384]{1,0:T(8,128)(2,1)S(1)} %get-tuple-element.34), channel_id=1, source_target_pairs={{0,1},{1,0},{2,3},{3,2},{4,5},{5,4},{6,7},{7,6},{8,9},{9,8},{10,11... | collective-permute-start | bytes 1327112 | tf_op jit(solution)/shard_map/ppermute | solution.py:29
  2.4 6.9 %collective-permute-start.1 = (bf16[960,128]{1,0:T(8,128)(2,1)S(1)}, bf16[960,128]{1,0:T(8,128)(2,1)S(1)}, u32[]{:S(2)}, u32[]{:S(2)}) collective-permute-start(bf16[960,128]{1,0:T(8,128)(2,1)S(1)} %get-tuple-element.36), channel_id=1, source_target_pairs={{0,1},{1,0},{2,3},{3,2},{4,5},{5,4},{6,7},{7,6},{8,9},{9,8},{10,11... | collective-permute-start | bytes 737288 | tf_op jit(solution)/shard_map/ppermute | solution.py:29
  2.5 8.8 %collective-permute-start.5 = (bf16[384,256]{1,0:T(8,128)(2,1)S(1)}, bf16[384,256]{1,0:T(8,128)(2,1)S(1)}, u32[]{:S(2)}, u32[]{:S(2)}) collective-permute-start(bf16[384,256]{1,0:T(8,128)(2,1)S(1)} %get-tuple-element.38), channel_id=1, source_target_pairs={{0,2},{1,3},{2,0},{3,1},{4,6},{5,7},{6,4},{7,5},{8,10},{9,11},{10,... | collective-permute-start | bytes 589832 | tf_op jit(solution)/shard_map/ppermute | solution.py:29
  3.7 10.8 %collective-permute-start.6 = (bf16[384,256]{1,0:T(8,128)(2,1)S(1)}, bf16[384,256]{1,0:T(8,128)(2,1)S(1)}, u32[]{:S(2)}, u32[]{:S(2)}) collective-permute-start(bf16[384,256]{1,0:T(8,128)(2,1)S(1)} %get-tuple-element.39), channel_id=1, source_target_pairs={{0,3},{1,2},{2,1},{3,0},{4,7},{5,6},{6,5},{7,4},{8,11},{9,10},{10,... | collective-permute-start | bytes 589832 | tf_op jit(solution)/shard_map/ppermute | solution.py:29
  4.7 15.4 %collective-permute-start.3 = (bf16[784,384]{1,0:T(8,128)(2,1)S(1)}, bf16[784,384]{1,0:T(8,128)(2,1)S(1)}, u32[]{:S(2)}, u32[]{:S(2)}) collective-permute-start(bf16[784,384]{1,0:T(8,128)(2,1)S(1)} %shard_map.48.refs_2_.refs_3_), channel_id=1, source_target_pairs={{0,4},{4,0},{8,12},{12,8},{1,5},{5,1},{9,13},{13,9},{2,6},{6,2},{1... | collective-permute-start | bytes 1806344 | tf_op jit(solution)/shard_map/ppermute | solution.py:38
  4.8 18.3 %collective-permute-start.4 = (bf16[784,384]{1,0:T(8,128)(2,1)S(1)}, bf16[784,384]{1,0:T(8,128)(2,1)S(1)}, u32[]{:S(2)}, u32[]{:S(2)}) collective-permute-start(bf16[784,384]{1,0:T(8,128)(2,1)S(1)} %shard_map.48.refs_2_.refs_3_), channel_id=1, source_target_pairs={{4,8},{8,4},{5,9},{9,5},{6,10},{10,6},{7,11},{11,7},{20,24},{24,20... | collective-permute-start | bytes 1806344 | tf_op jit(solution)/shard_map/ppermute | solution.py:38
  9.9 14.7 %collective-permute-start.2 = (bf16[1920,128]{1,0:T(8,128)(2,1)S(1)}, bf16[1920,128]{1,0:T(8,128)(2,1)S(1)}, u32[]{:S(2)}, u32[]{:S(2)}) collective-permute-start(bf16[1920,128]{1,0:T(8,128)(2,1)S(1)} %shard_map.47), channel_id=1, source_target_pairs={{0,2},{1,3},{2,0},{3,1},{4,6},{5,7},{6,4},{7,5},{8,10},{9,11},{10,... | collective-permute-start | bytes 1474568 | tf_op jit(solution)/shard_map/ppermute | solution.py:29
  15.0 15.9 %collective-permute-start.7 = (bf16[768,256]{1,0:T(8,128)(2,1)S(1)}, bf16[768,256]{1,0:T(8,128)(2,1)S(1)}, u32[]{:S(2)}, u32[]{:S(2)}) collective-permute-start(bf16[768,256]{1,0:T(8,128)(2,1)S(1)} %shard_map.49), channel_id=1, source_target_pairs={{0,4},{4,0},{8,12},{12,8},{1,5},{5,1},{9,13},{13,9},{2,6},{6,2},{1... | collective-permute-start | bytes 1179656 | tf_op jit(solution)/shard_map/ppermute | solution.py:38
  15.0 16.4 %collective-permute-start.8 = (bf16[768,256]{1,0:T(8,128)(2,1)S(1)}, bf16[768,256]{1,0:T(8,128)(2,1)S(1)}, u32[]{:S(2)}, u32[]{:S(2)}) collective-permute-start(bf16[768,256]{1,0:T(8,128)(2,1)S(1)} %shard_map.49), channel_id=1, source_target_pairs={{4,8},{8,4},{5,9},{9,5},{6,10},{10,6},{7,11},{11,7},{20,24},{24,20... | collective-permute-start | bytes 1179656 | tf_op jit(solution)/shard_map/ppermute | solution.py:38
  24.9 11.0 %collective-permute-start.12 = (bf16[768,128]{1,0:T(8,128)(2,1)S(1)}, bf16[768,128]{1,0:T(8,128)(2,1)S(1)}, u32[]{:S(2)}, u32[]{:S(2)}) collective-permute-start(bf16[768,128]{1,0:T(8,128)(2,1)S(1)} %shard_map.53), channel_id=1, source_target_pairs={{0,4},{4,0},{8,12},{12,8},{1,5},{5,1},{9,13},{13,9},{2,6},{6,2},{1... | collective-permute-start | bytes 589832 | tf_op jit(solution)/shard_map/ppermute | solution.py:38
  25.0 10.9 %collective-permute-start.13 = (bf16[768,128]{1,0:T(8,128)(2,1)S(1)}, bf16[768,128]{1,0:T(8,128)(2,1)S(1)}, u32[]{:S(2)}, u32[]{:S(2)}) collective-permute-start(bf16[768,128]{1,0:T(8,128)(2,1)S(1)} %shard_map.53), channel_id=1, source_target_pairs={{4,8},{8,4},{5,9},{9,5},{6,10},{10,6},{7,11},{11,7},{20,24},{24,20... | collective-permute-start | bytes 589832 | tf_op jit(solution)/shard_map/ppermute | solution.py:38
  32.9 2.9 %collective-permute-start.9 = (bf16[192,256]{1,0:T(8,128)(2,1)S(1)}, bf16[192,256]{1,0:T(8,128)(2,1)S(1)}, u32[]{:S(2)}, u32[]{:S(2)}) collective-permute-start(bf16[192,256]{1,0:T(8,128)(2,1)S(1)} %get-tuple-element.47), channel_id=1, source_target_pairs={{0,1},{1,0},{2,3},{3,2},{4,5},{5,4},{6,7},{7,6},{8,9},{9,8},{10,11... | collective-permute-start | bytes 294920 | tf_op jit(solution)/shard_map/ppermute | solution.py:29
  34.1 5.0 %collective-permute-start.10 = (bf16[192,256]{1,0:T(8,128)(2,1)S(1)}, bf16[192,256]{1,0:T(8,128)(2,1)S(1)}, u32[]{:S(2)}, u32[]{:S(2)}) collective-permute-start(bf16[192,256]{1,0:T(8,128)(2,1)S(1)} %get-tuple-element.52), channel_id=1, source_target_pairs={{0,2},{1,3},{2,0},{3,1},{4,6},{5,7},{6,4},{7,5},{8,10},{9,11},{10,... | collective-permute-start | bytes 294920 | tf_op jit(solution)/shard_map/ppermute | solution.py:29
  35.4 5.9 %collective-permute-start.11 = (bf16[192,256]{1,0:T(8,128)(2,1)S(1)}, bf16[192,256]{1,0:T(8,128)(2,1)S(1)}, u32[]{:S(2)}, u32[]{:S(2)}) collective-permute-start(bf16[192,256]{1,0:T(8,128)(2,1)S(1)} %get-tuple-element.53), channel_id=1, source_target_pairs={{0,3},{1,2},{2,1},{3,0},{4,7},{5,6},{6,5},{7,4},{8,11},{9,10},{10,... | collective-permute-start | bytes 294920 | tf_op jit(solution)/shard_map/ppermute | solution.py:29
  36.8 4.5 %collective-permute-start.14 = (bf16[192,128]{1,0:T(8,128)(2,1)S(1)}, bf16[192,128]{1,0:T(8,128)(2,1)S(1)}, u32[]{:S(2)}, u32[]{:S(2)}) collective-permute-start(bf16[192,128]{1,0:T(8,128)(2,1)S(1)} %get-tuple-element.58), channel_id=1, source_target_pairs={{0,1},{1,0},{2,3},{3,2},{4,5},{5,4},{6,7},{7,6},{8,9},{9,8},{10,11... | collective-permute-start | bytes 147464 | tf_op jit(solution)/shard_map/ppermute | solution.py:29
  37.4 4.3 %collective-permute-start.15 = (bf16[192,128]{1,0:T(8,128)(2,1)S(1)}, bf16[192,128]{1,0:T(8,128)(2,1)S(1)}, u32[]{:S(2)}, u32[]{:S(2)}) collective-permute-start(bf16[192,128]{1,0:T(8,128)(2,1)S(1)} %get-tuple-element.59), channel_id=1, source_target_pairs={{0,2},{1,3},{2,0},{3,1},{4,6},{5,7},{6,4},{7,5},{8,10},{9,11},{10,... | collective-permute-start | bytes 147464 | tf_op jit(solution)/shard_map/ppermute | solution.py:29
  38.6 4.3 %collective-permute-start.16 = (bf16[192,128]{1,0:T(8,128)(2,1)S(1)}, bf16[192,128]{1,0:T(8,128)(2,1)S(1)}, u32[]{:S(2)}, u32[]{:S(2)}) collective-permute-start(bf16[192,128]{1,0:T(8,128)(2,1)S(1)} %get-tuple-element.60), channel_id=1, source_target_pairs={{0,3},{1,2},{2,1},{3,0},{4,7},{5,6},{6,5},{7,4},{8,11},{9,10},{10,... | collective-permute-start | bytes 147464 | tf_op jit(solution)/shard_map/ppermute | solution.py:29

commit v6 on v5

--- a/solution.py
+++ b/solution.py
@@ -244,11 +244,11 @@
         total_ref[place, :] = summed[:, HEAD_DIM:]
 
 
-def late_body(groups, operands, layout, asked, tiles, tokens, heads, first, parts, *refs):
+def late_body(groups, operands, layout, asked, tiles, tokens, heads, first, parts, after, *refs):
     rows = tiles * tokens
     queries, arrays = refs[:asked], refs[asked : asked + operands]
     left = refs[asked + operands : asked + operands + 3 * parts]
-    outs = refs[asked + operands + 3 * parts :]
+    outs = refs[asked + operands + 3 * parts + after :]
     counts = counts_of(arrays, groups, rows)
     windows = [window_of(tile, tiles, groups) for tile in range(tiles)]
     block = len(layout) * tokens
@@ -277,25 +277,28 @@
         for count in counts
     ]
     worst = jnp.zeros((block, HEAD_DIM), jnp.float32)
-    for head in range(heads):
-        for tile, window in enumerate(windows):
-            largest, total, summed = early(head, tile)
-            scores = scored(head, tile)
-            largest = jnp.concatenate([largest] * (scores.shape[1] // HEAD_DIM), 1)
-            weight = jnp.exp2((scores - largest) * SCALE).astype(jnp.bfloat16)
-            kept = jnp.concatenate(
-                [real[group][n] for group, n in window for _ in groups[group][1]], 0
-            )
-            values = gather(arrays, groups, window, rows, tokens, head) * kept
-            added = jnp.dot(
-                weight,
-                jnp.concatenate([values, kept], 1),
-                preferred_element_type=jnp.float32,
-            )
-            total = total + added[:, HEAD_DIM:]
-            worst = jnp.where(total < LARGEST_TOTAL, worst, 1.0)
-            result = (summed + added[:, :HEAD_DIM]) / total
-            write(head, tile, result.astype(jnp.bfloat16))
+    steps = [(head, tile) for head in range(heads) for tile in range(tiles)]
+    ahead = scored(*steps[0])
+    for i, (head, tile) in enumerate(steps):
+        scores, window = ahead, windows[tile]
+        if i + 1 < len(steps):
+            ahead = scored(*steps[i + 1])
+        largest, total, summed = early(head, tile)
+        largest = jnp.concatenate([largest] * (scores.shape[1] // HEAD_DIM), 1)
+        weight = jnp.exp2((scores - largest) * SCALE).astype(jnp.bfloat16)
+        kept = jnp.concatenate(
+            [real[group][n] for group, n in window for _ in groups[group][1]], 0
+        )
+        values = gather(arrays, groups, window, rows, tokens, head) * kept
+        added = jnp.dot(
+            weight,
+            jnp.concatenate([values, kept], 1),
+            preferred_element_type=jnp.float32,
+        )
+        total = total + added[:, HEAD_DIM:]
+        worst = jnp.where(total < LARGEST_TOTAL, worst, 1.0)
+        result = (summed + added[:, :HEAD_DIM]) / total
+        write(head, tile, result.astype(jnp.bfloat16))
 
     @pl.when(jnp.max(worst) > 0.0)
     def _():
@@ -342,12 +345,11 @@
     return attend(kernel, [*queries, *arrays], outs, EARLY_FLOPS)
 
 
-def attend_late(queries, layout, arrays, groups, tiles, tokens, heads, first, left):
+def attend_late(queries, layout, arrays, groups, tiles, tokens, heads, first, left, after):
     outs = [pltpu.VMEM((tiles * tokens, heads * HEAD_DIM), jnp.bfloat16)] * len(layout)
-    kernel = functools.partial(
-        late_body, groups, len(arrays), layout, len(queries), tiles, tokens, heads, first, len(left) // 3
-    )
-    return attend(kernel, [*queries, *arrays, *left], outs)
+    sizes = (len(arrays), layout, len(queries), tiles, tokens, heads, first)
+    kernel = functools.partial(late_body, groups, *sizes, len(left) // 3, len(after))
+    return attend(kernel, [*queries, *arrays, *left, *after], outs)
 
 
 def join_body(jobs, part, me_ref, *rest):
@@ -451,13 +453,10 @@
             len(heads_now),
             first,
             left[len(pieces) > 0],
-        )
-        results = list(results)
-        results[1] = swap_head(results[1], 1, devices)
-        if not pieces:
-            results[1], *left[1] = lax.optimization_barrier((results[1], *left[1]))
+            [piece[2] for piece in pieces[:1]],
+        )
         pieces += [
-            (bit, first * HEAD_DIM, swap_head(b, bit, devices) if bit > 1 else b)
+            (bit, first * HEAD_DIM, swap_head(b, bit, devices) if bit else b)
             for bit, b in enumerate(results)
         ]
     return join(me, pieces, rows, heads * HEAD_DIM, devices).reshape(tiles, tokens, width)

time: 44.2 us -> 43.8 us (level)
  waiting for transfers between devices: 11.2 us -> 9.22 us
  starting transfers between devices: 21.7 us -> 23.6 us
    ppermute x11, waiting for transfers between devices: 7.05 us -> 5.03 us  [swap_head(): return lax.ppermute(block, 'head', [(i, i ^ bit) for i in range(devices)])]
    ppermute x11, starting transfers between devices: 9.44 us -> 11.3 us  [swap_head(): return lax.ppermute(block, 'head', [(i, i ^ bit) for i in range(devices)])]
  transfers between devices with their start and end apart: 17 -> 17, of which waited for: 7 -> 6; matrix products, arithmetic and copies ran while one was open for 0% -> 0% of each run, Pallas kernels for 19% -> 18%
where the time goes in v6:
time: 43.8 us; the launch traced here: 43.4 us
  starting transfers between devices  23.6 us (54%)
  Pallas kernels  10.4 us (24%)
  waiting for transfers between devices  9.22 us (21%)
    ppermute x6, starting transfers between devices, swap_pairs(): return lax.ppermute(block, 'tok', route)  12.3 us
    ppermute x11, starting transfers between devices, swap_head(): return lax.ppermute(block, 'head', [(i, i ^ bit) for i in range(devices)])  11.3 us
    pallas_call x4, Pallas kernels, attend(): pl.pallas_call(kernel, out_shape=outs, in_specs=in_vmem(len(operands)), o...  6.36 us
    ppermute x11, waiting for transfers between devices, swap_head(): return lax.ppermute(block, 'head', [(i, i ^ bit) for i in range(devices)])  5.03 us
    ppermute x6, waiting for transfers between devices, swap_pairs(): return lax.ppermute(block, 'tok', route)  4.19 us
    pallas_call x1, Pallas kernels, pack(): pl.pallas_call(functools.partial(pack_body, devices, heads), out_shape=[p...  1.63 us
    pallas_call x4, Pallas kernels, stack(): pl.pallas_call(functools.partial(stack_body, spans, len(after)), out_shap...  1.58 us
  transfers between devices with their start and end apart: 17, of which 6 were waited for; matrix products, arithmetic and copies ran while one was open for 0% of the time, Pallas kernels for 18%

profile of v6, /device:TPU:9, one launch (start us, length us, event | category | flops | bytes accessed | tf_op | source)
XLA Modules:
  0.0 43.4 jit_solution(11002830582479852379)
XLA Ops:
  0.0 1.6 %shard_map.46 = (bf16[400,384]{1,0:T(8,128)(2,1)S(1)}, bf16[576,384]{1,0:T(8,128)(2,1)S(1)}, bf16[960,128]{1,0:T(8,128)(2,1)S(1)}, bf16[192,384]{1,0:T(8,128)(2,...) custom-call(s32[3]{0:T(128)} %counts_in.1, s32[1]{0:T(128)} %bitcast.me_ref, ...), custom_call_target="tpu_custom_call" | custom-call | bytes 3538944 | tf_op jit(solution)/shard_map/pallas_call | solution.py:101
  1.6 0.7 %collective-permute-start = (bf16[576,384]{1,0:T(8,128)(2,1)S(1)}, bf16[576,384]{1,0:T(8,128)(2,1)S(1)}, u32[]{:S(2)}, u32[]{:S(2)}) collective-permute-start(bf16[576,384]{1,0:T(8,128)(2,1)S(1)} %get-tuple-element.30), channel_id=1, source_target_pairs={{0,1},{1,0},{2,3},{3,2},{4,5},{5,4},{6,7},{7,6},{8,9},{9,8},{10,11... | collective-permute-start | bytes 1327112 | tf_op jit(solution)/shard_map/ppermute | solution.py:29
  2.5 1.2 %collective-permute-start.5 = (bf16[384,256]{1,0:T(8,128)(2,1)S(1)}, bf16[384,256]{1,0:T(8,128)(2,1)S(1)}, u32[]{:S(2)}, u32[]{:S(2)}) collective-permute-start(bf16[384,256]{1,0:T(8,128)(2,1)S(1)} %get-tuple-element.34), channel_id=1, source_target_pairs={{0,2},{1,3},{2,0},{3,1},{4,6},{5,7},{6,4},{7,5},{8,10},{9,11},{10,... | collective-permute-start | bytes 589832 | tf_op jit(solution)/shard_map/ppermute | solution.py:29
  3.7 0.9 %collective-permute-start.6 = (bf16[384,256]{1,0:T(8,128)(2,1)S(1)}, bf16[384,256]{1,0:T(8,128)(2,1)S(1)}, u32[]{:S(2)}, u32[]{:S(2)}) collective-permute-start(bf16[384,256]{1,0:T(8,128)(2,1)S(1)} %get-tuple-element.35), channel_id=1, source_target_pairs={{0,3},{1,2},{2,1},{3,0},{4,7},{5,6},{6,5},{7,4},{8,11},{9,10},{10,... | collective-permute-start | bytes 589832 | tf_op jit(solution)/shard_map/ppermute | solution.py:29
  4.8 4.5 %collective-permute-start.4 = (bf16[784,384]{1,0:T(8,128)(2,1)S(1)}, bf16[784,384]{1,0:T(8,128)(2,1)S(1)}, u32[]{:S(2)}, u32[]{:S(2)}) collective-permute-start(bf16[784,384]{1,0:T(8,128)(2,1)S(1)} %shard_map.48.refs_2_.refs_3_), channel_id=1, source_target_pairs={{4,8},{8,4},{5,9},{9,5},{6,10},{10,6},{7,11},{11,7},{20,24},{24,20... | collective-permute-start | bytes 1806344 | tf_op jit(solution)/shard_map/ppermute | solution.py:38
  9.3 0.7 %shard_map.47 = bf16[1920,128]{1,0:T(8,128)(2,1)S(1)} custom-call(bf16[960,128]{1,0:T(8,128)(2,1)S(1)} %get-tuple-element.31.refs_0_, bf16[960,128]{1,0:T(8,128)(2,1)S(1)} %collective-permute-done.1.refs_1_), custom_call_target="tpu_custom_call" | custom-call | bytes 245760 | tf_op jit(solution)/shard_map/pallas_call | solution.py:136
  9.9 1.3 %collective-permute-start.2 = (bf16[1920,128]{1,0:T(8,128)(2,1)S(1)}, bf16[1920,128]{1,0:T(8,128)(2,1)S(1)}, u32[]{:S(2)}, u32[]{:S(2)}) collective-permute-start(bf16[1920,128]{1,0:T(8,128)(2,1)S(1)} %shard_map.47), channel_id=1, source_target_pairs={{0,2},{1,3},{2,0},{3,1},{4,6},{5,7},{6,4},{7,5},{8,10},{9,11},{10,... | collective-permute-start | bytes 1474568 | tf_op jit(solution)/shard_map/ppermute | solution.py:29
  11.2 3.2 %collective-permute-done.6.refs_1_.refs_6_.refs_7_ = bf16[384,256]{1,0:T(8,128)(2,1)S(1)} collective-permute-done((bf16[384,256]{1,0:T(8,128)(2,1)S(1)}, bf16[384,256]{1,0:T(8,128)(2,1)S(1)}, u32[]{:S(2)}, u32[]{:S(2)}) %collective-permute-start.6) | collective-permute-done | bytes 196640 | tf_op jit(solution)/shard_map/ppermute | solution.py:29
  15.0 4.5 %collective-permute-start.8 = (bf16[768,256]{1,0:T(8,128)(2,1)S(1)}, bf16[768,256]{1,0:T(8,128)(2,1)S(1)}, u32[]{:S(2)}, u32[]{:S(2)}) collective-permute-start(bf16[768,256]{1,0:T(8,128)(2,1)S(1)} %shard_map.49), channel_id=1, source_target_pairs={{4,8},{8,4},{5,9},{9,5},{6,10},{10,6},{7,11},{11,7},{20,24},{24,20... | collective-permute-start | bytes 1179656 | tf_op jit(solution)/shard_map/ppermute | solution.py:38
  19.5 0.5 %collective-permute-done.3.refs_3_.refs_4_ = bf16[784,384]{1,0:T(8,128)(2,1)S(1)} collective-permute-done((bf16[784,384]{1,0:T(8,128)(2,1)S(1)}, bf16[784,384]{1,0:T(8,128)(2,1)S(1)}, u32[]{:S(2)}, u32[]{:S(2)}) %collective-permute-start.3) | collective-permute-done | bytes 602144 | tf_op jit(solution)/shard_map/ppermute | solution.py:38
  20.0 3.0 %collective-permute-done.4.refs_4_.refs_5_ = bf16[784,384]{1,0:T(8,128)(2,1)S(1)} collective-permute-done((bf16[784,384]{1,0:T(8,128)(2,1)S(1)}, bf16[784,384]{1,0:T(8,128)(2,1)S(1)}, u32[]{:S(2)}, u32[]{:S(2)}) %collective-permute-start.4) | collective-permute-done | bytes 602144 | tf_op jit(solution)/shard_map/ppermute | solution.py:38
  23.1 1.5 %shard_map.50 = (f32[768,128]{1,0:T(8,128)S(1)}, f32[768,128]{1,0:T(8,128)S(1)}, f32[768,128]{1,0:T(8,128)S(1)}) custom-call(bf16[192,384]{1,0:T(8,128)(2,1)S(1)} %get-tuple-element.29.refs_0_, bf16[576,384]{1,0:T(8,128)(2,1)S(1)} %collective-permute-done.refs_1_, bf16[784,384]{1,0:T(8,128)(2,1)S(1)} %shard_map.48.refs_2_.refs_3_, ...), custom_call_target="tpu_custom_call" | custom-call | tf_op jit(solution)/shard_map/pallas_call | solution.py:326
  25.0 3.1 %collective-permute-start.13 = (bf16[768,128]{1,0:T(8,128)(2,1)S(1)}, bf16[768,128]{1,0:T(8,128)(2,1)S(1)}, u32[]{:S(2)}, u32[]{:S(2)}) collective-permute-start(bf16[768,128]{1,0:T(8,128)(2,1)S(1)} %shard_map.53), channel_id=1, source_target_pairs={{4,8},{8,4},{5,9},{9,5},{6,10},{10,6},{7,11},{11,7},{20,24},{24,20... | collective-permute-start | bytes 589832 | tf_op jit(solution)/shard_map/ppermute | solution.py:38
  28.1 2.7 %shard_map.51 = (f32[768,128]{1,0:T(8,128)S(1)}, f32[768,128]{1,0:T(8,128)S(1)}, f32[768,128]{1,0:T(8,128)S(1)}, f32[768,128]{1,0:T(8,128)S(1)}, f32[768,128]{1,0:T(8,128)S(1)}, /*index=5*/f32[768,128]{1,0:T(8,128)S(1)}) custom-call(bf16[192,384]{1,0:T(8,128)(2,1)S(1)} %get-tuple-element.29.refs_0_, bf16[576,384]{1,0:T(8,128)(2,1)S(1)} %collective-permute-done.refs_1_, ...), custom_call_target="tpu_custom_call" | custom-call | tf_op jit(solution)/shard_map/pallas_call | solution.py:326
  30.8 0.6 %collective-permute-done.8.refs_6_ = bf16[768,256]{1,0:T(8,128)(2,1)S(1)} collective-permute-done((bf16[768,256]{1,0:T(8,128)(2,1)S(1)}, bf16[768,256]{1,0:T(8,128)(2,1)S(1)}, u32[]{:S(2)}, u32[]{:S(2)}) %collective-permute-start.8) | collective-permute-done | bytes 393248 | tf_op jit(solution)/shard_map/ppermute | solution.py:38
  31.5 1.3 %shard_map.52 = (bf16[192,256]{1,0:T(8,128)(2,1)S(1)}, bf16[192,256]{1,0:T(8,128)(2,1)S(1)}, bf16[192,256]{1,0:T(8,128)(2,1)S(1)}, bf16[192,256]{1,0:T(8,128)(2,1)S(1)}) custom-call(bf16[192,384]{1,0:T(8,128)(2,1)S(1)} %get-tuple-element.29.refs_0_, bf16[576,384]{1,0:T(8,128)(2,1)S(1)} %collective-permute-done.refs_1_, ...), custom_call_target="tpu_custom_call" | custom-call | tf_op jit(solution)/shard_map/pallas_call | solution.py:326
  32.8 1.3 %collective-permute-start.10 = (bf16[192,256]{1,0:T(8,128)(2,1)S(1)}, bf16[192,256]{1,0:T(8,128)(2,1)S(1)}, u32[]{:S(2)}, u32[]{:S(2)}) collective-permute-start(bf16[192,256]{1,0:T(8,128)(2,1)S(1)} %get-tuple-element.44), channel_id=1, source_target_pairs={{0,2},{1,3},{2,0},{3,1},{4,6},{5,7},{6,4},{7,5},{8,10},{9,11},{10,... | collective-permute-start | bytes 294920 | tf_op jit(solution)/shard_map/ppermute | solution.py:29
  34.2 1.5 %collective-permute-start.11 = (bf16[192,256]{1,0:T(8,128)(2,1)S(1)}, bf16[192,256]{1,0:T(8,128)(2,1)S(1)}, u32[]{:S(2)}, u32[]{:S(2)}) collective-permute-start(bf16[192,256]{1,0:T(8,128)(2,1)S(1)} %get-tuple-element.45), channel_id=1, source_target_pairs={{0,3},{1,2},{2,1},{3,0},{4,7},{5,6},{6,5},{7,4},{8,11},{9,10},{10,... | collective-permute-start | bytes 294920 | tf_op jit(solution)/shard_map/ppermute | solution.py:29
  35.7 0.8 %shard_map.54 = (bf16[192,128]{1,0:T(8,128)(2,1)S(1)}, bf16[192,128]{1,0:T(8,128)(2,1)S(1)}, bf16[192,128]{1,0:T(8,128)(2,1)S(1)}, bf16[192,128]{1,0:T(8,128)(2,1)S(1)}) custom-call(bf16[192,384]{1,0:T(8,128)(2,1)S(1)} %get-tuple-element.29.refs_0_, bf16[576,384]{1,0:T(8,128)(2,1)S(1)} %collective-permute-done.refs_1_, ...), custom_call_target="tpu_custom_call" | custom-call | tf_op jit(solution)/shard_map/pallas_call | solution.py:326
  36.5 0.8 %collective-permute-start.14 = (bf16[192,128]{1,0:T(8,128)(2,1)S(1)}, bf16[192,128]{1,0:T(8,128)(2,1)S(1)}, u32[]{:S(2)}, u32[]{:S(2)}) collective-permute-start(bf16[192,128]{1,0:T(8,128)(2,1)S(1)} %get-tuple-element.50), channel_id=1, source_target_pairs={{0,1},{1,0},{2,3},{3,2},{4,5},{5,4},{6,7},{7,6},{8,9},{9,8},{10,11... | collective-permute-start | bytes 147464 | tf_op jit(solution)/shard_map/ppermute | solution.py:29
  37.3 1.2 %collective-permute-start.15 = (bf16[192,128]{1,0:T(8,128)(2,1)S(1)}, bf16[192,128]{1,0:T(8,128)(2,1)S(1)}, u32[]{:S(2)}, u32[]{:S(2)}) collective-permute-start(bf16[192,128]{1,0:T(8,128)(2,1)S(1)} %get-tuple-element.51), channel_id=1, source_target_pairs={{0,2},{1,3},{2,0},{3,1},{4,6},{5,7},{6,4},{7,5},{8,10},{9,11},{10,... | collective-permute-start | bytes 147464 | tf_op jit(solution)/shard_map/ppermute | solution.py:29
  38.5 2.3 %collective-permute-start.16 = (bf16[192,128]{1,0:T(8,128)(2,1)S(1)}, bf16[192,128]{1,0:T(8,128)(2,1)S(1)}, u32[]{:S(2)}, u32[]{:S(2)}) collective-permute-start(bf16[192,128]{1,0:T(8,128)(2,1)S(1)} %get-tuple-element.52), channel_id=1, source_target_pairs={{0,3},{1,2},{2,1},{3,0},{4,7},{5,6},{6,5},{7,4},{8,11},{9,10},{10,... | collective-permute-start | bytes 147464 | tf_op jit(solution)/shard_map/ppermute | solution.py:29
  41.3 1.3 %collective-permute-done.16.rest_7_ = bf16[192,128]{1,0:T(8,128)(2,1)S(1)} collective-permute-done((bf16[192,128]{1,0:T(8,128)(2,1)S(1)}, bf16[192,128]{1,0:T(8,128)(2,1)S(1)}, u32[]{:S(2)}, u32[]{:S(2)}) %collective-permute-start.16) | collective-permute-done | bytes 49184 | tf_op jit(solution)/shard_map/ppermute | solution.py:29
  42.5 0.9 %shard_map.55 = bf16[192,1536]{1,0:T(8,128)(2,1)} custom-call(s32[1]{0:T(128)} %bitcast.me_ref, bf16[192,256]{1,0:T(8,128)(2,1)S(1)} %get-tuple-element.42.refs_10_.rest_0_, bf16[192,256]{1,0:T(8,128)(2,1)S(1)} %collective-permute-done.9.rest_1_, bf16[192,256]{1,0:T(8,128)(2,1)S(1)} %collective-permute-done.10.rest_2_, ...), custom_call_target="tpu_custom_call" | custom-call | tf_op jit(solution)/shard_map/pallas_call | solution.py:370
  (20 shorter events, 1.7 us)
Async XLA Ops:
  1.6 2.9 %collective-permute-start = (bf16[576,384]{1,0:T(8,128)(2,1)S(1)}, bf16[576,384]{1,0:T(8,128)(2,1)S(1)}, u32[]{:S(2)}, u32[]{:S(2)}) collective-permute-start(bf16[576,384]{1,0:T(8,128)(2,1)S(1)} %get-tuple-element.30), channel_id=1, source_target_pairs={{0,1},{1,0},{2,3},{3,2},{4,5},{5,4},{6,7},{7,6},{8,9},{9,8},{10,11... | collective-permute-start | bytes 1327112 | tf_op jit(solution)/shard_map/ppermute | solution.py:29
  2.4 6.9 %collective-permute-start.1 = (bf16[960,128]{1,0:T(8,128)(2,1)S(1)}, bf16[960,128]{1,0:T(8,128)(2,1)S(1)}, u32[]{:S(2)}, u32[]{:S(2)}) collective-permute-start(bf16[960,128]{1,0:T(8,128)(2,1)S(1)} %get-tuple-element.32), channel_id=1, source_target_pairs={{0,1},{1,0},{2,3},{3,2},{4,5},{5,4},{6,7},{7,6},{8,9},{9,8},{10,11... | collective-permute-start | bytes 737288 | tf_op jit(solution)/shard_map/ppermute | solution.py:29
  2.5 8.8 %collective-permute-start.5 = (bf16[384,256]{1,0:T(8,128)(2,1)S(1)}, bf16[384,256]{1,0:T(8,128)(2,1)S(1)}, u32[]{:S(2)}, u32[]{:S(2)}) collective-permute-start(bf16[384,256]{1,0:T(8,128)(2,1)S(1)} %get-tuple-element.34), channel_id=1, source_target_pairs={{0,2},{1,3},{2,0},{3,1},{4,6},{5,7},{6,4},{7,5},{8,10},{9,11},{10,... | collective-permute-start | bytes 589832 | tf_op jit(solution)/shard_map/ppermute | solution.py:29
  3.7 10.8 %collective-permute-start.6 = (bf16[384,256]{1,0:T(8,128)(2,1)S(1)}, bf16[384,256]{1,0:T(8,128)(2,1)S(1)}, u32[]{:S(2)}, u32[]{:S(2)}) collective-permute-start(bf16[384,256]{1,0:T(8,128)(2,1)S(1)} %get-tuple-element.35), channel_id=1, source_target_pairs={{0,3},{1,2},{2,1},{3,0},{4,7},{5,6},{6,5},{7,4},{8,11},{9,10},{10,... | collective-permute-start | bytes 589832 | tf_op jit(solution)/shard_map/ppermute | solution.py:29
  4.7 15.4 %collective-permute-start.3 = (bf16[784,384]{1,0:T(8,128)(2,1)S(1)}, bf16[784,384]{1,0:T(8,128)(2,1)S(1)}, u32[]{:S(2)}, u32[]{:S(2)}) collective-permute-start(bf16[784,384]{1,0:T(8,128)(2,1)S(1)} %shard_map.48.refs_2_.refs_3_), channel_id=1, source_target_pairs={{0,4},{4,0},{8,12},{12,8},{1,5},{5,1},{9,13},{13,9},{2,6},{6,2},{1... | collective-permute-start | bytes 1806344 | tf_op jit(solution)/shard_map/ppermute | solution.py:38
  4.8 18.3 %collective-permute-start.4 = (bf16[784,384]{1,0:T(8,128)(2,1)S(1)}, bf16[784,384]{1,0:T(8,128)(2,1)S(1)}, u32[]{:S(2)}, u32[]{:S(2)}) collective-permute-start(bf16[784,384]{1,0:T(8,128)(2,1)S(1)} %shard_map.48.refs_2_.refs_3_), channel_id=1, source_target_pairs={{4,8},{8,4},{5,9},{9,5},{6,10},{10,6},{7,11},{11,7},{20,24},{24,20... | collective-permute-start | bytes 1806344 | tf_op jit(solution)/shard_map/ppermute | solution.py:38
  9.9 14.7 %collective-permute-start.2 = (bf16[1920,128]{1,0:T(8,128)(2,1)S(1)}, bf16[1920,128]{1,0:T(8,128)(2,1)S(1)}, u32[]{:S(2)}, u32[]{:S(2)}) collective-permute-start(bf16[1920,128]{1,0:T(8,128)(2,1)S(1)} %shard_map.47), channel_id=1, source_target_pairs={{0,2},{1,3},{2,0},{3,1},{4,6},{5,7},{6,4},{7,5},{8,10},{9,11},{10,... | collective-permute-start | bytes 1474568 | tf_op jit(solution)/shard_map/ppermute | solution.py:29
  15.0 15.9 %collective-permute-start.7 = (bf16[768,256]{1,0:T(8,128)(2,1)S(1)}, bf16[768,256]{1,0:T(8,128)(2,1)S(1)}, u32[]{:S(2)}, u32[]{:S(2)}) collective-permute-start(bf16[768,256]{1,0:T(8,128)(2,1)S(1)} %shard_map.49), channel_id=1, source_target_pairs={{0,4},{4,0},{8,12},{12,8},{1,5},{5,1},{9,13},{13,9},{2,6},{6,2},{1... | collective-permute-start | bytes 1179656 | tf_op jit(solution)/shard_map/ppermute | solution.py:38
  15.0 16.4 %collective-permute-start.8 = (bf16[768,256]{1,0:T(8,128)(2,1)S(1)}, bf16[768,256]{1,0:T(8,128)(2,1)S(1)}, u32[]{:S(2)}, u32[]{:S(2)}) collective-permute-start(bf16[768,256]{1,0:T(8,128)(2,1)S(1)} %shard_map.49), channel_id=1, source_target_pairs={{4,8},{8,4},{5,9},{9,5},{6,10},{10,6},{7,11},{11,7},{20,24},{24,20... | collective-permute-start | bytes 1179656 | tf_op jit(solution)/shard_map/ppermute | solution.py:38
  24.9 10.8 %collective-permute-start.12 = (bf16[768,128]{1,0:T(8,128)(2,1)S(1)}, bf16[768,128]{1,0:T(8,128)(2,1)S(1)}, u32[]{:S(2)}, u32[]{:S(2)}) collective-permute-start(bf16[768,128]{1,0:T(8,128)(2,1)S(1)} %shard_map.53), channel_id=1, source_target_pairs={{0,4},{4,0},{8,12},{12,8},{1,5},{5,1},{9,13},{13,9},{2,6},{6,2},{1... | collective-permute-start | bytes 589832 | tf_op jit(solution)/shard_map/ppermute | solution.py:38
  25.0 10.7 %collective-permute-start.13 = (bf16[768,128]{1,0:T(8,128)(2,1)S(1)}, bf16[768,128]{1,0:T(8,128)(2,1)S(1)}, u32[]{:S(2)}, u32[]{:S(2)}) collective-permute-start(bf16[768,128]{1,0:T(8,128)(2,1)S(1)} %shard_map.53), channel_id=1, source_target_pairs={{4,8},{8,4},{5,9},{9,5},{6,10},{10,6},{7,11},{11,7},{20,24},{24,20... | collective-permute-start | bytes 589832 | tf_op jit(solution)/shard_map/ppermute | solution.py:38
  32.8 5.7 %collective-permute-start.10 = (bf16[192,256]{1,0:T(8,128)(2,1)S(1)}, bf16[192,256]{1,0:T(8,128)(2,1)S(1)}, u32[]{:S(2)}, u32[]{:S(2)}) collective-permute-start(bf16[192,256]{1,0:T(8,128)(2,1)S(1)} %get-tuple-element.44), channel_id=1, source_target_pairs={{0,2},{1,3},{2,0},{3,1},{4,6},{5,7},{6,4},{7,5},{8,10},{9,11},{10,... | collective-permute-start | bytes 294920 | tf_op jit(solution)/shard_map/ppermute | solution.py:29
  34.2 6.6 %collective-permute-start.11 = (bf16[192,256]{1,0:T(8,128)(2,1)S(1)}, bf16[192,256]{1,0:T(8,128)(2,1)S(1)}, u32[]{:S(2)}, u32[]{:S(2)}) collective-permute-start(bf16[192,256]{1,0:T(8,128)(2,1)S(1)} %get-tuple-element.45), channel_id=1, source_target_pairs={{0,3},{1,2},{2,1},{3,0},{4,7},{5,6},{6,5},{7,4},{8,11},{9,10},{10,... | collective-permute-start | bytes 294920 | tf_op jit(solution)/shard_map/ppermute | solution.py:29
  35.7 5.1 %collective-permute-start.9 = (bf16[192,256]{1,0:T(8,128)(2,1)S(1)}, bf16[192,256]{1,0:T(8,128)(2,1)S(1)}, u32[]{:S(2)}, u32[]{:S(2)}) collective-permute-start(bf16[192,256]{1,0:T(8,128)(2,1)S(1)} %get-tuple-element.43), channel_id=1, source_target_pairs={{0,1},{1,0},{2,3},{3,2},{4,5},{5,4},{6,7},{7,6},{8,9},{9,8},{10,11... | collective-permute-start | bytes 294920 | tf_op jit(solution)/shard_map/ppermute | solution.py:29
  36.5 4.3 %collective-permute-start.14 = (bf16[192,128]{1,0:T(8,128)(2,1)S(1)}, bf16[192,128]{1,0:T(8,128)(2,1)S(1)}, u32[]{:S(2)}, u32[]{:S(2)}) collective-permute-start(bf16[192,128]{1,0:T(8,128)(2,1)S(1)} %get-tuple-element.50), channel_id=1, source_target_pairs={{0,1},{1,0},{2,3},{3,2},{4,5},{5,4},{6,7},{7,6},{8,9},{9,8},{10,11... | collective-permute-start | bytes 147464 | tf_op jit(solution)/shard_map/ppermute | solution.py:29
  37.3 4.0 %collective-permute-start.15 = (bf16[192,128]{1,0:T(8,128)(2,1)S(1)}, bf16[192,128]{1,0:T(8,128)(2,1)S(1)}, u32[]{:S(2)}, u32[]{:S(2)}) collective-permute-start(bf16[192,128]{1,0:T(8,128)(2,1)S(1)} %get-tuple-element.51), channel_id=1, source_target_pairs={{0,2},{1,3},{2,0},{3,1},{4,6},{5,7},{6,4},{7,5},{8,10},{9,11},{10,... | collective-permute-start | bytes 147464 | tf_op jit(solution)/shard_map/ppermute | solution.py:29
  38.5 4.1 %collective-permute-start.16 = (bf16[192,128]{1,0:T(8,128)(2,1)S(1)}, bf16[192,128]{1,0:T(8,128)(2,1)S(1)}, u32[]{:S(2)}, u32[]{:S(2)}) collective-permute-start(bf16[192,128]{1,0:T(8,128)(2,1)S(1)} %get-tuple-element.52), channel_id=1, source_target_pairs={{0,3},{1,2},{2,1},{3,0},{4,7},{5,6},{6,5},{7,4},{8,11},{9,10},{10,... | collective-permute-start | bytes 147464 | tf_op jit(solution)/shard_map/ppermute | solution.py:29

commit v7 on v6

--- a/solution.py
+++ b/solution.py
@@ -352,8 +352,9 @@
     return attend(kernel, [*queries, *arrays, *left, *after], outs)
 
 
-def join_body(jobs, part, me_ref, *rest):
+def join_body(jobs, part, held, me_ref, *rest):
     out_ref, sems = rest[-2:]
+    rest = rest[held:]
     me = me_ref[0]
     copies = []
     for i, (bit, base) in enumerate(jobs):
@@ -365,16 +366,20 @@
         copy.wait()
 
 
-def join(me, pieces, rows, part, devices):
+def join(me, pieces, rows, part, devices, begun=()):
     jobs = [piece[:2] for piece in pieces]
+    hbm = [pl.BlockSpec(memory_space=pltpu.HBM)]
     return pl.pallas_call(
-        functools.partial(join_body, jobs, part),
+        functools.partial(join_body, jobs, part, len(begun)),
         out_shape=jax.ShapeDtypeStruct((rows, devices * part), jnp.bfloat16),
-        in_specs=[pl.BlockSpec(memory_space=pltpu.SMEM)] + in_vmem(len(pieces)),
-        out_specs=pl.BlockSpec(memory_space=pl.ANY),
+        in_specs=[pl.BlockSpec(memory_space=pltpu.SMEM)]
+        + hbm * len(begun)
+        + in_vmem(len(pieces)),
+        out_specs=hbm[0],
         scratch_shapes=[pltpu.SemaphoreType.DMA((len(pieces),))],
+        input_output_aliases={1: 0} if begun else {},
         compiler_params=pltpu.CompilerParams(vmem_limit_bytes=VMEM_LIMIT),
-    )(me, *(piece[2] for piece in pieces))
+    )(me, *begun, *(piece[2] for piece in pieces))
 
 
 def body(query, key, value, valid_rows):
@@ -455,11 +460,17 @@
             left[len(pieces) > 0],
             [piece[2] for piece in pieces[:1]],
         )
+        order = range(devices) if not pieces else range(devices - 1, -1, -1)
         pieces += [
-            (bit, first * HEAD_DIM, swap_head(b, bit, devices) if bit else b)
-            for bit, b in enumerate(results)
+            (bit, first * HEAD_DIM, swap_head(results[bit], bit, devices) if bit else results[0])
+            for bit in order
         ]
-    return join(me, pieces, rows, heads * HEAD_DIM, devices).reshape(tiles, tokens, width)
+    begun, ended = [], []
+    for piece in pieces:
+        (ended if piece[0] and piece[1] else begun).append(piece)
+    shape = (rows, heads * HEAD_DIM, devices)
+    joined = join(me, ended, *shape, [join(me, begun, *shape)])
+    return joined.reshape(tiles, tokens, width)
 
 
 def solution(mesh):

time: 43.8 us -> 43.4 us (level)
  starting transfers between devices: 23.6 us -> 21.7 us
  waiting for transfers between devices: 9.22 us -> 10.1 us
  Pallas kernels: 10.4 us -> 11 us
    ppermute x11, starting transfers between devices: 11.3 us -> 9.39 us  [swap_head(): return lax.ppermute(block, 'head', [(i, i ^ bit) for i in range(devices)])]
    ppermute x11, waiting for transfers between devices: 5.03 us -> 5.94 us  [swap_head(): return lax.ppermute(block, 'head', [(i, i ^ bit) for i in range(devices)])]
    pallas_call x1 -> x2, Pallas kernels: 0.87 us -> 1.47 us  [join(): pl.pallas_call(functools.partial(join_body, jobs, part, len(begun)), out_...]
  transfers between devices with their start and end apart: 17 -> 17, of which waited for: 6 -> 6; matrix products, arithmetic and copies ran while one was open for 0% -> 0% of each run, Pallas kernels for 18% -> 20%
where the time goes in v7:
time: 43.4 us; the launch traced here: 43 us
  starting transfers between devices  21.7 us (50%)
  Pallas kernels  11 us (25%)
  waiting for transfers between devices  10.1 us (23%)
    ppermute x6, starting transfers between devices, swap_pairs(): return lax.ppermute(block, 'tok', route)  12.3 us
    ppermute x11, starting transfers between devices, swap_head(): return lax.ppermute(block, 'head', [(i, i ^ bit) for i in range(devices)])  9.39 us
    pallas_call x4, Pallas kernels, attend(): pl.pallas_call(kernel, out_shape=outs, in_specs=in_vmem(len(operands)), o...  6.36 us
    ppermute x11, waiting for transfers between devices, swap_head(): return lax.ppermute(block, 'head', [(i, i ^ bit) for i in range(devices)])  5.94 us
    ppermute x6, waiting for transfers between devices, swap_pairs(): return lax.ppermute(block, 'tok', route)  4.19 us
    pallas_call x1, Pallas kernels, pack(): pl.pallas_call(functools.partial(pack_body, devices, heads), out_shape=[p...  1.63 us
    pallas_call x4, Pallas kernels, stack(): pl.pallas_call(functools.partial(stack_body, spans, len(after)), out_shap...  1.58 us
    pallas_call x2, Pallas kernels, join(): pl.pallas_call(functools.partial(join_body, jobs, part, len(begun)), out_...  1.47 us
  transfers between devices with their start and end apart: 17, of which 6 were waited for; matrix products, arithmetic and copies ran while one was open for 0% of the time, Pallas kernels for 20%

profile of v7, /device:TPU:9, one launch (start us, length us, event | category | flops | bytes accessed | tf_op | source)
XLA Modules:
  0.0 43.0 jit_solution(17291716370264840851)
XLA Ops:
  0.0 1.6 %shard_map.46 = (bf16[400,384]{1,0:T(8,128)(2,1)S(1)}, bf16[576,384]{1,0:T(8,128)(2,1)S(1)}, bf16[960,128]{1,0:T(8,128)(2,1)S(1)}, bf16[192,384]{1,0:T(8,128)(2,...) custom-call(s32[3]{0:T(128)} %counts_in.1, s32[1]{0:T(128)} %bitcast.me_ref, ...), custom_call_target="tpu_custom_call" | custom-call | bytes 3538944 | tf_op jit(solution)/shard_map/pallas_call | solution.py:101
  1.6 0.7 %collective-permute-start = (bf16[576,384]{1,0:T(8,128)(2,1)S(1)}, bf16[576,384]{1,0:T(8,128)(2,1)S(1)}, u32[]{:S(2)}, u32[]{:S(2)}) collective-permute-start(bf16[576,384]{1,0:T(8,128)(2,1)S(1)} %get-tuple-element.30), channel_id=1, source_target_pairs={{0,1},{1,0},{2,3},{3,2},{4,5},{5,4},{6,7},{7,6},{8,9},{9,8},{10,11... | collective-permute-start | bytes 1327112 | tf_op jit(solution)/shard_map/ppermute | solution.py:29
  2.5 1.2 %collective-permute-start.5 = (bf16[384,256]{1,0:T(8,128)(2,1)S(1)}, bf16[384,256]{1,0:T(8,128)(2,1)S(1)}, u32[]{:S(2)}, u32[]{:S(2)}) collective-permute-start(bf16[384,256]{1,0:T(8,128)(2,1)S(1)} %get-tuple-element.34), channel_id=1, source_target_pairs={{0,2},{1,3},{2,0},{3,1},{4,6},{5,7},{6,4},{7,5},{8,10},{9,11},{10,... | collective-permute-start | bytes 589832 | tf_op jit(solution)/shard_map/ppermute | solution.py:29
  3.7 0.9 %collective-permute-start.6 = (bf16[384,256]{1,0:T(8,128)(2,1)S(1)}, bf16[384,256]{1,0:T(8,128)(2,1)S(1)}, u32[]{:S(2)}, u32[]{:S(2)}) collective-permute-start(bf16[384,256]{1,0:T(8,128)(2,1)S(1)} %get-tuple-element.35), channel_id=1, source_target_pairs={{0,3},{1,2},{2,1},{3,0},{4,7},{5,6},{6,5},{7,4},{8,11},{9,10},{10,... | collective-permute-start | bytes 589832 | tf_op jit(solution)/shard_map/ppermute | solution.py:29
  4.8 4.5 %collective-permute-start.4 = (bf16[784,384]{1,0:T(8,128)(2,1)S(1)}, bf16[784,384]{1,0:T(8,128)(2,1)S(1)}, u32[]{:S(2)}, u32[]{:S(2)}) collective-permute-start(bf16[784,384]{1,0:T(8,128)(2,1)S(1)} %shard_map.48.refs_2_.refs_3_), channel_id=1, source_target_pairs={{4,8},{8,4},{5,9},{9,5},{6,10},{10,6},{7,11},{11,7},{20,24},{24,20... | collective-permute-start | bytes 1806344 | tf_op jit(solution)/shard_map/ppermute | solution.py:38
  9.3 0.7 %shard_map.47 = bf16[1920,128]{1,0:T(8,128)(2,1)S(1)} custom-call(bf16[960,128]{1,0:T(8,128)(2,1)S(1)} %get-tuple-element.31.refs_0_, bf16[960,128]{1,0:T(8,128)(2,1)S(1)} %collective-permute-done.1.refs_1_), custom_call_target="tpu_custom_call" | custom-call | bytes 245760 | tf_op jit(solution)/shard_map/pallas_call | solution.py:136
  9.9 1.3 %collective-permute-start.2 = (bf16[1920,128]{1,0:T(8,128)(2,1)S(1)}, bf16[1920,128]{1,0:T(8,128)(2,1)S(1)}, u32[]{:S(2)}, u32[]{:S(2)}) collective-permute-start(bf16[1920,128]{1,0:T(8,128)(2,1)S(1)} %shard_map.47), channel_id=1, source_target_pairs={{0,2},{1,3},{2,0},{3,1},{4,6},{5,7},{6,4},{7,5},{8,10},{9,11},{10,... | collective-permute-start | bytes 1474568 | tf_op jit(solution)/shard_map/ppermute | solution.py:29
  11.2 3.2 %collective-permute-done.6.refs_1_.refs_6_.refs_7_ = bf16[384,256]{1,0:T(8,128)(2,1)S(1)} collective-permute-done((bf16[384,256]{1,0:T(8,128)(2,1)S(1)}, bf16[384,256]{1,0:T(8,128)(2,1)S(1)}, u32[]{:S(2)}, u32[]{:S(2)}) %collective-permute-start.6) | collective-permute-done | bytes 196640 | tf_op jit(solution)/shard_map/ppermute | solution.py:29
  15.0 4.5 %collective-permute-start.8 = (bf16[768,256]{1,0:T(8,128)(2,1)S(1)}, bf16[768,256]{1,0:T(8,128)(2,1)S(1)}, u32[]{:S(2)}, u32[]{:S(2)}) collective-permute-start(bf16[768,256]{1,0:T(8,128)(2,1)S(1)} %shard_map.49), channel_id=1, source_target_pairs={{4,8},{8,4},{5,9},{9,5},{6,10},{10,6},{7,11},{11,7},{20,24},{24,20... | collective-permute-start | bytes 1179656 | tf_op jit(solution)/shard_map/ppermute | solution.py:38
  19.5 0.5 %collective-permute-done.3.refs_3_.refs_4_ = bf16[784,384]{1,0:T(8,128)(2,1)S(1)} collective-permute-done((bf16[784,384]{1,0:T(8,128)(2,1)S(1)}, bf16[784,384]{1,0:T(8,128)(2,1)S(1)}, u32[]{:S(2)}, u32[]{:S(2)}) %collective-permute-start.3) | collective-permute-done | bytes 602144 | tf_op jit(solution)/shard_map/ppermute | solution.py:38
  20.0 3.0 %collective-permute-done.4.refs_4_.refs_5_ = bf16[784,384]{1,0:T(8,128)(2,1)S(1)} collective-permute-done((bf16[784,384]{1,0:T(8,128)(2,1)S(1)}, bf16[784,384]{1,0:T(8,128)(2,1)S(1)}, u32[]{:S(2)}, u32[]{:S(2)}) %collective-permute-start.4) | collective-permute-done | bytes 602144 | tf_op jit(solution)/shard_map/ppermute | solution.py:38
  23.1 1.5 %shard_map.50 = (f32[768,128]{1,0:T(8,128)S(1)}, f32[768,128]{1,0:T(8,128)S(1)}, f32[768,128]{1,0:T(8,128)S(1)}) custom-call(bf16[192,384]{1,0:T(8,128)(2,1)S(1)} %get-tuple-element.29.refs_0_, bf16[576,384]{1,0:T(8,128)(2,1)S(1)} %collective-permute-done.refs_1_, bf16[784,384]{1,0:T(8,128)(2,1)S(1)} %shard_map.48.refs_2_.refs_3_, ...), custom_call_target="tpu_custom_call" | custom-call | tf_op jit(solution)/shard_map/pallas_call | solution.py:326
  25.0 3.1 %collective-permute-start.13 = (bf16[768,128]{1,0:T(8,128)(2,1)S(1)}, bf16[768,128]{1,0:T(8,128)(2,1)S(1)}, u32[]{:S(2)}, u32[]{:S(2)}) collective-permute-start(bf16[768,128]{1,0:T(8,128)(2,1)S(1)} %shard_map.53), channel_id=1, source_target_pairs={{4,8},{8,4},{5,9},{9,5},{6,10},{10,6},{7,11},{11,7},{20,24},{24,20... | collective-permute-start | bytes 589832 | tf_op jit(solution)/shard_map/ppermute | solution.py:38
  28.1 2.7 %shard_map.51 = (f32[768,128]{1,0:T(8,128)S(1)}, f32[768,128]{1,0:T(8,128)S(1)}, f32[768,128]{1,0:T(8,128)S(1)}, f32[768,128]{1,0:T(8,128)S(1)}, f32[768,128]{1,0:T(8,128)S(1)}, /*index=5*/f32[768,128]{1,0:T(8,128)S(1)}) custom-call(bf16[192,384]{1,0:T(8,128)(2,1)S(1)} %get-tuple-element.29.refs_0_, bf16[576,384]{1,0:T(8,128)(2,1)S(1)} %collective-permute-done.refs_1_, ...), custom_call_target="tpu_custom_call" | custom-call | tf_op jit(solution)/shard_map/pallas_call | solution.py:326
  30.8 0.6 %collective-permute-done.8.refs_6_ = bf16[768,256]{1,0:T(8,128)(2,1)S(1)} collective-permute-done((bf16[768,256]{1,0:T(8,128)(2,1)S(1)}, bf16[768,256]{1,0:T(8,128)(2,1)S(1)}, u32[]{:S(2)}, u32[]{:S(2)}) %collective-permute-start.8) | collective-permute-done | bytes 393248 | tf_op jit(solution)/shard_map/ppermute | solution.py:38
  31.5 1.3 %shard_map.52 = (bf16[192,256]{1,0:T(8,128)(2,1)S(1)}, bf16[192,256]{1,0:T(8,128)(2,1)S(1)}, bf16[192,256]{1,0:T(8,128)(2,1)S(1)}, bf16[192,256]{1,0:T(8,128)(2,1)S(1)}) custom-call(bf16[192,384]{1,0:T(8,128)(2,1)S(1)} %get-tuple-element.29.refs_0_, bf16[576,384]{1,0:T(8,128)(2,1)S(1)} %collective-permute-done.refs_1_, ...), custom_call_target="tpu_custom_call" | custom-call | tf_op jit(solution)/shard_map/pallas_call | solution.py:326
  32.8 1.3 %collective-permute-start.10 = (bf16[192,256]{1,0:T(8,128)(2,1)S(1)}, bf16[192,256]{1,0:T(8,128)(2,1)S(1)}, u32[]{:S(2)}, u32[]{:S(2)}) collective-permute-start(bf16[192,256]{1,0:T(8,128)(2,1)S(1)} %get-tuple-element.44), channel_id=1, source_target_pairs={{0,2},{1,3},{2,0},{3,1},{4,6},{5,7},{6,4},{7,5},{8,10},{9,11},{10,... | collective-permute-start | bytes 294920 | tf_op jit(solution)/shard_map/ppermute | solution.py:29
  34.2 1.5 %collective-permute-start.11 = (bf16[192,256]{1,0:T(8,128)(2,1)S(1)}, bf16[192,256]{1,0:T(8,128)(2,1)S(1)}, u32[]{:S(2)}, u32[]{:S(2)}) collective-permute-start(bf16[192,256]{1,0:T(8,128)(2,1)S(1)} %get-tuple-element.45), channel_id=1, source_target_pairs={{0,3},{1,2},{2,1},{3,0},{4,7},{5,6},{6,5},{7,4},{8,11},{9,10},{10,... | collective-permute-start | bytes 294920 | tf_op jit(solution)/shard_map/ppermute | solution.py:29
  35.7 0.8 %shard_map.54 = (bf16[192,128]{1,0:T(8,128)(2,1)S(1)}, bf16[192,128]{1,0:T(8,128)(2,1)S(1)}, bf16[192,128]{1,0:T(8,128)(2,1)S(1)}, bf16[192,128]{1,0:T(8,128)(2,1)S(1)}) custom-call(bf16[192,384]{1,0:T(8,128)(2,1)S(1)} %get-tuple-element.29.refs_0_, bf16[576,384]{1,0:T(8,128)(2,1)S(1)} %collective-permute-done.refs_1_, ...), custom_call_target="tpu_custom_call" | custom-call | tf_op jit(solution)/shard_map/pallas_call | solution.py:326
  36.5 1.9 %collective-permute-start.14 = (bf16[192,128]{1,0:T(8,128)(2,1)S(1)}, bf16[192,128]{1,0:T(8,128)(2,1)S(1)}, u32[]{:S(2)}, u32[]{:S(2)}) collective-permute-start(bf16[192,128]{1,0:T(8,128)(2,1)S(1)} %get-tuple-element.50), channel_id=1, source_target_pairs={{0,3},{1,2},{2,1},{3,0},{4,7},{5,6},{6,5},{7,4},{8,11},{9,10},{10,... | collective-permute-start | bytes 147464 | tf_op jit(solution)/shard_map/ppermute | solution.py:29
  38.8 1.7 %collective-permute-done.11.rest_3_ = bf16[192,256]{1,0:T(8,128)(2,1)S(1)} collective-permute-done((bf16[192,256]{1,0:T(8,128)(2,1)S(1)}, bf16[192,256]{1,0:T(8,128)(2,1)S(1)}, u32[]{:S(2)}, u32[]{:S(2)}) %collective-permute-start.11) | collective-permute-done | bytes 98336 | tf_op jit(solution)/shard_map/ppermute | solution.py:29
  40.5 0.8 %shard_map.55.rest_0_ = bf16[192,1536]{1,0:T(8,128)(2,1)} custom-call(s32[1]{0:T(128)} %bitcast.me_ref, bf16[192,256]{1,0:T(8,128)(2,1)S(1)} %get-tuple-element.42.refs_10_.rest_0_, bf16[192,256]{1,0:T(8,128)(2,1)S(1)} %collective-permute-done.9.rest_1_, bf16[192,256]{1,0:T(8,128)(2,1)S(1)} %collective-permute-done.10.rest_2_, ...), custom_call_target="tpu_custom_call" | custom-call | tf_op jit(solution)/shard_map/pallas_call | solution.py:372
  41.3 1.0 %collective-permute-done.15.rest_2_ = bf16[192,128]{1,0:T(8,128)(2,1)S(1)} collective-permute-done((bf16[192,128]{1,0:T(8,128)(2,1)S(1)}, bf16[192,128]{1,0:T(8,128)(2,1)S(1)}, u32[]{:S(2)}, u32[]{:S(2)}) %collective-permute-start.15) | collective-permute-done | bytes 49184 | tf_op jit(solution)/shard_map/ppermute | solution.py:29
  42.3 0.7 %shard_map.56 = bf16[192,1536]{1,0:T(8,128)(2,1)} custom-call(s32[1]{0:T(128)} %bitcast.me_ref, bf16[192,1536]{1,0:T(8,128)(2,1)} %shard_map.55.rest_0_, bf16[192,128]{1,0:T(8,128)(2,1)S(1)} %collective-permute-done.14.rest_1_, bf16[192,128]{1,0:T(8,128)(2,1)S(1)} %collective-permute-done.15.rest_2_, ...), custom_call_target="tpu_custom_call", output_to_operand_aliasing={{}: (1, {})} | custom-call | tf_op jit(solution)/shard_map/pallas_call | solution.py:372
  (21 shorter events, 1.7 us)
Async XLA Ops:
  1.6 2.9 %collective-permute-start = (bf16[576,384]{1,0:T(8,128)(2,1)S(1)}, bf16[576,384]{1,0:T(8,128)(2,1)S(1)}, u32[]{:S(2)}, u32[]{:S(2)}) collective-permute-start(bf16[576,384]{1,0:T(8,128)(2,1)S(1)} %get-tuple-element.30), channel_id=1, source_target_pairs={{0,1},{1,0},{2,3},{3,2},{4,5},{5,4},{6,7},{7,6},{8,9},{9,8},{10,11... | collective-permute-start | bytes 1327112 | tf_op jit(solution)/shard_map/ppermute | solution.py:29
  2.4 6.9 %collective-permute-start.1 = (bf16[960,128]{1,0:T(8,128)(2,1)S(1)}, bf16[960,128]{1,0:T(8,128)(2,1)S(1)}, u32[]{:S(2)}, u32[]{:S(2)}) collective-permute-start(bf16[960,128]{1,0:T(8,128)(2,1)S(1)} %get-tuple-element.32), channel_id=1, source_target_pairs={{0,1},{1,0},{2,3},{3,2},{4,5},{5,4},{6,7},{7,6},{8,9},{9,8},{10,11... | collective-permute-start | bytes 737288 | tf_op jit(solution)/shard_map/ppermute | solution.py:29
  2.5 8.8 %collective-permute-start.5 = (bf16[384,256]{1,0:T(8,128)(2,1)S(1)}, bf16[384,256]{1,0:T(8,128)(2,1)S(1)}, u32[]{:S(2)}, u32[]{:S(2)}) collective-permute-start(bf16[384,256]{1,0:T(8,128)(2,1)S(1)} %get-tuple-element.34), channel_id=1, source_target_pairs={{0,2},{1,3},{2,0},{3,1},{4,6},{5,7},{6,4},{7,5},{8,10},{9,11},{10,... | collective-permute-start | bytes 589832 | tf_op jit(solution)/shard_map/ppermute | solution.py:29
  3.7 10.8 %collective-permute-start.6 = (bf16[384,256]{1,0:T(8,128)(2,1)S(1)}, bf16[384,256]{1,0:T(8,128)(2,1)S(1)}, u32[]{:S(2)}, u32[]{:S(2)}) collective-permute-start(bf16[384,256]{1,0:T(8,128)(2,1)S(1)} %get-tuple-element.35), channel_id=1, source_target_pairs={{0,3},{1,2},{2,1},{3,0},{4,7},{5,6},{6,5},{7,4},{8,11},{9,10},{10,... | collective-permute-start | bytes 589832 | tf_op jit(solution)/shard_map/ppermute | solution.py:29
  4.7 15.4 %collective-permute-start.3 = (bf16[784,384]{1,0:T(8,128)(2,1)S(1)}, bf16[784,384]{1,0:T(8,128)(2,1)S(1)}, u32[]{:S(2)}, u32[]{:S(2)}) collective-permute-start(bf16[784,384]{1,0:T(8,128)(2,1)S(1)} %shard_map.48.refs_2_.refs_3_), channel_id=1, source_target_pairs={{0,4},{4,0},{8,12},{12,8},{1,5},{5,1},{9,13},{13,9},{2,6},{6,2},{1... | collective-permute-start | bytes 1806344 | tf_op jit(solution)/shard_map/ppermute | solution.py:38
  4.8 18.3 %collective-permute-start.4 = (bf16[784,384]{1,0:T(8,128)(2,1)S(1)}, bf16[784,384]{1,0:T(8,128)(2,1)S(1)}, u32[]{:S(2)}, u32[]{:S(2)}) collective-permute-start(bf16[784,384]{1,0:T(8,128)(2,1)S(1)} %shard_map.48.refs_2_.refs_3_), channel_id=1, source_target_pairs={{4,8},{8,4},{5,9},{9,5},{6,10},{10,6},{7,11},{11,7},{20,24},{24,20... | collective-permute-start | bytes 1806344 | tf_op jit(solution)/shard_map/ppermute | solution.py:38
  9.9 14.7 %collective-permute-start.2 = (bf16[1920,128]{1,0:T(8,128)(2,1)S(1)}, bf16[1920,128]{1,0:T(8,128)(2,1)S(1)}, u32[]{:S(2)}, u32[]{:S(2)}) collective-permute-start(bf16[1920,128]{1,0:T(8,128)(2,1)S(1)} %shard_map.47), channel_id=1, source_target_pairs={{0,2},{1,3},{2,0},{3,1},{4,6},{5,7},{6,4},{7,5},{8,10},{9,11},{10,... | collective-permute-start | bytes 1474568 | tf_op jit(solution)/shard_map/ppermute | solution.py:29
  15.0 15.9 %collective-permute-start.7 = (bf16[768,256]{1,0:T(8,128)(2,1)S(1)}, bf16[768,256]{1,0:T(8,128)(2,1)S(1)}, u32[]{:S(2)}, u32[]{:S(2)}) collective-permute-start(bf16[768,256]{1,0:T(8,128)(2,1)S(1)} %shard_map.49), channel_id=1, source_target_pairs={{0,4},{4,0},{8,12},{12,8},{1,5},{5,1},{9,13},{13,9},{2,6},{6,2},{1... | collective-permute-start | bytes 1179656 | tf_op jit(solution)/shard_map/ppermute | solution.py:38
  15.0 16.4 %collective-permute-start.8 = (bf16[768,256]{1,0:T(8,128)(2,1)S(1)}, bf16[768,256]{1,0:T(8,128)(2,1)S(1)}, u32[]{:S(2)}, u32[]{:S(2)}) collective-permute-start(bf16[768,256]{1,0:T(8,128)(2,1)S(1)} %shard_map.49), channel_id=1, source_target_pairs={{4,8},{8,4},{5,9},{9,5},{6,10},{10,6},{7,11},{11,7},{20,24},{24,20... | collective-permute-start | bytes 1179656 | tf_op jit(solution)/shard_map/ppermute | solution.py:38
  24.9 10.8 %collective-permute-start.12 = (bf16[768,128]{1,0:T(8,128)(2,1)S(1)}, bf16[768,128]{1,0:T(8,128)(2,1)S(1)}, u32[]{:S(2)}, u32[]{:S(2)}) collective-permute-start(bf16[768,128]{1,0:T(8,128)(2,1)S(1)} %shard_map.53), channel_id=1, source_target_pairs={{0,4},{4,0},{8,12},{12,8},{1,5},{5,1},{9,13},{13,9},{2,6},{6,2},{1... | collective-permute-start | bytes 589832 | tf_op jit(solution)/shard_map/ppermute | solution.py:38
  25.0 10.7 %collective-permute-start.13 = (bf16[768,128]{1,0:T(8,128)(2,1)S(1)}, bf16[768,128]{1,0:T(8,128)(2,1)S(1)}, u32[]{:S(2)}, u32[]{:S(2)}) collective-permute-start(bf16[768,128]{1,0:T(8,128)(2,1)S(1)} %shard_map.53), channel_id=1, source_target_pairs={{4,8},{8,4},{5,9},{9,5},{6,10},{10,6},{7,11},{11,7},{20,24},{24,20... | collective-permute-start | bytes 589832 | tf_op jit(solution)/shard_map/ppermute | solution.py:38
  32.8 5.8 %collective-permute-start.10 = (bf16[192,256]{1,0:T(8,128)(2,1)S(1)}, bf16[192,256]{1,0:T(8,128)(2,1)S(1)}, u32[]{:S(2)}, u32[]{:S(2)}) collective-permute-start(bf16[192,256]{1,0:T(8,128)(2,1)S(1)} %get-tuple-element.44), channel_id=1, source_target_pairs={{0,2},{1,3},{2,0},{3,1},{4,6},{5,7},{6,4},{7,5},{8,10},{9,11},{10,... | collective-permute-start | bytes 294920 | tf_op jit(solution)/shard_map/ppermute | solution.py:29
  34.2 6.4 %collective-permute-start.11 = (bf16[192,256]{1,0:T(8,128)(2,1)S(1)}, bf16[192,256]{1,0:T(8,128)(2,1)S(1)}, u32[]{:S(2)}, u32[]{:S(2)}) collective-permute-start(bf16[192,256]{1,0:T(8,128)(2,1)S(1)} %get-tuple-element.45), channel_id=1, source_target_pairs={{0,3},{1,2},{2,1},{3,0},{4,7},{5,6},{6,5},{7,4},{8,11},{9,10},{10,... | collective-permute-start | bytes 294920 | tf_op jit(solution)/shard_map/ppermute | solution.py:29
  35.7 4.9 %collective-permute-start.9 = (bf16[192,256]{1,0:T(8,128)(2,1)S(1)}, bf16[192,256]{1,0:T(8,128)(2,1)S(1)}, u32[]{:S(2)}, u32[]{:S(2)}) collective-permute-start(bf16[192,256]{1,0:T(8,128)(2,1)S(1)} %get-tuple-element.43), channel_id=1, source_target_pairs={{0,1},{1,0},{2,3},{3,2},{4,5},{5,4},{6,7},{7,6},{8,9},{9,8},{10,11... | collective-permute-start | bytes 294920 | tf_op jit(solution)/shard_map/ppermute | solution.py:29
  36.5 4.9 %collective-permute-start.14 = (bf16[192,128]{1,0:T(8,128)(2,1)S(1)}, bf16[192,128]{1,0:T(8,128)(2,1)S(1)}, u32[]{:S(2)}, u32[]{:S(2)}) collective-permute-start(bf16[192,128]{1,0:T(8,128)(2,1)S(1)} %get-tuple-element.50), channel_id=1, source_target_pairs={{0,3},{1,2},{2,1},{3,0},{4,7},{5,6},{6,5},{7,4},{8,11},{9,10},{10,... | collective-permute-start | bytes 147464 | tf_op jit(solution)/shard_map/ppermute | solution.py:29
  38.4 4.0 %collective-permute-start.15 = (bf16[192,128]{1,0:T(8,128)(2,1)S(1)}, bf16[192,128]{1,0:T(8,128)(2,1)S(1)}, u32[]{:S(2)}, u32[]{:S(2)}) collective-permute-start(bf16[192,128]{1,0:T(8,128)(2,1)S(1)} %get-tuple-element.51), channel_id=1, source_target_pairs={{0,2},{1,3},{2,0},{3,1},{4,6},{5,7},{6,4},{7,5},{8,10},{9,11},{10,... | collective-permute-start | bytes 147464 | tf_op jit(solution)/shard_map/ppermute | solution.py:29
  38.6 3.7 %collective-permute-start.16 = (bf16[192,128]{1,0:T(8,128)(2,1)S(1)}, bf16[192,128]{1,0:T(8,128)(2,1)S(1)}, u32[]{:S(2)}, u32[]{:S(2)}) collective-permute-start(bf16[192,128]{1,0:T(8,128)(2,1)S(1)} %get-tuple-element.52), channel_id=1, source_target_pairs={{0,1},{1,0},{2,3},{3,2},{4,5},{5,4},{6,7},{7,6},{8,9},{9,8},{10,11... | collective-permute-start | bytes 147464 | tf_op jit(solution)/shard_map/ppermute | solution.py:29

commit v8 on v7

--- a/solution.py
+++ b/solution.py
@@ -38,46 +38,52 @@
     return lax.ppermute(block, "tok", route)
 
 
+def lanes_of(owner, heads, first=0, count=None):
+    start = pl.multiple_of((owner * heads + first) * HEAD_DIM, HEAD_DIM)
+    return pl.ds(start, (heads if count is None else count) * HEAD_DIM)
+
+
+def run_copies(jobs, sems):
+    copies = [pltpu.make_async_copy(src, dst, sems.at[i]) for i, (src, dst) in enumerate(jobs)]
+    for copy in copies:
+        copy.start()
+    return copies
+
+
+def last_of(q_ref, k_ref, v_ref, owner, heads):
+    sources = [q_ref.at[:, lanes_of(owner, heads, head, 1)] for head in range(heads)]
+    return sources + [ref.at[:, lanes_of(owner, heads, heads - 1, 1)] for ref in (k_ref, v_ref)]
+
+
 def pack_body(devices, heads, counts_in, me_ref, q_ref, k_ref, v_ref, *rest):
-    far = devices - 2
-    own_ref, sibling_ref, passed_ref, own_q_ref = rest[:4]
-    far_refs, last_refs = rest[4 : 4 + far], rest[4 + far : -3]
+    own_ref, sibling_ref, passed_ref = rest[:3]
+    far_refs = rest[3:-3]
     counts_ref, count_sem, sems = rest[-3:]
     rows = k_ref.shape[0]
     me = me_ref[0]
-
-    def lanes(bit, first=0, count=heads):
-        start = ((me ^ bit) * heads + first) * HEAD_DIM
-        return pl.ds(pl.multiple_of(start, HEAD_DIM), count * HEAD_DIM)
-
     count_copy = pltpu.make_async_copy(counts_in, counts_ref, count_sem)
     count_copy.start()
+    beside = lanes_of(me ^ 1, heads)
     jobs = [
-        (k_ref.at[:, lanes(1)], sibling_ref.at[pl.ds(0, rows)]),
-        (v_ref.at[:, lanes(1)], sibling_ref.at[pl.ds(rows, rows)]),
-        (q_ref.at[:, lanes(1)], sibling_ref.at[pl.ds(2 * rows, rows)]),
+        (ref.at[:, beside], sibling_ref.at[pl.ds(i * rows, rows)])
+        for i, ref in enumerate((k_ref, v_ref, q_ref))
     ]
-    for bit, ref in enumerate(far_refs, 2):
+    for bit, far_ref in enumerate(far_refs, 2):
         jobs += [
-            (k_ref.at[:, lanes(bit, 0, heads - 1)], ref.at[pl.ds(0, rows)]),
-            (v_ref.at[:, lanes(bit, 0, heads - 1)], ref.at[pl.ds(rows, rows)]),
+            (ref.at[:, lanes_of(me ^ bit, heads, 0, heads - 1)], far_ref.at[pl.ds(i * rows, rows)])
+            for i, ref in enumerate((k_ref, v_ref))
         ]
     jobs += [
-        (k_ref.at[:, lanes(0)], own_ref.at[pl.ds(0, rows)]),
-        (v_ref.at[:, lanes(0)], own_ref.at[pl.ds(rows, rows)]),
-        (q_ref.at[:, lanes(0)], own_q_ref),
+        (ref.at[:, lanes_of(me, heads)], own_ref.at[pl.ds(i * rows, rows)])
+        for i, ref in enumerate((k_ref, v_ref))
     ]
-    for bit in range(2, devices):
-        pair = bit // 2 - 1
-        ref, base = (passed_ref, pair * (heads + 2)) if bit % 2 else (last_refs[pair], 0)
-        sources = [q_ref.at[:, lanes(bit, head, 1)] for head in range(heads)]
-        sources += [k_ref.at[:, lanes(bit, heads - 1, 1)], v_ref.at[:, lanes(bit, heads - 1, 1)]]
-        jobs += [
-            (source, ref.at[pl.ds((base + i) * rows, rows)]) for i, source in enumerate(sources)
-        ]
-    copies = [pltpu.make_async_copy(src, dst, sems.at[i]) for i, (src, dst) in enumerate(jobs)]
-    for copy in copies:
-        copy.start()
+    passed = [
+        source
+        for bit in range(3, devices, 2)
+        for source in last_of(q_ref, k_ref, v_ref, me ^ bit, heads)
+    ]
+    jobs += [(source, passed_ref.at[pl.ds(i * rows, rows)]) for i, source in enumerate(passed)]
+    copies = run_copies(jobs, sems)
     count_copy.wait()
     shape = (COUNT_ROWS, own_ref.shape[1])
     row = lax.broadcasted_iota(jnp.int32, shape, 0)
@@ -89,15 +95,13 @@
         copy.wait()
 
 
-def pack(me, counts, query, key, value, devices):
-    rows, width = query.shape
+def pack(me, counts, fields, devices):
+    rows, width = fields[0].shape
     part = width // devices
     heads = part // HEAD_DIM
     far = devices - 2
     shapes = [(2 * rows + COUNT_ROWS, part), (3 * rows, part)]
-    shapes += [(far // 2 * (heads + 2) * rows, HEAD_DIM), (rows, part)]
-    shapes += [(2 * rows, part - HEAD_DIM)] * far + [((heads + 2) * rows, HEAD_DIM)] * (far // 2)
-    fields = [pltpu.with_memory_space_constraint(f, pltpu.HBM) for f in (query, key, value)]
+    shapes += [(far // 2 * (heads + 2) * rows, HEAD_DIM)] + [(2 * rows, part - HEAD_DIM)] * far
     results = pl.pallas_call(
         functools.partial(pack_body, devices, heads),
         out_shape=[pltpu.VMEM(shape, jnp.bfloat16) for shape in shapes],
@@ -107,12 +111,50 @@
         scratch_shapes=[
             pltpu.SMEM(counts.shape, jnp.int32),
             pltpu.SemaphoreType.DMA,
-            pltpu.SemaphoreType.DMA((6 + far * (heads + 4),)),
+            pltpu.SemaphoreType.DMA((5 + 2 * far + far // 2 * (heads + 2),)),
         ],
         compiler_params=pltpu.CompilerParams(vmem_limit_bytes=VMEM_LIMIT),
-        cost_estimate=pl.CostEstimate(flops=0, bytes_accessed=12 * query.size, transcendentals=0),
+        cost_estimate=pl.CostEstimate(
+            flops=0, bytes_accessed=12 * rows * width, transcendentals=0
+        ),
     )(pltpu.with_memory_space_constraint(counts, pltpu.HBM), me, *fields)
-    return (*results[:4], results[4 : 4 + far], results[4 + far :])
+    return results[0], results[1], results[2], results[3:]
+
+
+def pack_last_body(devices, heads, me_ref, q_ref, k_ref, v_ref, passed_ref, *rest):
+    own_q_ref, last_refs, sems = rest[0], rest[1:-1], rest[-1]
+    rows = k_ref.shape[0]
+    unit = (heads + 2) * rows
+    me = me_ref[0]
+    jobs = [(q_ref.at[:, lanes_of(me, heads)], own_q_ref)]
+    for pair, last_ref in enumerate(last_refs):
+        sources = last_of(q_ref, k_ref, v_ref, me ^ (2 * pair + 2), heads)
+        jobs += [(source, last_ref.at[pl.ds(i * rows, rows)]) for i, source in enumerate(sources)]
+        jobs.append((passed_ref.at[pl.ds(pair * unit, unit)], last_ref.at[pl.ds(unit, unit)]))
+    for copy in run_copies(jobs, sems):
+        copy.wait()
+
+
+def pack_last(me, fields, passed, devices):
+    rows, width = fields[0].shape
+    part = width // devices
+    heads = part // HEAD_DIM
+    far = devices // 2 - 1
+    shapes = [(rows, part)] + [(2 * (heads + 2) * rows, HEAD_DIM)] * far
+    results = pl.pallas_call(
+        functools.partial(pack_last_body, devices, heads),
+        out_shape=[pltpu.VMEM(shape, jnp.bfloat16) for shape in shapes],
+        in_specs=[pl.BlockSpec(memory_space=pltpu.SMEM)]
+        + [pl.BlockSpec(memory_space=pltpu.HBM)] * 3
+        + in_vmem(1),
+        out_specs=in_vmem(len(shapes)),
+        scratch_shapes=[pltpu.SemaphoreType.DMA((1 + far * (heads + 3),))],
+        compiler_params=pltpu.CompilerParams(vmem_limit_bytes=VMEM_LIMIT),
+        cost_estimate=pl.CostEstimate(
+            flops=0, bytes_accessed=2 * (heads + 2) * rows * HEAD_DIM, transcendentals=0
+        ),
+    )(me, *fields, passed)
+    return results[0], results[1:]
 
 
 def stack_body(jobs, after, *refs):
@@ -390,7 +432,8 @@
     heads = width // HEAD_DIM // devices
     me = lax.axis_index("head").astype(jnp.int32).reshape(1)
     flat = [field.reshape(tiles * tokens, width) for field in (query, key, value)]
-    own, sibling, passed, own_query, far, last = pack(me, valid_rows, *flat, devices)
+    flat = [pltpu.with_memory_space_constraint(field, pltpu.HBM) for field in flat]
+    own, sibling, passed, far = pack(me, valid_rows, flat, devices)
     rows = tiles * tokens
 
     def by_height(block):
@@ -410,10 +453,8 @@
     near = near + by_time(near)
 
     unit = (heads + 2) * rows
-    last = [
-        swap_head(stack([b, passed], [(0, unit), (i * unit, unit)]), 2 * i + 2, devices)
-        for i, b in enumerate(last)
-    ]
+    own_query, last = pack_last(me, flat, passed, devices)
+    last = [swap_head(b, 2 * i + 2, devices) for i, b in enumerate(last)]
     queries = [own_query, sibling, *last]
     layout = [(0, 0, False), (1, 2 * rows, False)]
     layout += [(2 + bit // 2, bit % 2 * unit, True) for bit in range(devices - 2)]

time: 43.4 us -> 43.2 us (level)
  waiting for transfers between devices: 10.1 us -> 9.31 us
    pallas_call x0 -> x1, Pallas kernels: none -> 1.04 us  [pack_last(): pl.pallas_call(functools.partial(pack_last_body, devices, heads), out_sha...]
    ppermute x11, waiting for transfers between devices: 5.94 us -> 5.13 us  [swap_head(): return lax.ppermute(block, 'head', [(i, i ^ bit) for i in range(devices)])]
    pallas_call x4 -> x3, Pallas kernels: 1.58 us -> 0.93 us  [stack(): pl.pallas_call(functools.partial(stack_body, spans, len(after)), out_shap...]
    ppermute x6, starting transfers between devices: 12.3 us -> 12.7 us  [swap_pairs(): return lax.ppermute(block, 'tok', route)]
  transfers between devices with their start and end apart: 17 -> 17, of which waited for: 6 -> 6; matrix products, arithmetic and copies ran while one was open for 0% -> 0% of each run, Pallas kernels for 20% -> 21%
where the time goes in v8:
time: 43.2 us; the launch traced here: 42.8 us
  starting transfers between devices  22.1 us (51%)
  Pallas kernels  11.3 us (26%)
  waiting for transfers between devices  9.31 us (22%)
    ppermute x6, starting transfers between devices, swap_pairs(): return lax.ppermute(block, 'tok', route)  12.7 us
    ppermute x11, starting transfers between devices, swap_head(): return lax.ppermute(block, 'head', [(i, i ^ bit) for i in range(devices)])  9.39 us
    pallas_call x4, Pallas kernels, attend(): pl.pallas_call(kernel, out_shape=outs, in_specs=in_vmem(len(operands)), o...  6.36 us
    ppermute x11, waiting for transfers between devices, swap_head(): return lax.ppermute(block, 'head', [(i, i ^ bit) for i in range(devices)])  5.13 us
    ppermute x6, waiting for transfers between devices, swap_pairs(): return lax.ppermute(block, 'tok', route)  4.18 us
    pallas_call x2, Pallas kernels, join(): pl.pallas_call(functools.partial(join_body, jobs, part, len(begun)), out_...  1.47 us
    pallas_call x1, Pallas kernels, pack(): pl.pallas_call(functools.partial(pack_body, devices, heads), out_shape=[p...  1.46 us
    pallas_call x1, Pallas kernels, pack_last(): pl.pallas_call(functools.partial(pack_last_body, devices, heads), out_sha...  1.04 us
  transfers between devices with their start and end apart: 17, of which 6 were waited for; matrix products, arithmetic and copies ran while one was open for 0% of the time, Pallas kernels for 21%

profile of v8, /device:TPU:9, one launch (start us, length us, event | category | flops | bytes accessed | tf_op | source)
XLA Modules:
  0.0 42.8 jit_solution(14674417210803509211)
XLA Ops:
  0.0 1.5 %shard_map.46 = (bf16[400,384]{1,0:T(8,128)(2,1)S(1)}, bf16[576,384]{1,0:T(8,128)(2,1)S(1)}, bf16[960,128]{1,0:T(8,128)(2,1)S(1)}, bf16[384,256]{1,0:T(8,128)(2,1)S(1)}, bf16[384,256]{1,0:T(8,128)(2,1)S(1)}) custom-call(s32[3]{0:T(128)} %counts_in.1, s32[1]{0:T(128)} %bitcast.me_ref, bf16[192,1536]{1,0:T(8,128)(2,1)} %bitcast.5, bf16[192,1536]{1,0:T(8,128)(2,1)} %bitcast.7, ...), custom_call_target="tpu_custom_call" | custom-call | bytes 3538944 | tf_op jit(solution)/shard_map/pallas_call | solution.py:105
  1.5 0.7 %collective-permute-start.1 = (bf16[576,384]{1,0:T(8,128)(2,1)S(1)}, bf16[576,384]{1,0:T(8,128)(2,1)S(1)}, u32[]{:S(2)}, u32[]{:S(2)}) collective-permute-start(bf16[576,384]{1,0:T(8,128)(2,1)S(1)} %get-tuple-element.31), channel_id=1, source_target_pairs={{0,1},{1,0},{2,3},{3,2},{4,5},{5,4},{6,7},{7,6},{8,9},{9,8},{10,11... | collective-permute-start | bytes 1327112 | tf_op jit(solution)/shard_map/ppermute | solution.py:29
  2.3 1.2 %collective-permute-start.5 = (bf16[384,256]{1,0:T(8,128)(2,1)S(1)}, bf16[384,256]{1,0:T(8,128)(2,1)S(1)}, u32[]{:S(2)}, u32[]{:S(2)}) collective-permute-start(bf16[384,256]{1,0:T(8,128)(2,1)S(1)} %get-tuple-element.34), channel_id=1, source_target_pairs={{0,2},{1,3},{2,0},{3,1},{4,6},{5,7},{6,4},{7,5},{8,10},{9,11},{10,... | collective-permute-start | bytes 589832 | tf_op jit(solution)/shard_map/ppermute | solution.py:29
  3.5 0.9 %collective-permute-start.6 = (bf16[384,256]{1,0:T(8,128)(2,1)S(1)}, bf16[384,256]{1,0:T(8,128)(2,1)S(1)}, u32[]{:S(2)}, u32[]{:S(2)}) collective-permute-start(bf16[384,256]{1,0:T(8,128)(2,1)S(1)} %get-tuple-element.35), channel_id=1, source_target_pairs={{0,3},{1,2},{2,1},{3,0},{4,7},{5,6},{6,5},{7,4},{8,11},{9,10},{10,... | collective-permute-start | bytes 589832 | tf_op jit(solution)/shard_map/ppermute | solution.py:29
  4.6 4.5 %collective-permute-start.4 = (bf16[784,384]{1,0:T(8,128)(2,1)S(1)}, bf16[784,384]{1,0:T(8,128)(2,1)S(1)}, u32[]{:S(2)}, u32[]{:S(2)}) collective-permute-start(bf16[784,384]{1,0:T(8,128)(2,1)S(1)} %shard_map.48.refs_2_.refs_3_), channel_id=1, source_target_pairs={{4,8},{8,4},{5,9},{9,5},{6,10},{10,6},{7,11},{11,7},{20,24},{24,20... | collective-permute-start | bytes 1806344 | tf_op jit(solution)/shard_map/ppermute | solution.py:38
  9.1 1.0 %shard_map.47 = (bf16[192,384]{1,0:T(8,128)(2,1)S(1)}, bf16[1920,128]{1,0:T(8,128)(2,1)S(1)}) custom-call(s32[1]{0:T(128)} %bitcast.me_ref, bf16[192,1536]{1,0:T(8,128)(2,1)} %bitcast.6, bf16[192,1536]{1,0:T(8,128)(2,1)} %bitcast.8, bf16[192,1536]{1,0:T(8,128)(2,1)} %bitcast.10, bf16[960,128]{1,0:T(8,128)(2,1)S(1)} %collective-permute-done.passed_ref), custom_call_target="tpu_custom_call" | custom-call | bytes 245760 | tf_op jit(solution)/shard_map/pallas_call | solution.py:144
  10.1 1.3 %collective-permute-start.2 = (bf16[1920,128]{1,0:T(8,128)(2,1)S(1)}, bf16[1920,128]{1,0:T(8,128)(2,1)S(1)}, u32[]{:S(2)}, u32[]{:S(2)}) collective-permute-start(bf16[1920,128]{1,0:T(8,128)(2,1)S(1)} %get-tuple-element.32), channel_id=1, source_target_pairs={{0,2},{1,3},{2,0},{3,1},{4,6},{5,7},{6,4},{7,5},{8,10},{9,11},{10,... | collective-permute-start | bytes 1474568 | tf_op jit(solution)/shard_map/ppermute | solution.py:29
  11.4 2.4 %collective-permute-done.6.refs_1_.refs_6_.refs_7_ = bf16[384,256]{1,0:T(8,128)(2,1)S(1)} collective-permute-done((bf16[384,256]{1,0:T(8,128)(2,1)S(1)}, bf16[384,256]{1,0:T(8,128)(2,1)S(1)}, u32[]{:S(2)}, u32[]{:S(2)}) %collective-permute-start.6) | collective-permute-done | bytes 196640 | tf_op jit(solution)/shard_map/ppermute | solution.py:29
  14.5 4.9 %collective-permute-start.8 = (bf16[768,256]{1,0:T(8,128)(2,1)S(1)}, bf16[768,256]{1,0:T(8,128)(2,1)S(1)}, u32[]{:S(2)}, u32[]{:S(2)}) collective-permute-start(bf16[768,256]{1,0:T(8,128)(2,1)S(1)} %shard_map.49), channel_id=1, source_target_pairs={{4,8},{8,4},{5,9},{9,5},{6,10},{10,6},{7,11},{11,7},{20,24},{24,20... | collective-permute-start | bytes 1179656 | tf_op jit(solution)/shard_map/ppermute | solution.py:38
  19.4 0.5 %collective-permute-done.3.refs_3_.refs_4_ = bf16[784,384]{1,0:T(8,128)(2,1)S(1)} collective-permute-done((bf16[784,384]{1,0:T(8,128)(2,1)S(1)}, bf16[784,384]{1,0:T(8,128)(2,1)S(1)}, u32[]{:S(2)}, u32[]{:S(2)}) %collective-permute-start.3) | collective-permute-done | bytes 602144 | tf_op jit(solution)/shard_map/ppermute | solution.py:38
  19.9 3.0 %collective-permute-done.4.refs_4_.refs_5_ = bf16[784,384]{1,0:T(8,128)(2,1)S(1)} collective-permute-done((bf16[784,384]{1,0:T(8,128)(2,1)S(1)}, bf16[784,384]{1,0:T(8,128)(2,1)S(1)}, u32[]{:S(2)}, u32[]{:S(2)}) %collective-permute-start.4) | collective-permute-done | bytes 602144 | tf_op jit(solution)/shard_map/ppermute | solution.py:38
  22.9 1.5 %shard_map.50 = (f32[768,128]{1,0:T(8,128)S(1)}, f32[768,128]{1,0:T(8,128)S(1)}, f32[768,128]{1,0:T(8,128)S(1)}) custom-call(bf16[192,384]{1,0:T(8,128)(2,1)S(1)} %get-tuple-element.30.refs_0_, bf16[576,384]{1,0:T(8,128)(2,1)S(1)} %collective-permute-done.1.refs_1_, bf16[784,384]{1,0:T(8,128)(2,1)S(1)} %shard_map.48.refs_2_.refs_3_, ...), custom_call_target="tpu_custom_call" | custom-call | tf_op jit(solution)/shard_map/pallas_call | solution.py:368
  24.8 3.1 %collective-permute-start.13 = (bf16[768,128]{1,0:T(8,128)(2,1)S(1)}, bf16[768,128]{1,0:T(8,128)(2,1)S(1)}, u32[]{:S(2)}, u32[]{:S(2)}) collective-permute-start(bf16[768,128]{1,0:T(8,128)(2,1)S(1)} %shard_map.53), channel_id=1, source_target_pairs={{4,8},{8,4},{5,9},{9,5},{6,10},{10,6},{7,11},{11,7},{20,24},{24,20... | collective-permute-start | bytes 589832 | tf_op jit(solution)/shard_map/ppermute | solution.py:38
  27.9 2.7 %shard_map.51 = (f32[768,128]{1,0:T(8,128)S(1)}, f32[768,128]{1,0:T(8,128)S(1)}, f32[768,128]{1,0:T(8,128)S(1)}, f32[768,128]{1,0:T(8,128)S(1)}, f32[768,128]{1,0:T(8,128)S(1)}, /*index=5*/f32[768,128]{1,0:T(8,128)S(1)}) custom-call(bf16[192,384]{1,0:T(8,128)(2,1)S(1)} %get-tuple-element.30.refs_0_, bf16[576,384]{1,0:T(8,128)(2,1)S(1)} %collective-permute-done.1.refs_1_, ...), custom_call_target="tpu_custom_call" | custom-call | tf_op jit(solution)/shard_map/pallas_call | solution.py:368
  30.7 0.6 %collective-permute-done.8.refs_6_ = bf16[768,256]{1,0:T(8,128)(2,1)S(1)} collective-permute-done((bf16[768,256]{1,0:T(8,128)(2,1)S(1)}, bf16[768,256]{1,0:T(8,128)(2,1)S(1)}, u32[]{:S(2)}, u32[]{:S(2)}) %collective-permute-start.8) | collective-permute-done | bytes 393248 | tf_op jit(solution)/shard_map/ppermute | solution.py:38
  31.3 1.3 %shard_map.52 = (bf16[192,256]{1,0:T(8,128)(2,1)S(1)}, bf16[192,256]{1,0:T(8,128)(2,1)S(1)}, bf16[192,256]{1,0:T(8,128)(2,1)S(1)}, bf16[192,256]{1,0:T(8,128)(2,1)S(1)}) custom-call(bf16[192,384]{1,0:T(8,128)(2,1)S(1)} %get-tuple-element.30.refs_0_, bf16[576,384]{1,0:T(8,128)(2,1)S(1)} %collective-permute-done.1.refs_1_, ...), custom_call_target="tpu_custom_call" | custom-call | tf_op jit(solution)/shard_map/pallas_call | solution.py:368
  32.7 1.3 %collective-permute-start.10 = (bf16[192,256]{1,0:T(8,128)(2,1)S(1)}, bf16[192,256]{1,0:T(8,128)(2,1)S(1)}, u32[]{:S(2)}, u32[]{:S(2)}) collective-permute-start(bf16[192,256]{1,0:T(8,128)(2,1)S(1)} %get-tuple-element.44), channel_id=1, source_target_pairs={{0,2},{1,3},{2,0},{3,1},{4,6},{5,7},{6,4},{7,5},{8,10},{9,11},{10,... | collective-permute-start | bytes 294920 | tf_op jit(solution)/shard_map/ppermute | solution.py:29
  34.0 1.5 %collective-permute-start.11 = (bf16[192,256]{1,0:T(8,128)(2,1)S(1)}, bf16[192,256]{1,0:T(8,128)(2,1)S(1)}, u32[]{:S(2)}, u32[]{:S(2)}) collective-permute-start(bf16[192,256]{1,0:T(8,128)(2,1)S(1)} %get-tuple-element.45), channel_id=1, source_target_pairs={{0,3},{1,2},{2,1},{3,0},{4,7},{5,6},{6,5},{7,4},{8,11},{9,10},{10,... | collective-permute-start | bytes 294920 | tf_op jit(solution)/shard_map/ppermute | solution.py:29
  35.5 0.8 %shard_map.54 = (bf16[192,128]{1,0:T(8,128)(2,1)S(1)}, bf16[192,128]{1,0:T(8,128)(2,1)S(1)}, bf16[192,128]{1,0:T(8,128)(2,1)S(1)}, bf16[192,128]{1,0:T(8,128)(2,1)S(1)}) custom-call(bf16[192,384]{1,0:T(8,128)(2,1)S(1)} %get-tuple-element.30.refs_0_, bf16[576,384]{1,0:T(8,128)(2,1)S(1)} %collective-permute-done.1.refs_1_, ...), custom_call_target="tpu_custom_call" | custom-call | tf_op jit(solution)/shard_map/pallas_call | solution.py:368
  36.3 1.9 %collective-permute-start.14 = (bf16[192,128]{1,0:T(8,128)(2,1)S(1)}, bf16[192,128]{1,0:T(8,128)(2,1)S(1)}, u32[]{:S(2)}, u32[]{:S(2)}) collective-permute-start(bf16[192,128]{1,0:T(8,128)(2,1)S(1)} %get-tuple-element.50), channel_id=1, source_target_pairs={{0,3},{1,2},{2,1},{3,0},{4,7},{5,6},{6,5},{7,4},{8,11},{9,10},{10,... | collective-permute-start | bytes 147464 | tf_op jit(solution)/shard_map/ppermute | solution.py:29
  38.7 1.7 %collective-permute-done.11.rest_3_ = bf16[192,256]{1,0:T(8,128)(2,1)S(1)} collective-permute-done((bf16[192,256]{1,0:T(8,128)(2,1)S(1)}, bf16[192,256]{1,0:T(8,128)(2,1)S(1)}, u32[]{:S(2)}, u32[]{:S(2)}) %collective-permute-start.11) | collective-permute-done | bytes 98336 | tf_op jit(solution)/shard_map/ppermute | solution.py:29
  40.4 0.8 %shard_map.55.rest_0_ = bf16[192,1536]{1,0:T(8,128)(2,1)} custom-call(s32[1]{0:T(128)} %bitcast.me_ref, bf16[192,256]{1,0:T(8,128)(2,1)S(1)} %get-tuple-element.42.refs_10_.rest_0_, bf16[192,256]{1,0:T(8,128)(2,1)S(1)} %collective-permute-done.9.rest_1_, bf16[192,256]{1,0:T(8,128)(2,1)S(1)} %collective-permute-done.10.rest_2_, ...), custom_call_target="tpu_custom_call" | custom-call | tf_op jit(solution)/shard_map/pallas_call | solution.py:414
  41.2 1.0 %collective-permute-done.15.rest_2_ = bf16[192,128]{1,0:T(8,128)(2,1)S(1)} collective-permute-done((bf16[192,128]{1,0:T(8,128)(2,1)S(1)}, bf16[192,128]{1,0:T(8,128)(2,1)S(1)}, u32[]{:S(2)}, u32[]{:S(2)}) %collective-permute-start.15) | collective-permute-done | bytes 49184 | tf_op jit(solution)/shard_map/ppermute | solution.py:29
  42.2 0.7 %shard_map.56 = bf16[192,1536]{1,0:T(8,128)(2,1)} custom-call(s32[1]{0:T(128)} %bitcast.me_ref, bf16[192,1536]{1,0:T(8,128)(2,1)} %shard_map.55.rest_0_, bf16[192,128]{1,0:T(8,128)(2,1)S(1)} %collective-permute-done.14.rest_1_, bf16[192,128]{1,0:T(8,128)(2,1)S(1)} %collective-permute-done.15.rest_2_, ...), custom_call_target="tpu_custom_call", output_to_operand_aliasing={{}: (1, {})} | custom-call | tf_op jit(solution)/shard_map/pallas_call | solution.py:414
  (21 shorter events, 1.7 us)
Async XLA Ops:
  1.5 2.9 %collective-permute-start.1 = (bf16[576,384]{1,0:T(8,128)(2,1)S(1)}, bf16[576,384]{1,0:T(8,128)(2,1)S(1)}, u32[]{:S(2)}, u32[]{:S(2)}) collective-permute-start(bf16[576,384]{1,0:T(8,128)(2,1)S(1)} %get-tuple-element.31), channel_id=1, source_target_pairs={{0,1},{1,0},{2,3},{3,2},{4,5},{5,4},{6,7},{7,6},{8,9},{9,8},{10,11... | collective-permute-start | bytes 1327112 | tf_op jit(solution)/shard_map/ppermute | solution.py:29
  2.2 6.9 %collective-permute-start = (bf16[960,128]{1,0:T(8,128)(2,1)S(1)}, bf16[960,128]{1,0:T(8,128)(2,1)S(1)}, u32[]{:S(2)}, u32[]{:S(2)}) collective-permute-start(bf16[960,128]{1,0:T(8,128)(2,1)S(1)} %get-tuple-element.29), channel_id=1, source_target_pairs={{0,1},{1,0},{2,3},{3,2},{4,5},{5,4},{6,7},{7,6},{8,9},{9,8},{10,11... | collective-permute-start | bytes 737288 | tf_op jit(solution)/shard_map/ppermute | solution.py:29
  2.3 9.1 %collective-permute-start.5 = (bf16[384,256]{1,0:T(8,128)(2,1)S(1)}, bf16[384,256]{1,0:T(8,128)(2,1)S(1)}, u32[]{:S(2)}, u32[]{:S(2)}) collective-permute-start(bf16[384,256]{1,0:T(8,128)(2,1)S(1)} %get-tuple-element.34), channel_id=1, source_target_pairs={{0,2},{1,3},{2,0},{3,1},{4,6},{5,7},{6,4},{7,5},{8,10},{9,11},{10,... | collective-permute-start | bytes 589832 | tf_op jit(solution)/shard_map/ppermute | solution.py:29
  3.5 10.4 %collective-permute-start.6 = (bf16[384,256]{1,0:T(8,128)(2,1)S(1)}, bf16[384,256]{1,0:T(8,128)(2,1)S(1)}, u32[]{:S(2)}, u32[]{:S(2)}) collective-permute-start(bf16[384,256]{1,0:T(8,128)(2,1)S(1)} %get-tuple-element.35), channel_id=1, source_target_pairs={{0,3},{1,2},{2,1},{3,0},{4,7},{5,6},{6,5},{7,4},{8,11},{9,10},{10,... | collective-permute-start | bytes 589832 | tf_op jit(solution)/shard_map/ppermute | solution.py:29
  4.5 15.4 %collective-permute-start.3 = (bf16[784,384]{1,0:T(8,128)(2,1)S(1)}, bf16[784,384]{1,0:T(8,128)(2,1)S(1)}, u32[]{:S(2)}, u32[]{:S(2)}) collective-permute-start(bf16[784,384]{1,0:T(8,128)(2,1)S(1)} %shard_map.48.refs_2_.refs_3_), channel_id=1, source_target_pairs={{0,4},{4,0},{8,12},{12,8},{1,5},{5,1},{9,13},{13,9},{2,6},{6,2},{1... | collective-permute-start | bytes 1806344 | tf_op jit(solution)/shard_map/ppermute | solution.py:38
  4.6 18.3 %collective-permute-start.4 = (bf16[784,384]{1,0:T(8,128)(2,1)S(1)}, bf16[784,384]{1,0:T(8,128)(2,1)S(1)}, u32[]{:S(2)}, u32[]{:S(2)}) collective-permute-start(bf16[784,384]{1,0:T(8,128)(2,1)S(1)} %shard_map.48.refs_2_.refs_3_), channel_id=1, source_target_pairs={{4,8},{8,4},{5,9},{9,5},{6,10},{10,6},{7,11},{11,7},{20,24},{24,20... | collective-permute-start | bytes 1806344 | tf_op jit(solution)/shard_map/ppermute | solution.py:38
  10.1 14.3 %collective-permute-start.2 = (bf16[1920,128]{1,0:T(8,128)(2,1)S(1)}, bf16[1920,128]{1,0:T(8,128)(2,1)S(1)}, u32[]{:S(2)}, u32[]{:S(2)}) collective-permute-start(bf16[1920,128]{1,0:T(8,128)(2,1)S(1)} %get-tuple-element.32), channel_id=1, source_target_pairs={{0,2},{1,3},{2,0},{3,1},{4,6},{5,7},{6,4},{7,5},{8,10},{9,11},{10,... | collective-permute-start | bytes 1474568 | tf_op jit(solution)/shard_map/ppermute | solution.py:29
  14.4 16.3 %collective-permute-start.7 = (bf16[768,256]{1,0:T(8,128)(2,1)S(1)}, bf16[768,256]{1,0:T(8,128)(2,1)S(1)}, u32[]{:S(2)}, u32[]{:S(2)}) collective-permute-start(bf16[768,256]{1,0:T(8,128)(2,1)S(1)} %shard_map.49), channel_id=1, source_target_pairs={{0,4},{4,0},{8,12},{12,8},{1,5},{5,1},{9,13},{13,9},{2,6},{6,2},{1... | collective-permute-start | bytes 1179656 | tf_op jit(solution)/shard_map/ppermute | solution.py:38
  14.5 16.9 %collective-permute-start.8 = (bf16[768,256]{1,0:T(8,128)(2,1)S(1)}, bf16[768,256]{1,0:T(8,128)(2,1)S(1)}, u32[]{:S(2)}, u32[]{:S(2)}) collective-permute-start(bf16[768,256]{1,0:T(8,128)(2,1)S(1)} %shard_map.49), channel_id=1, source_target_pairs={{4,8},{8,4},{5,9},{9,5},{6,10},{10,6},{7,11},{11,7},{20,24},{24,20... | collective-permute-start | bytes 1179656 | tf_op jit(solution)/shard_map/ppermute | solution.py:38
  24.7 10.8 %collective-permute-start.12 = (bf16[768,128]{1,0:T(8,128)(2,1)S(1)}, bf16[768,128]{1,0:T(8,128)(2,1)S(1)}, u32[]{:S(2)}, u32[]{:S(2)}) collective-permute-start(bf16[768,128]{1,0:T(8,128)(2,1)S(1)} %shard_map.53), channel_id=1, source_target_pairs={{0,4},{4,0},{8,12},{12,8},{1,5},{5,1},{9,13},{13,9},{2,6},{6,2},{1... | collective-permute-start | bytes 589832 | tf_op jit(solution)/shard_map/ppermute | solution.py:38
  24.8 10.7 %collective-permute-start.13 = (bf16[768,128]{1,0:T(8,128)(2,1)S(1)}, bf16[768,128]{1,0:T(8,128)(2,1)S(1)}, u32[]{:S(2)}, u32[]{:S(2)}) collective-permute-start(bf16[768,128]{1,0:T(8,128)(2,1)S(1)} %shard_map.53), channel_id=1, source_target_pairs={{4,8},{8,4},{5,9},{9,5},{6,10},{10,6},{7,11},{11,7},{20,24},{24,20... | collective-permute-start | bytes 589832 | tf_op jit(solution)/shard_map/ppermute | solution.py:38
  32.7 5.8 %collective-permute-start.10 = (bf16[192,256]{1,0:T(8,128)(2,1)S(1)}, bf16[192,256]{1,0:T(8,128)(2,1)S(1)}, u32[]{:S(2)}, u32[]{:S(2)}) collective-permute-start(bf16[192,256]{1,0:T(8,128)(2,1)S(1)} %get-tuple-element.44), channel_id=1, source_target_pairs={{0,2},{1,3},{2,0},{3,1},{4,6},{5,7},{6,4},{7,5},{8,10},{9,11},{10,... | collective-permute-start | bytes 294920 | tf_op jit(solution)/shard_map/ppermute | solution.py:29
  34.0 6.4 %collective-permute-start.11 = (bf16[192,256]{1,0:T(8,128)(2,1)S(1)}, bf16[192,256]{1,0:T(8,128)(2,1)S(1)}, u32[]{:S(2)}, u32[]{:S(2)}) collective-permute-start(bf16[192,256]{1,0:T(8,128)(2,1)S(1)} %get-tuple-element.45), channel_id=1, source_target_pairs={{0,3},{1,2},{2,1},{3,0},{4,7},{5,6},{6,5},{7,4},{8,11},{9,10},{10,... | collective-permute-start | bytes 294920 | tf_op jit(solution)/shard_map/ppermute | solution.py:29
  35.5 4.9 %collective-permute-start.9 = (bf16[192,256]{1,0:T(8,128)(2,1)S(1)}, bf16[192,256]{1,0:T(8,128)(2,1)S(1)}, u32[]{:S(2)}, u32[]{:S(2)}) collective-permute-start(bf16[192,256]{1,0:T(8,128)(2,1)S(1)} %get-tuple-element.43), channel_id=1, source_target_pairs={{0,1},{1,0},{2,3},{3,2},{4,5},{5,4},{6,7},{7,6},{8,9},{9,8},{10,11... | collective-permute-start | bytes 294920 | tf_op jit(solution)/shard_map/ppermute | solution.py:29
  36.3 4.9 %collective-permute-start.14 = (bf16[192,128]{1,0:T(8,128)(2,1)S(1)}, bf16[192,128]{1,0:T(8,128)(2,1)S(1)}, u32[]{:S(2)}, u32[]{:S(2)}) collective-permute-start(bf16[192,128]{1,0:T(8,128)(2,1)S(1)} %get-tuple-element.50), channel_id=1, source_target_pairs={{0,3},{1,2},{2,1},{3,0},{4,7},{5,6},{6,5},{7,4},{8,11},{9,10},{10,... | collective-permute-start | bytes 147464 | tf_op jit(solution)/shard_map/ppermute | solution.py:29
  38.2 4.0 %collective-permute-start.15 = (bf16[192,128]{1,0:T(8,128)(2,1)S(1)}, bf16[192,128]{1,0:T(8,128)(2,1)S(1)}, u32[]{:S(2)}, u32[]{:S(2)}) collective-permute-start(bf16[192,128]{1,0:T(8,128)(2,1)S(1)} %get-tuple-element.51), channel_id=1, source_target_pairs={{0,2},{1,3},{2,0},{3,1},{4,6},{5,7},{6,4},{7,5},{8,10},{9,11},{10,... | collective-permute-start | bytes 147464 | tf_op jit(solution)/shard_map/ppermute | solution.py:29
  38.5 3.7 %collective-permute-start.16 = (bf16[192,128]{1,0:T(8,128)(2,1)S(1)}, bf16[192,128]{1,0:T(8,128)(2,1)S(1)}, u32[]{:S(2)}, u32[]{:S(2)}) collective-permute-start(bf16[192,128]{1,0:T(8,128)(2,1)S(1)} %get-tuple-element.52), channel_id=1, source_target_pairs={{0,1},{1,0},{2,3},{3,2},{4,5},{5,4},{6,7},{7,6},{8,9},{9,8},{10,11... | collective-permute-start | bytes 147464 | tf_op jit(solution)/shard_map/ppermute | solution.py:29

commit v9 on v8

--- a/solution.py
+++ b/solution.py
@@ -477,13 +477,19 @@
     across_last = sent(stack([last[i] for i, _ in ends], spans, after=close[:1]))
     for field, (i, base) in zip(own_fields, ends):
         field.append((len(near) + len(far) + i, base, heads - 1))
-    jobs = [(layout[2:], first_heads), (layout, last_head)]
+    jobs = [(layout[2:], first_heads), (layout[:2], last_head), (layout[2:], last_head)]
     groups = [(0, near_groups[0][1] + own_fields), *near_groups[1:]]
     left = attend_early(queries, jobs, near + far + last, groups, tiles, tokens)
     left = [[*close, *left[:3]], left[3:]]
 
-    pieces = []
-    for others, heads_now in ((across, first_heads), (across_last, last_head)):
+    pieces, after = [], []
+    rounds = [
+        (across, first_heads, range(2, devices), left[0][3:]),
+        (across, first_heads, range(2), left[0][:3]),
+        (across_last, last_head, range(2, devices), left[1][3:]),
+        (across_last, last_head, range(2), left[1][:3]),
+    ]
+    for others, heads_now, frames, before in rounds:
         first = heads_now[0]
         groups = [
             (i, [[(len(others) + i, 2 * rows * bit, 0)] for bit in range(devices - 2)])
@@ -491,20 +497,21 @@
         ]
         results = attend_late(
             queries,
-            layout,
+            [layout[frame] for frame in frames],
             near[1:] + others,
             groups,
             tiles,
             tokens,
             len(heads_now),
             first,
-            left[len(pieces) > 0],
-            [piece[2] for piece in pieces[:1]],
+            before,
+            after,
         )
-        order = range(devices) if not pieces else range(devices - 1, -1, -1)
+        after = [results[0]]
+        found = list(zip(frames, results))
         pieces += [
-            (bit, first * HEAD_DIM, swap_head(results[bit], bit, devices) if bit else results[0])
-            for bit in order
+            (bit, first * HEAD_DIM, swap_head(b, bit, devices) if bit else b)
+            for bit, b in (found[::-1] if first else found)
         ]
     begun, ended = [], []
     for piece in pieces:

time: 43.2 us -> 42.8 us (level)
  waiting for transfers between devices: 9.31 us -> 7.76 us
  Pallas kernels: 11.3 us -> 12.3 us
    ppermute x11, waiting for transfers between devices: 5.13 us -> 3.74 us  [swap_head(): return lax.ppermute(block, 'head', [(i, i ^ bit) for i in range(devices)])]
    pallas_call x4 -> x6, Pallas kernels: 6.36 us -> 7.36 us  [attend(): pl.pallas_call(kernel, out_shape=outs, in_specs=in_vmem(len(operands)), o...]
  transfers between devices with their start and end apart: 17 -> 17, of which waited for: 6 -> 7; matrix products, arithmetic and copies ran while one was open for 0% -> 0% of each run, Pallas kernels for 21% -> 24%
where the time goes in v9:
time: 42.8 us; the launch traced here: 42.5 us
  starting transfers between devices  22.2 us (52%)
  Pallas kernels  12.3 us (29%)
  waiting for transfers between devices  7.76 us (18%)
    ppermute x6, starting transfers between devices, swap_pairs(): return lax.ppermute(block, 'tok', route)  12.7 us
    ppermute x11, starting transfers between devices, swap_head(): return lax.ppermute(block, 'head', [(i, i ^ bit) for i in range(devices)])  9.53 us
    pallas_call x6, Pallas kernels, attend(): pl.pallas_call(kernel, out_shape=outs, in_specs=in_vmem(len(operands)), o...  7.36 us
    ppermute x6, waiting for transfers between devices, swap_pairs(): return lax.ppermute(block, 'tok', route)  4.03 us
    ppermute x11, waiting for transfers between devices, swap_head(): return lax.ppermute(block, 'head', [(i, i ^ bit) for i in range(devices)])  3.74 us
    pallas_call x2, Pallas kernels, join(): pl.pallas_call(functools.partial(join_body, jobs, part, len(begun)), out_...  1.47 us
    pallas_call x1, Pallas kernels, pack(): pl.pallas_call(functools.partial(pack_body, devices, heads), out_shape=[p...  1.46 us
    pallas_call x1, Pallas kernels, pack_last(): pl.pallas_call(functools.partial(pack_last_body, devices, heads), out_sha...  1.04 us
  transfers between devices with their start and end apart: 17, of which 7 were waited for; matrix products, arithmetic and copies ran while one was open for 0% of the time, Pallas kernels for 24%

profile of v9, /device:TPU:9, one launch (start us, length us, event | category | flops | bytes accessed | tf_op | source)
XLA Modules:
  0.0 42.5 jit_solution(14414742264307624979)
XLA Ops:
  0.0 1.5 %shard_map.46 = (bf16[400,384]{1,0:T(8,128)(2,1)S(1)}, bf16[576,384]{1,0:T(8,128)(2,1)S(1)}, bf16[960,128]{1,0:T(8,128)(2,1)S(1)}, bf16[384,256]{1,0:T(8,128)(2,1)S(1)}, bf16[384,256]{1,0:T(8,128)(2,1)S(1)}) custom-call(s32[3]{0:T(128)} %counts_in.1, s32[1]{0:T(128)} %bitcast.me_ref, bf16[192,1536]{1,0:T(8,128)(2,1)} %bitcast.5, bf16[192,1536]{1,0:T(8,128)(2,1)} %bitcast.7, ...), custom_call_target="tpu_custom_call" | custom-call | bytes 3538944 | tf_op jit(solution)/shard_map/pallas_call | solution.py:105
  1.5 0.7 %collective-permute-start.1 = (bf16[576,384]{1,0:T(8,128)(2,1)S(1)}, bf16[576,384]{1,0:T(8,128)(2,1)S(1)}, u32[]{:S(2)}, u32[]{:S(2)}) collective-permute-start(bf16[576,384]{1,0:T(8,128)(2,1)S(1)} %get-tuple-element.34), channel_id=1, source_target_pairs={{0,1},{1,0},{2,3},{3,2},{4,5},{5,4},{6,7},{7,6},{8,9},{9,8},{10,11... | collective-permute-start | bytes 1327112 | tf_op jit(solution)/shard_map/ppermute | solution.py:29
  2.3 1.2 %collective-permute-start.5 = (bf16[384,256]{1,0:T(8,128)(2,1)S(1)}, bf16[384,256]{1,0:T(8,128)(2,1)S(1)}, u32[]{:S(2)}, u32[]{:S(2)}) collective-permute-start(bf16[384,256]{1,0:T(8,128)(2,1)S(1)} %get-tuple-element.37), channel_id=1, source_target_pairs={{0,2},{1,3},{2,0},{3,1},{4,6},{5,7},{6,4},{7,5},{8,10},{9,11},{10,... | collective-permute-start | bytes 589832 | tf_op jit(solution)/shard_map/ppermute | solution.py:29
  3.5 0.9 %collective-permute-start.6 = (bf16[384,256]{1,0:T(8,128)(2,1)S(1)}, bf16[384,256]{1,0:T(8,128)(2,1)S(1)}, u32[]{:S(2)}, u32[]{:S(2)}) collective-permute-start(bf16[384,256]{1,0:T(8,128)(2,1)S(1)} %get-tuple-element.38), channel_id=1, source_target_pairs={{0,3},{1,2},{2,1},{3,0},{4,7},{5,6},{6,5},{7,4},{8,11},{9,10},{10,... | collective-permute-start | bytes 589832 | tf_op jit(solution)/shard_map/ppermute | solution.py:29
  4.6 4.5 %collective-permute-start.4 = (bf16[784,384]{1,0:T(8,128)(2,1)S(1)}, bf16[784,384]{1,0:T(8,128)(2,1)S(1)}, u32[]{:S(2)}, u32[]{:S(2)}) collective-permute-start(bf16[784,384]{1,0:T(8,128)(2,1)S(1)} %shard_map.48.refs_3_.refs_2_), channel_id=1, source_target_pairs={{4,8},{8,4},{5,9},{9,5},{6,10},{10,6},{7,11},{11,7},{20,24},{24,20... | collective-permute-start | bytes 1806344 | tf_op jit(solution)/shard_map/ppermute | solution.py:38
  9.1 1.0 %shard_map.47 = (bf16[192,384]{1,0:T(8,128)(2,1)S(1)}, bf16[1920,128]{1,0:T(8,128)(2,1)S(1)}) custom-call(s32[1]{0:T(128)} %bitcast.me_ref, bf16[192,1536]{1,0:T(8,128)(2,1)} %bitcast.6, bf16[192,1536]{1,0:T(8,128)(2,1)} %bitcast.8, bf16[192,1536]{1,0:T(8,128)(2,1)} %bitcast.10, bf16[960,128]{1,0:T(8,128)(2,1)S(1)} %collective-permute-done.passed_ref), custom_call_target="tpu_custom_call" | custom-call | bytes 245760 | tf_op jit(solution)/shard_map/pallas_call | solution.py:144
  10.1 1.3 %collective-permute-start.2 = (bf16[1920,128]{1,0:T(8,128)(2,1)S(1)}, bf16[1920,128]{1,0:T(8,128)(2,1)S(1)}, u32[]{:S(2)}, u32[]{:S(2)}) collective-permute-start(bf16[1920,128]{1,0:T(8,128)(2,1)S(1)} %get-tuple-element.35), channel_id=1, source_target_pairs={{0,2},{1,3},{2,0},{3,1},{4,6},{5,7},{6,4},{7,5},{8,10},{9,11},{10,... | collective-permute-start | bytes 1474568 | tf_op jit(solution)/shard_map/ppermute | solution.py:29
  11.4 2.4 %collective-permute-done.6.refs_1_.refs_7_.refs_6_ = bf16[384,256]{1,0:T(8,128)(2,1)S(1)} collective-permute-done((bf16[384,256]{1,0:T(8,128)(2,1)S(1)}, bf16[384,256]{1,0:T(8,128)(2,1)S(1)}, u32[]{:S(2)}, u32[]{:S(2)}) %collective-permute-start.6) | collective-permute-done | bytes 196640 | tf_op jit(solution)/shard_map/ppermute | solution.py:29
  14.5 4.9 %collective-permute-start.8 = (bf16[768,256]{1,0:T(8,128)(2,1)S(1)}, bf16[768,256]{1,0:T(8,128)(2,1)S(1)}, u32[]{:S(2)}, u32[]{:S(2)}) collective-permute-start(bf16[768,256]{1,0:T(8,128)(2,1)S(1)} %shard_map.49), channel_id=1, source_target_pairs={{4,8},{8,4},{5,9},{9,5},{6,10},{10,6},{7,11},{11,7},{20,24},{24,20... | collective-permute-start | bytes 1179656 | tf_op jit(solution)/shard_map/ppermute | solution.py:38
  19.4 0.5 %collective-permute-done.3.refs_4_.refs_3_ = bf16[784,384]{1,0:T(8,128)(2,1)S(1)} collective-permute-done((bf16[784,384]{1,0:T(8,128)(2,1)S(1)}, bf16[784,384]{1,0:T(8,128)(2,1)S(1)}, u32[]{:S(2)}, u32[]{:S(2)}) %collective-permute-start.3) | collective-permute-done | bytes 602144 | tf_op jit(solution)/shard_map/ppermute | solution.py:38
  19.9 3.0 %collective-permute-done.4.refs_5_.refs_4_ = bf16[784,384]{1,0:T(8,128)(2,1)S(1)} collective-permute-done((bf16[784,384]{1,0:T(8,128)(2,1)S(1)}, bf16[784,384]{1,0:T(8,128)(2,1)S(1)}, u32[]{:S(2)}, u32[]{:S(2)}) %collective-permute-start.4) | collective-permute-done | bytes 602144 | tf_op jit(solution)/shard_map/ppermute | solution.py:38
  22.9 1.5 %shard_map.52 = (f32[768,128]{1,0:T(8,128)S(1)}, f32[768,128]{1,0:T(8,128)S(1)}, f32[768,128]{1,0:T(8,128)S(1)}) custom-call(bf16[192,384]{1,0:T(8,128)(2,1)S(1)} %get-tuple-element.33.refs_0_, bf16[576,384]{1,0:T(8,128)(2,1)S(1)} %collective-permute-done.1.refs_1_, bf16[784,384]{1,0:T(8,128)(2,1)S(1)} %shard_map.48.refs_3_.refs_2_, ...), custom_call_target="tpu_custom_call" | custom-call | tf_op jit(solution)/shard_map/pallas_call | solution.py:368
  24.8 3.1 %collective-permute-start.13 = (bf16[768,128]{1,0:T(8,128)(2,1)S(1)}, bf16[768,128]{1,0:T(8,128)(2,1)S(1)}, u32[]{:S(2)}, u32[]{:S(2)}) collective-permute-start(bf16[768,128]{1,0:T(8,128)(2,1)S(1)} %shard_map.54), channel_id=1, source_target_pairs={{4,8},{8,4},{5,9},{9,5},{6,10},{10,6},{7,11},{11,7},{20,24},{24,20... | collective-permute-start | bytes 589832 | tf_op jit(solution)/shard_map/ppermute | solution.py:38
  27.9 2.9 %shard_map.50 = (f32[768,128]{1,0:T(8,128)S(1)}, f32[768,128]{1,0:T(8,128)S(1)}, f32[768,128]{1,0:T(8,128)S(1)}, f32[384,128]{1,0:T(8,128)S(1)}, f32[384,128]{1,...) custom-call(bf16[192,384]{1,0:T(8,128)(2,1)S(1)} %get-tuple-element., ...), custom_call_target="tpu_custom_call" | custom-call | tf_op jit(solution)/shard_map/pallas_call | solution.py:368
  31.3 0.9 %shard_map.51 = (bf16[192,256]{1,0:T(8,128)(2,1)S(1)}, bf16[192,256]{1,0:T(8,128)(2,1)S(1)}) custom-call(bf16[192,384]{1,0:T(8,128)(2,1)S(1)} %get-tuple-element.33.refs_0_, bf16[576,384]{1,0:T(8,128)(2,1)S(1)} %collective-permute-done.1.refs_1_, bf16[1920,128]{1,0:T(8,128)(2,1)S(1)} %collective-permute-done.2.refs_2_.refs_8_.refs_0_.refs_1_, ...), custom_call_target="tpu_custom_call" | custom-call | tf_op jit(solution)/shard_map/pallas_call | solution.py:368
  32.2 1.3 %collective-permute-start.9 = (bf16[192,256]{1,0:T(8,128)(2,1)S(1)}, bf16[192,256]{1,0:T(8,128)(2,1)S(1)}, u32[]{:S(2)}, u32[]{:S(2)}) collective-permute-start(bf16[192,256]{1,0:T(8,128)(2,1)S(1)} %get-tuple-element.42.refs_10_), channel_id=1, source_target_pairs={{0,2},{1,3},{2,0},{3,1},{4,6},{5,7},{6,4},{7,5},{8,10},{9,11},{10,... | collective-permute-start | bytes 294920 | tf_op jit(solution)/shard_map/ppermute | solution.py:29
  33.5 1.7 %collective-permute-start.10 = (bf16[192,256]{1,0:T(8,128)(2,1)S(1)}, bf16[192,256]{1,0:T(8,128)(2,1)S(1)}, u32[]{:S(2)}, u32[]{:S(2)}) collective-permute-start(bf16[192,256]{1,0:T(8,128)(2,1)S(1)} %get-tuple-element.43), channel_id=1, source_target_pairs={{0,3},{1,2},{2,1},{3,0},{4,7},{5,6},{6,5},{7,4},{8,11},{9,10},{10,... | collective-permute-start | bytes 294920 | tf_op jit(solution)/shard_map/ppermute | solution.py:29
  35.2 0.9 %shard_map.53 = (bf16[192,256]{1,0:T(8,128)(2,1)S(1)}, bf16[192,256]{1,0:T(8,128)(2,1)S(1)}) custom-call(bf16[192,384]{1,0:T(8,128)(2,1)S(1)} %get-tuple-element.33.refs_0_, bf16[576,384]{1,0:T(8,128)(2,1)S(1)} %collective-permute-done.1.refs_1_, bf16[1920,128]{1,0:T(8,128)(2,1)S(1)} %collective-permute-done.2.refs_2_.refs_8_.refs_0_.refs_1_, ...), custom_call_target="tpu_custom_call" | custom-call | tf_op jit(solution)/shard_map/pallas_call | solution.py:368
  36.2 0.6 %shard_map.55 = (bf16[192,128]{1,0:T(8,128)(2,1)S(1)}, bf16[192,128]{1,0:T(8,128)(2,1)S(1)}) custom-call(bf16[192,384]{1,0:T(8,128)(2,1)S(1)} %get-tuple-element.33.refs_0_, bf16[576,384]{1,0:T(8,128)(2,1)S(1)} %collective-permute-done.1.refs_1_, bf16[1920,128]{1,0:T(8,128)(2,1)S(1)} %collective-permute-done.2.refs_2_.refs_8_.refs_0_.refs_1_, ...), custom_call_target="tpu_custom_call" | custom-call | tf_op jit(solution)/shard_map/pallas_call | solution.py:368
  36.8 1.6 %collective-permute-start.14 = (bf16[192,128]{1,0:T(8,128)(2,1)S(1)}, bf16[192,128]{1,0:T(8,128)(2,1)S(1)}, u32[]{:S(2)}, u32[]{:S(2)}) collective-permute-start(bf16[192,128]{1,0:T(8,128)(2,1)S(1)} %get-tuple-element.57), channel_id=1, source_target_pairs={{0,3},{1,2},{2,1},{3,0},{4,7},{5,6},{6,5},{7,4},{8,11},{9,10},{10,... | collective-permute-start | bytes 147464 | tf_op jit(solution)/shard_map/ppermute | solution.py:29
  38.7 0.6 %shard_map.56 = (bf16[192,128]{1,0:T(8,128)(2,1)S(1)}, bf16[192,128]{1,0:T(8,128)(2,1)S(1)}) custom-call(bf16[192,384]{1,0:T(8,128)(2,1)S(1)} %get-tuple-element.33.refs_0_, bf16[576,384]{1,0:T(8,128)(2,1)S(1)} %collective-permute-done.1.refs_1_, bf16[1920,128]{1,0:T(8,128)(2,1)S(1)} %collective-permute-done.2.refs_2_.refs_8_.refs_0_.refs_1_, ...), custom_call_target="tpu_custom_call" | custom-call | tf_op jit(solution)/shard_map/pallas_call | solution.py:368
  39.8 0.8 %shard_map.57.rest_0_ = bf16[192,1536]{1,0:T(8,128)(2,1)} custom-call(s32[1]{0:T(128)} %bitcast.me_ref, bf16[192,256]{1,0:T(8,128)(2,1)S(1)} %collective-permute-done.9.rest_0_, bf16[192,256]{1,0:T(8,128)(2,1)S(1)} %collective-permute-done.10.rest_1_, bf16[192,256]{1,0:T(8,128)(2,1)S(1)} %get-tuple-element.47.refs_10_.rest_2_, ...), custom_call_target="tpu_custom_call" | custom-call | tf_op jit(solution)/shard_map/pallas_call | solution.py:414
  40.8 1.0 %collective-permute-done.15.rest_2_ = bf16[192,128]{1,0:T(8,128)(2,1)S(1)} collective-permute-done((bf16[192,128]{1,0:T(8,128)(2,1)S(1)}, bf16[192,128]{1,0:T(8,128)(2,1)S(1)}, u32[]{:S(2)}, u32[]{:S(2)}) %collective-permute-start.15) | collective-permute-done | bytes 49184 | tf_op jit(solution)/shard_map/ppermute | solution.py:29
  41.8 0.7 %shard_map.58 = bf16[192,1536]{1,0:T(8,128)(2,1)} custom-call(s32[1]{0:T(128)} %bitcast.me_ref, bf16[192,1536]{1,0:T(8,128)(2,1)} %shard_map.57.rest_0_, bf16[192,128]{1,0:T(8,128)(2,1)S(1)} %collective-permute-done.14.rest_1_, bf16[192,128]{1,0:T(8,128)(2,1)S(1)} %collective-permute-done.15.rest_2_, ...), custom_call_target="tpu_custom_call", output_to_operand_aliasing={{}: (1, {})} | custom-call | tf_op jit(solution)/shard_map/pallas_call | solution.py:414
  (23 shorter events, 2.7 us)
Async XLA Ops:
  1.5 2.9 %collective-permute-start.1 = (bf16[576,384]{1,0:T(8,128)(2,1)S(1)}, bf16[576,384]{1,0:T(8,128)(2,1)S(1)}, u32[]{:S(2)}, u32[]{:S(2)}) collective-permute-start(bf16[576,384]{1,0:T(8,128)(2,1)S(1)} %get-tuple-element.34), channel_id=1, source_target_pairs={{0,1},{1,0},{2,3},{3,2},{4,5},{5,4},{6,7},{7,6},{8,9},{9,8},{10,11... | collective-permute-start | bytes 1327112 | tf_op jit(solution)/shard_map/ppermute | solution.py:29
  2.2 6.9 %collective-permute-start = (bf16[960,128]{1,0:T(8,128)(2,1)S(1)}, bf16[960,128]{1,0:T(8,128)(2,1)S(1)}, u32[]{:S(2)}, u32[]{:S(2)}) collective-permute-start(bf16[960,128]{1,0:T(8,128)(2,1)S(1)} %get-tuple-element.32), channel_id=1, source_target_pairs={{0,1},{1,0},{2,3},{3,2},{4,5},{5,4},{6,7},{7,6},{8,9},{9,8},{10,11... | collective-permute-start | bytes 737288 | tf_op jit(solution)/shard_map/ppermute | solution.py:29
  2.3 9.1 %collective-permute-start.5 = (bf16[384,256]{1,0:T(8,128)(2,1)S(1)}, bf16[384,256]{1,0:T(8,128)(2,1)S(1)}, u32[]{:S(2)}, u32[]{:S(2)}) collective-permute-start(bf16[384,256]{1,0:T(8,128)(2,1)S(1)} %get-tuple-element.37), channel_id=1, source_target_pairs={{0,2},{1,3},{2,0},{3,1},{4,6},{5,7},{6,4},{7,5},{8,10},{9,11},{10,... | collective-permute-start | bytes 589832 | tf_op jit(solution)/shard_map/ppermute | solution.py:29
  3.5 10.4 %collective-permute-start.6 = (bf16[384,256]{1,0:T(8,128)(2,1)S(1)}, bf16[384,256]{1,0:T(8,128)(2,1)S(1)}, u32[]{:S(2)}, u32[]{:S(2)}) collective-permute-start(bf16[384,256]{1,0:T(8,128)(2,1)S(1)} %get-tuple-element.38), channel_id=1, source_target_pairs={{0,3},{1,2},{2,1},{3,0},{4,7},{5,6},{6,5},{7,4},{8,11},{9,10},{10,... | collective-permute-start | bytes 589832 | tf_op jit(solution)/shard_map/ppermute | solution.py:29
  4.5 15.4 %collective-permute-start.3 = (bf16[784,384]{1,0:T(8,128)(2,1)S(1)}, bf16[784,384]{1,0:T(8,128)(2,1)S(1)}, u32[]{:S(2)}, u32[]{:S(2)}) collective-permute-start(bf16[784,384]{1,0:T(8,128)(2,1)S(1)} %shard_map.48.refs_3_.refs_2_), channel_id=1, source_target_pairs={{0,4},{4,0},{8,12},{12,8},{1,5},{5,1},{9,13},{13,9},{2,6},{6,2},{1... | collective-permute-start | bytes 1806344 | tf_op jit(solution)/shard_map/ppermute | solution.py:38
  4.6 18.3 %collective-permute-start.4 = (bf16[784,384]{1,0:T(8,128)(2,1)S(1)}, bf16[784,384]{1,0:T(8,128)(2,1)S(1)}, u32[]{:S(2)}, u32[]{:S(2)}) collective-permute-start(bf16[784,384]{1,0:T(8,128)(2,1)S(1)} %shard_map.48.refs_3_.refs_2_), channel_id=1, source_target_pairs={{4,8},{8,4},{5,9},{9,5},{6,10},{10,6},{7,11},{11,7},{20,24},{24,20... | collective-permute-start | bytes 1806344 | tf_op jit(solution)/shard_map/ppermute | solution.py:38
  10.1 14.3 %collective-permute-start.2 = (bf16[1920,128]{1,0:T(8,128)(2,1)S(1)}, bf16[1920,128]{1,0:T(8,128)(2,1)S(1)}, u32[]{:S(2)}, u32[]{:S(2)}) collective-permute-start(bf16[1920,128]{1,0:T(8,128)(2,1)S(1)} %get-tuple-element.35), channel_id=1, source_target_pairs={{0,2},{1,3},{2,0},{3,1},{4,6},{5,7},{6,4},{7,5},{8,10},{9,11},{10,... | collective-permute-start | bytes 1474568 | tf_op jit(solution)/shard_map/ppermute | solution.py:29
  14.4 16.4 %collective-permute-start.7 = (bf16[768,256]{1,0:T(8,128)(2,1)S(1)}, bf16[768,256]{1,0:T(8,128)(2,1)S(1)}, u32[]{:S(2)}, u32[]{:S(2)}) collective-permute-start(bf16[768,256]{1,0:T(8,128)(2,1)S(1)} %shard_map.49), channel_id=1, source_target_pairs={{0,4},{4,0},{8,12},{12,8},{1,5},{5,1},{9,13},{13,9},{2,6},{6,2},{1... | collective-permute-start | bytes 1179656 | tf_op jit(solution)/shard_map/ppermute | solution.py:38
  14.5 16.9 %collective-permute-start.8 = (bf16[768,256]{1,0:T(8,128)(2,1)S(1)}, bf16[768,256]{1,0:T(8,128)(2,1)S(1)}, u32[]{:S(2)}, u32[]{:S(2)}) collective-permute-start(bf16[768,256]{1,0:T(8,128)(2,1)S(1)} %shard_map.49), channel_id=1, source_target_pairs={{4,8},{8,4},{5,9},{9,5},{6,10},{10,6},{7,11},{11,7},{20,24},{24,20... | collective-permute-start | bytes 1179656 | tf_op jit(solution)/shard_map/ppermute | solution.py:38
  24.7 11.5 %collective-permute-start.12 = (bf16[768,128]{1,0:T(8,128)(2,1)S(1)}, bf16[768,128]{1,0:T(8,128)(2,1)S(1)}, u32[]{:S(2)}, u32[]{:S(2)}) collective-permute-start(bf16[768,128]{1,0:T(8,128)(2,1)S(1)} %shard_map.54), channel_id=1, source_target_pairs={{0,4},{4,0},{8,12},{12,8},{1,5},{5,1},{9,13},{13,9},{2,6},{6,2},{1... | collective-permute-start | bytes 589832 | tf_op jit(solution)/shard_map/ppermute | solution.py:38
  24.8 11.4 %collective-permute-start.13 = (bf16[768,128]{1,0:T(8,128)(2,1)S(1)}, bf16[768,128]{1,0:T(8,128)(2,1)S(1)}, u32[]{:S(2)}, u32[]{:S(2)}) collective-permute-start(bf16[768,128]{1,0:T(8,128)(2,1)S(1)} %shard_map.54), channel_id=1, source_target_pairs={{4,8},{8,4},{5,9},{9,5},{6,10},{10,6},{7,11},{11,7},{20,24},{24,20... | collective-permute-start | bytes 589832 | tf_op jit(solution)/shard_map/ppermute | solution.py:38
  32.2 7.1 %collective-permute-start.9 = (bf16[192,256]{1,0:T(8,128)(2,1)S(1)}, bf16[192,256]{1,0:T(8,128)(2,1)S(1)}, u32[]{:S(2)}, u32[]{:S(2)}) collective-permute-start(bf16[192,256]{1,0:T(8,128)(2,1)S(1)} %get-tuple-element.42.refs_10_), channel_id=1, source_target_pairs={{0,2},{1,3},{2,0},{3,1},{4,6},{5,7},{6,4},{7,5},{8,10},{9,11},{10,... | collective-permute-start | bytes 294920 | tf_op jit(solution)/shard_map/ppermute | solution.py:29
  33.5 6.2 %collective-permute-start.10 = (bf16[192,256]{1,0:T(8,128)(2,1)S(1)}, bf16[192,256]{1,0:T(8,128)(2,1)S(1)}, u32[]{:S(2)}, u32[]{:S(2)}) collective-permute-start(bf16[192,256]{1,0:T(8,128)(2,1)S(1)} %get-tuple-element.43), channel_id=1, source_target_pairs={{0,3},{1,2},{2,1},{3,0},{4,7},{5,6},{6,5},{7,4},{8,11},{9,10},{10,... | collective-permute-start | bytes 294920 | tf_op jit(solution)/shard_map/ppermute | solution.py:29
  36.1 3.7 %collective-permute-start.11 = (bf16[192,256]{1,0:T(8,128)(2,1)S(1)}, bf16[192,256]{1,0:T(8,128)(2,1)S(1)}, u32[]{:S(2)}, u32[]{:S(2)}) collective-permute-start(bf16[192,256]{1,0:T(8,128)(2,1)S(1)} %get-tuple-element.48), channel_id=1, source_target_pairs={{0,1},{1,0},{2,3},{3,2},{4,5},{5,4},{6,7},{7,6},{8,9},{9,8},{10,11... | collective-permute-start | bytes 294920 | tf_op jit(solution)/shard_map/ppermute | solution.py:29
  36.8 4.0 %collective-permute-start.14 = (bf16[192,128]{1,0:T(8,128)(2,1)S(1)}, bf16[192,128]{1,0:T(8,128)(2,1)S(1)}, u32[]{:S(2)}, u32[]{:S(2)}) collective-permute-start(bf16[192,128]{1,0:T(8,128)(2,1)S(1)} %get-tuple-element.57), channel_id=1, source_target_pairs={{0,3},{1,2},{2,1},{3,0},{4,7},{5,6},{6,5},{7,4},{8,11},{9,10},{10,... | collective-permute-start | bytes 147464 | tf_op jit(solution)/shard_map/ppermute | solution.py:29
  38.4 3.3 %collective-permute-start.15 = (bf16[192,128]{1,0:T(8,128)(2,1)S(1)}, bf16[192,128]{1,0:T(8,128)(2,1)S(1)}, u32[]{:S(2)}, u32[]{:S(2)}) collective-permute-start(bf16[192,128]{1,0:T(8,128)(2,1)S(1)} %get-tuple-element.55.refs_10_), channel_id=1, source_target_pairs={{0,2},{1,3},{2,0},{3,1},{4,6},{5,7},{6,4},{7,5},{8,10},{9,11},{10,... | collective-permute-start | bytes 147464 | tf_op jit(solution)/shard_map/ppermute | solution.py:29
  39.3 2.5 %collective-permute-start.16 = (bf16[192,128]{1,0:T(8,128)(2,1)S(1)}, bf16[192,128]{1,0:T(8,128)(2,1)S(1)}, u32[]{:S(2)}, u32[]{:S(2)}) collective-permute-start(bf16[192,128]{1,0:T(8,128)(2,1)S(1)} %get-tuple-element.58), channel_id=1, source_target_pairs={{0,1},{1,0},{2,3},{3,2},{4,5},{5,4},{6,7},{7,6},{8,9},{9,8},{10,11... | collective-permute-start | bytes 147464 | tf_op jit(solution)/shard_map/ppermute | solution.py:29
